TPU v7x, 128 devices: a whole 4x4x4 slice. The times are simulated.
128 devices in a mesh: replica: 4 (over z), fsdp: 16 (over y, x), tensor: 2 (over core).
Axes of the slice: x: 4, y: 4, z: 4, core: 2. Of those that a mesh axis runs over, the one named last changes fastest.
Arguments:
- tokens: bfloat16 [49152, 12288], P(('replica', 'fsdp', 'tensor')), may hold values from -60 to 60
- norm_gain: bfloat16 [12288], replicated, may hold values from 0.099609375 to 1.8984375
- fragment: bfloat16 [4, 12288, 2048], P('replica', 'fsdp', 'tensor'), may hold values from -6.25 to 6.25
- exponents: int32 [4, 12288, 64], P('replica', 'fsdp', 'tensor'), may hold values from -4 to -1
- base_weight: float32 [12288, 2048], P(('fsdp', 'replica'), 'tensor'), may hold values from -5 to 5, as said below
- momentum: float32 [12288, 2048], P(('fsdp', 'replica'), 'tensor'), may hold values from -3 to 3
Outputs:
- new_base: float32 [12288, 2048], P(('fsdp', 'replica'), 'tensor')
- new_momentum: float32 [12288, 2048], P(('fsdp', 'replica'), 'tensor')
- keys_values: bfloat16 [49152, 2048], P(('replica', 'fsdp'), 'tensor')
Inputs may be any that keep to these rules, and one draw needn't show every extreme that they name: base_weight holds multiples of 2 ** -10.
All inputs are finite; a program needn't handle non-finite values.
Results may differ from a plain program's by a relative error of at most 0.0054.
Values may be sent and summed in bfloat16 or wider, within the bound.
A program may use at most 192 MiB of HBM per device.

v0:
```python
import jax
import jax.numpy as jnp
from jax import lax
from jax.sharding import PartitionSpec as P

BLOCK = 32


OUTER_RATE = 0.7
MOMENTUM_COEF = 0.9
LEVEL_STEPS = (
    (0.25, 0.5),
    (0.75, 0.5),
    (1.25, 0.5),
    (1.75, 0.5),
    (2.5, 1.0),
    (3.5, 1.0),
    (5.0, 2.0),
)


def block_factors(exponents, sign):
    return jnp.repeat(jnp.exp2(sign * exponents.astype(jnp.float32)), BLOCK, axis=-1)


def fp4_levels(values):
    clipped = jnp.clip(values, -6.0, 6.0)
    magnitude = jnp.abs(clipped)
    level = jnp.zeros_like(magnitude)
    for middle, rise in LEVEL_STEPS:
        level = level + jnp.where(magnitude >= middle, rise, 0.0).astype(magnitude.dtype)
    return jnp.where(clipped < 0.0, -level, level)


def encoded_terms(base, fragment, exponents):
    inverse = block_factors(exponents, -1.0)
    scales = block_factors(exponents, 1.0)
    codes = fp4_levels((base - fragment.astype(jnp.float32)) * inverse).astype(jnp.bfloat16)
    codes = lax.optimization_barrier(codes)
    return codes.astype(jnp.float32) * scales


def outer_step(base, moment, summed, count):
    gradient = summed / count
    new_moment = MOMENTUM_COEF * moment + gradient
    new_base = base - OUTER_RATE * (gradient + MOMENTUM_COEF * new_moment)
    return (new_base, new_moment)


def normalize(rows, gain):
    values = rows.astype(jnp.float32)
    factor = lax.rsqrt(jnp.mean(values * values, axis=-1, keepdims=True) + 1e-05)
    return (values * factor * gain.astype(jnp.float32)).astype(jnp.bfloat16)


def body(tokens, norm_gain, fragment, exponents, base_weight, momentum):
    replicas = lax.axis_size("replica")
    base_block = lax.all_gather(base_weight, "replica", axis=0, tiled=True)
    terms = encoded_terms(base_block, fragment[0], exponents[0])
    summed = lax.psum_scatter(
        terms.astype(jnp.bfloat16), "replica", scatter_dimension=0, tiled=True
    ).astype(jnp.float32)
    new_base, new_moment = outer_step(base_weight, momentum, summed, replicas)
    weight_block = lax.all_gather(new_base.astype(jnp.bfloat16), "replica", axis=0, tiled=True)
    group_rows = lax.all_gather(normalize(tokens, norm_gain), "tensor", axis=0, tiled=True)
    total = jnp.dot(
        group_rows,
        lax.all_gather(weight_block, "fsdp", axis=0, tiled=True),
        preferred_element_type=jnp.float32,
    )
    keys_values = (total * group_rows.shape[1] ** (-0.5)).astype(jnp.bfloat16)
    return (new_base, new_moment, keys_values)


def solution(mesh):
    in_specs = (
        P(("replica", "fsdp", "tensor"), None),
        P(),
        P("replica", "fsdp", "tensor"),
        P("replica", "fsdp", "tensor"),
        P(("fsdp", "replica"), "tensor"),
        P(("fsdp", "replica"), "tensor"),
    )
    out_specs = (
        P(("fsdp", "replica"), "tensor"),
        P(("fsdp", "replica"), "tensor"),
        P(("replica", "fsdp"), "tensor"),
    )
    return jax.shard_map(body, mesh=mesh, in_specs=in_specs, out_specs=out_specs, check_vma=False)
```

profile of v0, /device:TPU:0, one launch (start us, length us, event | category | flops | bytes accessed | tf_op | source)
XLA Modules:
  0.0 347.2 jit_solution(16400052524570058241)
XLA Ops:
  7.2 0.0 all-gather.5.cloned.1.call-start
  7.2 0.7 all-gather.5.cloned.1.call-update
  7.9 0.0 reduce-scatter.4.cloned.1.call-start
  8.0 2.6 copy.17
  10.5 0.0 copy-done.1
  10.6 41.4 %all-gather.5.cloned.1.call-done = f32[768,1024]{1,0:T(8,128)} async-done(((f32[192,1024]{1,0:T(8,128)}), f32[768,1024]{1,0:T(8,128)}) %all-gather.5.cloned.1.call-update) | async-done | bytes 3145744 | tf_op jit(solution)/shard_map/all_gather | solution.py:58
  51.9 2.4 copy.18
  54.3 4.1 %fusion.3 = bf16[768,1024]{0,1:T(8,128)(2,1)S(1)} fusion(f32[768,1024]{0,1:T(8,128)S(1)} %copy.18, bf16[1,768,1024]{1,2,0:T(8,128)(2,1)} %copy.17, f32[768,32]{0,1:T(8,128)S(1)} %get-tuple-element.13), kind=kLoop, calls=%fused_computation.6 | loop fusion | flops 22806528 | bytes 6389760 | tf_op jit(solution)/shard_map/convert_element_type | solution.py:38
  58.4 0.3 fusion.6
  58.8 1.6 copy.24
  60.4 0.0 reduce-scatter.4.cloned.1.call-update
  60.4 0.0 all-gather.9.cloned.1.call-start
  60.5 1.5 copy.20
  62.0 1.3 copy.19
  63.3 0.0 copy-done.2
  63.4 5.6 %fusion = f32[384]{0:T(512)S(1)} fusion(bf16[384,12288]{1,0:T(8,128)(2,1)} %param.6), kind=kLoop, calls=%fused_computation.2 | loop fusion | flops 14155392 | bytes 9438720 | tf_op jit(solution)/shard_map/reduce_sum | solution.py:52
  69.0 17.5 %reduce-scatter.4.cloned.1.call-done = bf16[192,1024]{1,0:T(8,128)(2,1)} async-done(((bf16[768,1024]{1,0:T(8,128)(2,1)}), bf16[192,1024]{1,0:T(8,128)(2,1)}) %reduce-scatter.4.cloned.1.call-update) | async-done | bytes 393232
  86.5 2.0 copy.25
  88.5 2.4 fusion.7
  90.9 2.0 copy.21
  92.9 0.0 all-gather.9.cloned.1.call-update
  92.9 0.0 all-gather.7.cloned.1.call-start
  93.0 10.4 %fusion.2 = bf16[384,12288]{1,0:T(8,128)(2,1)} fusion(bf16[384,12288]{1,0:T(8,128)(2,1)} %param.6, f32[12288]{0:T(1024)S(1)} %convert_element_type.46, f32[384]{0:T(512)S(1)} %add_rsqrt_fusion), kind=kLoop, calls=%fused_computation.4 | loop fusion | flops 18874368 | bytes 18925056 | tf_op jit(solution)/shard_map/convert_element_type | solution.py:53
  103.4 0.0 all-gather.7.cloned.1.call-update
  103.4 0.2 all-gather.11.cloned.1.call-start
  103.6 15.8 %all-gather.9.cloned.1.call-done = bf16[768,1024]{1,0:T(8,128)(2,1)} async-done(((bf16[192,1024]{1,0:T(8,128)(2,1)}), bf16[768,1024]{1,0:T(8,128)(2,1)}) %all-gather.9.cloned.1.call-update) | async-done | bytes 1572880 | tf_op jit(solution)/shard_map/all_gather | solution.py:64
  119.4 0.0 all-gather.11.cloned.1.call-update
  119.4 1.2 copy.22
  120.6 1.2 copy.23
  121.8 35.6 %all-gather.7.cloned.1.call-done = bf16[768,12288]{1,0:T(8,128)(2,1)} async-done(((bf16[384,12288]{1,0:T(8,128)(2,1)}), bf16[768,12288]{1,0:T(8,128)(2,1)}) %all-gather.7.cloned.1.call-update) | async-done | bytes 18874384 | tf_op jit(solution)/shard_map/all_gather | solution.py:65
  157.4 157.4 %all-gather.11.cloned.1.call-done = bf16[12288,1024]{1,0:T(8,128)(2,1)} async-done(((bf16[768,1024]{1,0:T(8,128)(2,1)}), bf16[12288,1024]{1,0:T(8,128)(2,1)}) %all-gather.11.cloned.1.call-update) | async-done | bytes 25165840 | tf_op jit(solution)/shard_map/all_gather | solution.py:68
  314.8 25.8 %multiply_convert_fusion = bf16[768,1024]{1,0:T(8,128)(2,1)} fusion(bf16[768,12288]{1,0:T(8,128)(2,1)} %all-gather.7.cloned.1.call-done, bf16[12288,1024]{1,0:T(8,128)(2,1)} %all-gather.11.cloned.1.call-done), kind=kOutput, calls=%fused_computation.12 | convolution fusion | flops 19328925696 | bytes 45613056 | tf_op jit(solution)/shard_map/dot_general | solution.py:66
  (7 shorter events, 0.1 us)
Async XLA Ops:
  7.2 3.4 copy-start.1
  7.2 44.8 %all-gather.5.cloned.1.call-start = ((), (), s32[]{:S(2)}) async-start(), calls=%async_computation.1 | async-start | bytes 3932160 | tf_op jit(solution)/shard_map/all_gather | solution.py:58
  7.9 78.6 %reduce-scatter.4.cloned.1.call-start = ((), (), s32[]{:S(2)}) async-start(), calls=%async_computation.5 | async-start | bytes 1966080
  60.4 1.6 copy-start
  60.4 2.9 copy-start.2
  60.4 59.0 %all-gather.9.cloned.1.call-start = ((), (), s32[]{:S(2)}) async-start(), calls=%async_computation.3 | async-start | bytes 1966080 | tf_op jit(solution)/shard_map/all_gather | solution.py:64
  92.9 64.5 %all-gather.7.cloned.1.call-start = ((), (), s32[]{:S(2)}) async-start(), calls=%async_computation.2 | async-start | bytes 28311552 | tf_op jit(solution)/shard_map/all_gather | solution.py:65
  103.4 211.4 %all-gather.11.cloned.1.call-start = ((), (), s32[]{:S(2)}) async-start(), calls=%async_computation.4 | async-start | bytes 26738688 | tf_op jit(solution)/shard_map/all_gather | solution.py:68
Sparse Core Ops, SparseCore 0:
  9.7 42.2 all-gather.4
  60.6 25.8 reduce-scatter.3
  93.1 26.3 all-gather.8
  120.9 36.4 all-gather.6
  159.4 155.4 all-gather.10
where the time goes:
time: 348 us; the launch traced here: 347 us
  waiting for transfers between devices  268 us (77%)
  matrix products  25.8 us (7%)
  other arithmetic  23 us (7%)
  local copies, waits for them, and re-layouts  15.8 us (5%)
  between operations  13.8 us (4%)
    all_gather x1, waiting for transfers between devices, body(): lax.all_gather(weight_block, 'fsdp', axis=0, tiled=True)  157 us
    all_gather x1, waiting for transfers between devices, body(): base_block = lax.all_gather(base_weight, 'replica', axis=0, tiled=True)  41.4 us
    all_gather x1, waiting for transfers between devices, body(): lax.all_gather(normalize(tokens, norm_gain), 'tensor', axis=0, tiled=True)  35.6 us
    dot_general x1, matrix products, body(): jnp.dot(group_rows, lax.all_gather(weight_block, 'fsdp', axis=0, tiled=Tr...  25.8 us
    unnamed x6, waiting for transfers between devices  18.3 us
    all_gather x1, waiting for transfers between devices, body(): lax.all_gather(new_base.astype(jnp.bfloat16), 'replica', axis=0, tiled=True)  15.8 us
    unnamed x13, local copies, waits for them, and re-layouts  11.5 us
    convert_element_type x2, other arithmetic, normalize(): return (values * factor * gain.astype(jnp.float32)).astype(jnp.bfloat16)  10.4 us
  transfers between devices with their start and end apart: 5, of which 5 were waited for; matrix products, arithmetic and copies ran while one was open for 7% of the time, Pallas kernels for 0%

commit v1 on v0

v1 whole, which is shorter than its diff:
```python
import jax
import jax.numpy as jnp
from jax import lax
from jax.experimental import pallas as pl
from jax.experimental.pallas import tpu as pltpu
from jax.sharding import PartitionSpec as P

MESH = pl.DeviceIdType.MESH
F32, BF16 = jnp.float32, jnp.bfloat16
D, KVW, BLOCK, TOK = 12288, 1024, 32, 384
ROWS = 192
FROWS = 768
SLAB = 48
OUTER_RATE = 0.7
MOMENTUM_COEF = 0.9
CLS = ((0, 384), (384, 384), (768, 256))
ORDER = (("x", "y", "z"), ("z", "y", "x"), ("z", "x", "y"))
THRESH = ((0.25, 0.5), (0.75, 1.0), (1.25, 1.5), (1.75, 2.0), (2.5, 3.0), (3.5, 4.0), (5.0, 6.0))


def mod4(v):
    return lax.rem(v + 8, 4)


def kernel(
    tokens, gain, frag, exps, base, mom,
    nb_out, nm_out, kv_out,
    w0, w1, w2, tok, acc, kv, fb, rl, bs, ms, gn, ex, ep, er, erl, sc, iv, ss,
    loc, a_snd, a_rcv, e_snd, e_rcv, t_snd, t_rcv, g_snd, g_rcv, o_sem,
):
    W = (w0, w1, w2)
    rep = lax.axis_index("replica")
    fs = lax.axis_index("fsdp")
    core = lax.axis_index("tensor")
    pos = {"x": lax.rem(fs, 4), "y": lax.div(fs, 4), "z": rep}

    def nbr(axis, step):
        c = dict(pos)
        c[axis] = mod4(pos[axis] + step)
        return (c["z"], c["y"] * 4 + c["x"], core)

    other = (rep, fs, 1 - core)

    def remote(src, dst, ss_, rs_, dev):
        return pltpu.make_async_remote_copy(
            src_ref=src, dst_ref=dst, send_sem=ss_, recv_sem=rs_, device_id=dev, device_id_type=MESH
        )

    pending = []

    def go(copy):
        copy.start()
        pending.append(copy)

    l_ex = pltpu.make_async_copy(exps, ex, loc.at[0])
    l_ex.start()
    l_fr = pltpu.make_async_copy(frag.at[rep], fb.at[0], loc.at[1])
    l_fr.start()
    l_bs = pltpu.make_async_copy(base, bs, loc.at[2])
    l_bs.start()
    l_ms = pltpu.make_async_copy(mom, ms, loc.at[3])
    l_ms.start()
    l_gn = pltpu.make_async_copy(gain, gn, loc.at[4])
    l_gn.start()

    barrier = pltpu.get_barrier_semaphore()
    peers = [nbr(a, s) for a in "xyz" for s in (1, -1)] + [other]
    for p in peers:
        pl.semaphore_signal(barrier, inc=1, device_id=p, device_id_type=MESH)

    l_ex.wait()
    for d in range(4):
        packed = jnp.zeros((SLAB, 128), F32)
        for q in range(4):
            rows = ex[pl.ds(d * ROWS + q * SLAB, SLAB), :].astype(F32).astype(BF16)
            i = lax.broadcasted_iota(jnp.int32, (BLOCK, 128), 0)
            l = lax.broadcasted_iota(jnp.int32, (BLOCK, 128), 1)
            place = jnp.where(l == i + BLOCK * q, 1.0, 0.0).astype(BF16)
            packed = packed + jnp.dot(rows, place, preferred_element_type=F32)
        ep[d] = packed.astype(BF16)

    pl.semaphore_wait(barrier, len(peers))

    up, down = nbr("z", 1), nbr("z", -1)
    zu, zd, zo = mod4(rep + 1), mod4(rep - 1), mod4(rep + 2)

    e_cp = [
        remote(ep.at[zo], erl, e_snd.at[0], e_rcv.at[0], up),
        remote(ep.at[zu], er.at[1], e_snd.at[1], e_rcv.at[1], up),
        remote(ep.at[zd], er.at[2], e_snd.at[2], e_rcv.at[2], down),
        remote(erl, er.at[3], e_snd.at[3], e_rcv.at[3], up),
    ]

    def cols(c):
        return pl.ds(CLS[c][0], CLS[c][1])

    H = ROWS // 2

    def a2a(c):
        k = 6 * c
        cc = cols(c)
        return [
            remote(frag.at[zo, pl.ds(0, H), cc], rl.at[0, :, cc], a_snd.at[k], a_rcv.at[k], up),
            remote(frag.at[zo, pl.ds(H, H), cc], rl.at[1, :, cc], a_snd.at[k + 1], a_rcv.at[k + 1], down),
            remote(frag.at[zu, :, cc], fb.at[1, :, cc], a_snd.at[k + 2], a_rcv.at[k + 2], up),
            remote(frag.at[zd, :, cc], fb.at[2, :, cc], a_snd.at[k + 3], a_rcv.at[k + 3], down),
            remote(rl.at[0, :, cc], fb.at[3, pl.ds(0, H), cc], a_snd.at[k + 4], a_rcv.at[k + 4], up),
            remote(rl.at[1, :, cc], fb.at[3, pl.ds(H, H), cc], a_snd.at[k + 5], a_rcv.at[k + 5], down),
        ]

    A = [a2a(c) for c in range(3)]

    def a2a_send(c):
        for m in A[c][:4]:
            go(m)

    def a2a_relay(c):
        for m in (0, 1):
            A[c][m].wait_recv()
            go(A[c][4 + m])

    for m in e_cp[:3]:
        go(m)
    a2a_send(0)
    mine = pl.ds(pl.multiple_of(core * TOK, TOK), TOK)
    t_cp = remote(tokens, tok.at[mine, :], t_snd.at[0], t_rcv.at[0], other)
    l_tk = pltpu.make_async_copy(tokens, tok.at[mine, :], loc.at[5])

    def expand(slot):
        e = (ep[rep] if slot == 0 else er[slot]).astype(F32)
        small = jnp.exp2(e).astype(BF16)
        small_inv = jnp.exp2(-e).astype(BF16)
        l = lax.broadcasted_iota(jnp.int32, (128, KVW), 0)
        n = lax.broadcasted_iota(jnp.int32, (128, KVW), 1)
        for q in range(4):
            pick = jnp.where(l == BLOCK * q + lax.div(n, BLOCK), 1.0, 0.0).astype(BF16)
            sc[slot, pl.ds(q * SLAB, SLAB), :] = jnp.dot(small, pick, preferred_element_type=F32).astype(BF16)
            iv[slot, pl.ds(q * SLAB, SLAB), :] = jnp.dot(small_inv, pick, preferred_element_type=F32).astype(BF16)

    e_cp[0].wait_recv()
    go(e_cp[3])
    a2a_relay(0)
    a2a_send(1)
    go(t_cp)
    l_tk.start()
    expand(0)
    for s in (1, 2, 3):
        e_cp[s].wait_recv()
        expand(s)
    acc[...] = jnp.zeros_like(acc)
    l_fr.wait()
    l_bs.wait()
    l_ms.wait()
    l_gn.wait()

    def encode(c):
        lo, width = CLS[c]
        for m in A[c][2:]:
            m.wait_recv()
        row0 = pl.multiple_of(rep * ROWS, ROWS)

        def step(t, carry):
            rr = pl.ds(pl.multiple_of(t * SLAB, SLAB), SLAB)
            wr = pl.ds(pl.multiple_of(row0 + t * SLAB, SLAB), SLAB)
            g = gn[rr, :]
            for k in range(width // 128):
                cc = pl.ds(lo + 128 * k, 128)
                b = bs[rr, cc]
                total = jnp.zeros((SLAB, 128), F32)
                for s in range(4):
                    v = (b - fb[s, rr, cc].astype(F32)) * iv[s, rr, cc].astype(F32)
                    m = jnp.abs(v)
                    level = jnp.zeros_like(m)
                    for mid, val in THRESH:
                        level = jnp.where(m >= mid, val, level)
                    total = total + jnp.where(v < 0.0, -level, level) * sc[s, rr, cc].astype(F32)
                grad = total * 0.25
                nm = MOMENTUM_COEF * ms[rr, cc] + grad
                nb = b - OUTER_RATE * (grad + MOMENTUM_COEF * nm)
                ms[rr, cc] = nm
                bs[rr, cc] = nb
                W[c][pos["y"], pos["x"], wr, pl.ds(128 * k, 128)] = (nb * g).astype(BF16)
            return carry

        lax.fori_loop(0, ROWS // SLAB, step, 0)

    def region(c, xs, ys, z0, z1):
        return W[c].at[ys, xs, pl.ds(z0, z1), :]

    def place(c, **at):
        half = at.pop("half", None)
        xs, ys = at.get("x", slice(None)), at.get("y", slice(None))
        if "z" in at:
            r0, n = at["z"] * ROWS, ROWS
        else:
            r0, n = 0, FROWS
        if half is not None:
            n = n // 2
            r0 = r0 + half * n
        if not isinstance(r0, int):
            r0 = pl.multiple_of(r0, 96)
        return W[c].at[ys, xs, pl.ds(r0, n), :]

    def ring(c, axis, idx, fixed):
        k = 24 * c + 4 * idx
        out = []
        here = place(c, **{**fixed, axis: pos[axis]})
        for j, s in enumerate((1, -1)):
            out.append(remote(here, here, g_snd.at[k + j], g_rcv.at[k + j], nbr(axis, s)))
        for j, s in enumerate((1, -1)):
            part = place(c, **{**fixed, axis: mod4(pos[axis] - s), "half": j})
            out.append(remote(part, part, g_snd.at[k + 2 + j], g_rcv.at[k + 2 + j], nbr(axis, s)))
        return out

    OFF = (0, 1, -1, 2)
    R = {}
    for c in range(3):
        a, b, l = ORDER[c]
        R[c, 1] = ring(c, a, 0, {b: pos[b], l: pos[l]})
        R[c, 2] = ring(c, b, 1, {l: pos[l]})
        for i in range(4):
            R[c, 3, i] = ring(c, l, 2 + i, {b: mod4(pos[b] + OFF[i])})

    def send(*key):
        go(R[key][0])
        go(R[key][1])

    def fwd(*key):
        for j in (0, 1):
            R[key][j].wait_recv()
            go(R[key][2 + j])

    def halves(*key):
        R[key][2].wait_recv()
        R[key][3].wait_recv()

    def mm(c, count, coords):
        lo, width = CLS[c]
        cc = pl.ds(lo, width)

        def chunk(t, carry):
            yy, xx = coords(t)
            kk = pl.ds(pl.multiple_of((yy * 4 + xx) * FROWS, FROWS), FROWS)

            def block(m, carry):
                mr = pl.ds(pl.multiple_of(m * 256, 256), 256)
                acc[mr, cc] += jnp.dot(tok[mr, kk], W[c][yy, xx], preferred_element_type=F32)
                return carry

            return lax.fori_loop(0, 3, block, carry)

        lax.fori_loop(0, count, chunk, 0)

    def mm_near(c, i):
        if c == 1:
            yy = mod4(pos["y"] + OFF[i])
            mm(c, 3, lambda t: (yy, mod4(pos["x"] + t + lax.div(t, 2))))
        else:
            xx = mod4(pos["x"] + OFF[i])
            mm(c, 3, lambda t: (mod4(pos["y"] + t + lax.div(t, 2)), xx))

    def mm_far(c, i):
        if c == 0:
            yy = mod4(pos["y"] + OFF[i])
            mm(c, 4, lambda t: (yy, t))
        elif c == 1:
            yy = mod4(pos["y"] + OFF[i])
            mm(c, 1, lambda t: (yy, mod4(pos["x"] + 2)))
        else:
            xx = mod4(pos["x"] + OFF[i])
            mm(c, 1, lambda t: (mod4(pos["y"] + 2), xx))

    def squares(i):
        rr = pl.ds(i * 128, 128)

        def step(t, s):
            for k in range(4):
                v = tok[rr, pl.ds(pl.multiple_of(t * 512 + k * 128, 128), 128)].astype(F32)
                s = s + v * v
            return s

        s = lax.fori_loop(0, D // 512, step, jnp.zeros((128, 128), F32))
        mean = jnp.sum(s, axis=1, keepdims=True) * (1.0 / D)
        ss[rr, :] = jnp.broadcast_to(lax.rsqrt(mean + 1e-05) * (D ** -0.5), (128, 128))

    encode(0)
    send(0, 1)
    a2a_relay(1)
    a2a_send(2)
    fwd(0, 1)
    encode(1)
    send(1, 1)
    a2a_relay(2)
    halves(0, 1)
    send(0, 2)
    fwd(1, 1)
    encode(2)
    send(2, 1)
    outs = [
        pltpu.make_async_copy(bs, nb_out, o_sem.at[0]),
        pltpu.make_async_copy(ms, nm_out, o_sem.at[1]),
    ]
    for o in outs:
        o.start()
    halves(1, 1)
    send(1, 2)
    send(1, 3, 0)
    fwd(2, 1)
    send(0, 3, 0)
    halves(2, 1)
    send(2, 2)
    send(2, 3, 0)
    l_tk.wait()
    t_cp.wait_recv()
    squares(0)
    squares(1)
    fwd(0, 2)
    squares(2)
    squares(3)
    fwd(1, 3, 0)
    fwd(1, 2)
    send(1, 3, 1)
    squares(4)
    squares(5)
    fwd(2, 2)
    fwd(2, 3, 0)
    send(2, 3, 1)
    fwd(0, 3, 0)
    halves(0, 2)
    send(0, 3, 1)
    halves(1, 2)
    halves(2, 2)
    for i in range(4):
        if i:
            fwd(1, 3, i)
        if i < 2:
            send(1, 3, i + 2)
        mm_near(1, i)
        if i:
            fwd(2, 3, i)
        if i < 2:
            send(2, 3, i + 2)
        mm_near(2, i)
        if i:
            fwd(0, 3, i)
        if i < 2:
            send(0, 3, i + 2)
        halves(1, 3, i)
        mm_far(1, i)
        halves(2, 3, i)
        mm_far(2, i)
        halves(0, 3, i)
        mm_far(0, i)

    for m in range(3):
        mr = pl.ds(m * 256, 256)

        def scale(k, carry):
            cc = pl.ds(pl.multiple_of(k * 128, 128), 128)
            kv[mr, cc] = (acc[mr, cc] * ss[mr, :]).astype(BF16)
            return carry

        lax.fori_loop(0, KVW // 128, scale, 0)
        o = pltpu.make_async_copy(kv.at[mr, :], kv_out.at[mr, :], o_sem.at[2 + m])
        o.start()
        outs.append(o)
    for p in pending:
        p.wait_send()
    for o in outs:
        o.wait()


def body(tokens, norm_gain, fragment, exponents, base_weight, momentum):
    row0 = lax.axis_index("fsdp") * FROWS + lax.axis_index("replica") * ROWS
    gain = lax.dynamic_slice(norm_gain, (row0,), (ROWS,)).astype(F32)
    gain = jnp.broadcast_to(gain[:, None], (ROWS, 128))
    any_ = pl.BlockSpec(memory_space=pl.ANY)
    dma = pltpu.SemaphoreType.DMA
    vm = pltpu.VMEM
    return pl.pallas_call(
        kernel,
        out_shape=(
            jax.ShapeDtypeStruct((ROWS, KVW), F32),
            jax.ShapeDtypeStruct((ROWS, KVW), F32),
            jax.ShapeDtypeStruct((2 * TOK, KVW), BF16),
        ),
        in_specs=[any_] * 6,
        out_specs=[any_] * 3,
        scratch_shapes=[
            vm((4, 4, FROWS, CLS[0][1]), BF16),
            vm((4, 4, FROWS, CLS[1][1]), BF16),
            vm((4, 4, FROWS, CLS[2][1]), BF16),
            vm((2 * TOK, D), BF16),
            vm((2 * TOK, KVW), F32),
            vm((2 * TOK, KVW), BF16),
            vm((4, ROWS, KVW), BF16),
            vm((2, ROWS // 2, KVW), BF16),
            vm((ROWS, KVW), F32),
            vm((ROWS, KVW), F32),
            vm((ROWS, 128), F32),
            vm((4 * ROWS, BLOCK), jnp.int32),
            vm((4, SLAB, 128), BF16),
            vm((4, SLAB, 128), BF16),
            vm((SLAB, 128), BF16),
            vm((4, ROWS, KVW), BF16),
            vm((4, ROWS, KVW), BF16),
            vm((2 * TOK, 128), F32),
            dma((6,)),
            dma((18,)),
            dma((18,)),
            dma((4,)),
            dma((4,)),
            dma((1,)),
            dma((1,)),
            dma((72,)),
            dma((72,)),
            dma((5,)),
        ],
        compiler_params=pltpu.CompilerParams(
            collective_id=0, has_side_effects=True, vmem_limit_bytes=62 * 1024 * 1024
        ),
        cost_estimate=pl.CostEstimate(flops=2 * 768 * 12288 * 1024, bytes_accessed=30_000_000, transcendentals=0),
    )(tokens, gain, fragment.reshape(4, ROWS, KVW), exponents.reshape(4 * ROWS, BLOCK), base_weight, momentum)


def solution(mesh):
    in_specs = (
        P(("replica", "fsdp", "tensor"), None),
        P(),
        P("replica", "fsdp", "tensor"),
        P("replica", "fsdp", "tensor"),
        P(("fsdp", "replica"), "tensor"),
        P(("fsdp", "replica"), "tensor"),
    )
    out_specs = (
        P(("fsdp", "replica"), "tensor"),
        P(("fsdp", "replica"), "tensor"),
        P(("replica", "fsdp"), "tensor"),
    )
    return jax.shard_map(body, mesh=mesh, in_specs=in_specs, out_specs=out_specs, check_vma=False)
```

time: 348 us -> 157 us (0.45)
  waiting for transfers between devices: 268 us -> 0 us
  Pallas kernels: 0 us -> 148 us
  matrix products: 25.8 us -> 0 us
  other arithmetic: 23 us -> 0.77 us
  between operations: 13.8 us -> 0.66 us
  local copies, waits for them, and re-layouts: 15.8 us -> 6.81 us
    all_gather x4 -> x0, waiting for transfers between devices: 250 us -> none  [the longest x1 157 us: body(): lax.all_gather(weight_block, 'fsdp', axis=0, tiled=True)]
    pallas_call x0 -> x1, Pallas kernels: none -> 148 us  [body(): pl.pallas_call(kernel, out_shape=(jax.ShapeDtypeStruct((ROWS, KVW), F32),...]
    dot_general x1 -> x0, matrix products: 25.8 us -> none  [body(): jnp.dot(group_rows, lax.all_gather(weight_block, 'fsdp', axis=0, tiled=Tr...]
    unnamed x6 -> x0, waiting for transfers between devices: 18.3 us -> none
    convert_element_type x5 -> x1, other arithmetic: 17.3 us -> 0.77 us  [body(): gain = lax.dynamic_slice(norm_gain, (row0,), (ROWS,)).astype(F32)]
    reduce_sum x1 -> x0, other arithmetic: 5.62 us -> none  [normalize(): jnp.mean(values * values, axis=-1, keepdims=True) + 1e-05]
    unnamed x13 -> x8, local copies, waits for them, and re-layouts: 11.5 us -> 6.08 us
  transfers between devices with their start and end apart: 5 -> 0, of which waited for: 5 -> 0; matrix products, arithmetic and copies ran while one was open for 7% -> 0% of each run, Pallas kernels for 0% -> 0%
where the time goes in v1:
time: 157 us
  Pallas kernels  148 us (94%)
  local copies, waits for them, and re-layouts  6.81 us (4%)
    pallas_call x1, Pallas kernels, body(): pl.pallas_call(kernel, out_shape=(jax.ShapeDtypeStruct((ROWS, KVW), F32),...  148 us
    unnamed x8, local copies, waits for them, and re-layouts  6.08 us

profile of v1, /device:TPU:0, one launch (start us, length us, event | category | flops | bytes accessed | tf_op | source)
XLA Modules:
  0.0 156.6 jit_solution(16182674520182997026)
XLA Ops:
  0.6 0.8 dynamic-slice_convert_fusion
  1.4 0.7 broadcast_in_dim.2.gain
  2.1 1.8 %copy.9 = s32[1,768,32]{2,1,0:T(8,128)} copy(s32[1,768,32]{1,2,0:T(8,128)} %param.9) | data formatting | bytes 196608 | tf_op args[3]
  3.9 148.3 %shard_map.85 = (f32[192,1024]{1,0:T(8,128)}, f32[192,1024]{1,0:T(8,128)}, bf16[768,1024]{1,0:T(8,128)(2,1)}) custom-call(bf16[384,12288]{1,0:T(8,128)(2,1)} %tokens.1, f32[192,128]{1,0:T(8,128)} %broadcast_in_dim.2.gain, bf16[4,192,1024]{2,1,0:T(8,128)(2,1)} %bitcast.3, s32[768,32]{1,0:T(8,128)} %bitcast.2, f32[192,1024]{1,0:T(8,128)} %base.1, f32[192,1024]{1,0:T(8,128)} %mom.1), custom_call_target="tpu_custom_call" | custom-call | flops 19327352832 | bytes 30000000 | tf_op jit(solution)/shard_map/pallas_call | solution.py:380
  152.3 0.0 copy-start.1
  152.3 0.0 copy-start
  152.3 2.2 %copy.13 = f32[192,1024]{1,0:T(8,128)} copy(f32[192,1024]{1,0:T(8,128)} %get-tuple-element.6) | data formatting | bytes 1572864
  154.5 0.0 copy-done.1
  154.5 0.9 copy.14
  155.4 0.0 copy-done
  155.4 1.1 copy.15
Async XLA Ops:
  152.3 2.3 %copy-start.1 = (f32[192,1024]{1,0:T(8,128)S(1)}, f32[192,1024]{1,0:T(8,128)}, u32[]{:S(2)}) copy-start(f32[192,1024]{1,0:T(8,128)} %get-tuple-element.7) | copy-start | bytes 2359300
  152.3 3.1 %copy-start = (bf16[768,1024]{1,0:T(8,128)(2,1)S(1)}, bf16[768,1024]{1,0:T(8,128)(2,1)}, u32[]{:S(2)}) copy-start(bf16[768,1024]{1,0:T(8,128)(2,1)} %get-tuple-element.8) | copy-start | bytes 4718596

commit v2 on v1

v2 whole, which is shorter than its diff:
```python
import jax
import jax.numpy as jnp
from jax import lax
from jax.experimental import pallas as pl
from jax.experimental.pallas import tpu as pltpu
from jax.sharding import PartitionSpec as P

MESH = pl.DeviceIdType.MESH
F32, BF16 = jnp.float32, jnp.bfloat16
D, KVW, BLOCK, TOK = 12288, 1024, 32, 384
ROWS = 192
FROWS = 768
SLAB = 48
OUTER_RATE = 0.7
MOMENTUM_COEF = 0.9
CLS = ((0, 384), (384, 384), (768, 256))
ORDER = (("x", "y", "z"), ("z", "y", "x"), ("z", "x", "y"))

SCHEDULE = (
    ("S", "r", 0), ("S", "d", 0), ("S", "r", 1), ("S", "d", 1), ("W", "r", 0), ("S", "f", 0), ("S", "r", 2),
    ("W", "r", 1), ("S", "f", 1), ("S", "d", 2), ("W", "d", 0), ("W", "f", 0), ("E", 0), ("S", "1", 0),
    ("S", "2", 0, 0), ("W", "r", 2), ("S", "f", 2), ("S", "3", 0, 0), ("W", "d", 1), ("W", "f", 1), ("E", 1),
    ("S", "3", 1, 0), ("S", "2", 1, 0), ("S", "1", 1), ("W", "d", 2), ("D", "r", 0), ("W", "f", 2), ("E", 2),
    ("W", "1", 0), ("S", "1h", 0), ("S", "2", 2, 0), ("W", "2", 0, 0), ("S", "2h", 0, 0), ("S", "2", 0, 1),
    ("S", "1", 2), ("S", "3", 0, 1), ("S", "2", 0, 2), ("D", "d", 0), ("D", "r", 1), ("W", "3", 1, 0),
    ("S", "3h", 1, 0), ("W", "3", 0, 0), ("S", "3h", 0, 0), ("W", "1", 1), ("S", "3", 1, 1), ("W", "1h", 0),
    ("S", "2", 0, 3), ("S", "3", 1, 2), ("S", "1h", 1), ("D", "d", 1), ("D", "f", 0), ("W", "1", 2), ("S", "1h", 2),
    ("W", "2", 0, 1), ("S", "2h", 0, 1), ("W", "2", 2, 0), ("S", "2h", 2, 0), ("S", "3", 0, 2), ("S", "2", 2, 1),
    ("W", "2", 1, 0), ("S", "2h", 1, 0), ("D", "r", 2), ("D", "f", 1), ("W", "2", 0, 2), ("S", "2h", 0, 2),
    ("S", "2", 2, 2), ("W", "3", 0, 1), ("S", "3h", 0, 1), ("S", "2", 1, 1), ("S", "3", 0, 3), ("W", "3", 1, 1),
    ("S", "3h", 1, 1), ("D", "d", 2), ("D", "1", 0), ("D", "f", 2), ("W", "1h", 2), ("S", "2", 2, 3),
    ("W", "2", 0, 3), ("S", "2h", 0, 3), ("S", "3", 0, 4), ("C", "sq", 0), ("D", "2", 0, 0), ("D", "3", 0, 0),
    ("D", "3", 1, 0), ("D", "2", 1, 0), ("W", "2", 2, 1), ("S", "2h", 2, 1), ("S", "2", 1, 2), ("C", "sq", 1),
    ("D", "1", 1), ("D", "1h", 0), ("D", "2", 2, 0), ("D", "2h", 0, 0), ("W", "2", 2, 2), ("S", "2h", 2, 2),
    ("C", "sq", 2), ("W", "1h", 1), ("S", "3", 1, 3), ("C", "sq", 3), ("W", "2", 1, 1), ("S", "2h", 1, 1),
    ("C", "sq", 4), ("W", "2", 2, 3), ("S", "2h", 2, 3), ("S", "2", 1, 3), ("C", "sq", 5), ("W", "3", 1, 2),
    ("S", "3h", 1, 2), ("S", "3", 2, 0), ("D", "2", 0, 1), ("D", "1", 2), ("D", "3", 0, 1), ("D", "2", 0, 2),
    ("W", "2", 1, 2), ("S", "2h", 1, 2), ("D", "3h", 1, 0), ("D", "3h", 0, 0), ("D", "3", 1, 1), ("D", "2", 0, 3),
    ("W", "3", 1, 3), ("S", "3h", 1, 3), ("C", "mm", 1, 0, "near"), ("S", "3", 2, 1), ("W", "3", 0, 2),
    ("S", "3h", 0, 2), ("W", "2", 1, 3), ("S", "3", 1, 4), ("W", "3", 0, 3), ("S", "3h", 0, 3), ("S", "2h", 1, 3),
    ("W", "3h", 1, 0), ("W", "3h", 1, 1), ("W", "3h", 1, 2), ("D", "3", 1, 2), ("D", "1h", 1), ("D", "1h", 2),
    ("D", "2h", 0, 1), ("W", "3h", 1, 3), ("C", "mm", 1, 0, "far"), ("W", "3", 2, 0), ("S", "3h", 2, 0),
    ("S", "3", 0, 5), ("S", "3", 2, 2), ("S", "3", 2, 3), ("W", "3h", 0, 0), ("W", "3h", 0, 1), ("D", "2h", 2, 0),
    ("D", "3", 0, 2), ("D", "2", 2, 1), ("D", "2h", 1, 0), ("W", "3h", 0, 2), ("D", "2h", 0, 2), ("D", "2", 2, 2),
    ("D", "3h", 0, 1), ("D", "2", 1, 1), ("W", "3h", 0, 3), ("C", "mm", 0, 0, "all"), ("S", "3", 1, 5),
    ("W", "3", 2, 1), ("S", "3h", 2, 1), ("S", "3", 2, 4), ("W", "3", 2, 2), ("D", "3", 0, 3), ("D", "3h", 1, 1),
    ("D", "2", 2, 3), ("D", "2h", 0, 3), ("W", "3", 2, 3), ("C", "mm", 2, 0, "near"), ("W", "3", 1, 4),
    ("C", "mm", 1, 1, "near"), ("W", "3", 0, 4), ("S", "3h", 0, 4), ("S", "3h", 2, 2), ("S", "3h", 2, 3),
    ("S", "3", 2, 5), ("W", "2h", 0, 0), ("W", "2h", 0, 1), ("W", "2h", 0, 3), ("W", "2h", 0, 2), ("S", "3", 0, 6),
    ("S", "3h", 1, 4), ("D", "3", 0, 4), ("D", "2h", 2, 1), ("D", "2", 1, 2), ("D", "2h", 2, 2), ("W", "3", 2, 4),
    ("C", "mm", 2, 1, "near"), ("W", "3h", 2, 0), ("W", "3h", 2, 1), ("W", "3h", 2, 2), ("W", "3h", 2, 3),
    ("C", "mm", 2, 0, "far"), ("D", "3", 1, 3), ("D", "2h", 1, 1), ("D", "2h", 2, 3), ("D", "2", 1, 3),
    ("W", "3h", 0, 4), ("C", "mm", 0, 1, "all"), ("W", "2h", 1, 0), ("W", "2h", 1, 1), ("W", "2h", 1, 3),
    ("W", "2h", 1, 2), ("S", "3", 1, 6), ("S", "3h", 2, 4), ("W", "3", 1, 5), ("C", "mm", 1, 2, "near"),
    ("W", "2h", 2, 0), ("W", "2h", 2, 1), ("W", "2h", 2, 3), ("W", "2h", 2, 2), ("S", "3", 2, 6), ("D", "3h", 1, 2),
    ("D", "3", 2, 0), ("D", "2h", 1, 2), ("D", "3h", 1, 3), ("W", "3", 2, 5), ("C", "mm", 2, 2, "near"),
    ("W", "3", 0, 5), ("S", "3h", 0, 5), ("W", "3h", 1, 4), ("C", "mm", 1, 1, "far"), ("D", "3", 2, 1),
    ("D", "3h", 0, 2), ("D", "3", 1, 4), ("D", "3h", 0, 3), ("W", "3h", 2, 4), ("C", "mm", 2, 1, "far"),
    ("D", "2h", 1, 3), ("D", "3h", 2, 0), ("D", "3", 0, 5), ("D", "3", 2, 2), ("W", "3", 0, 6), ("S", "3h", 0, 6),
    ("S", "3h", 2, 5), ("S", "3h", 1, 5), ("D", "3", 2, 3), ("D", "3", 1, 5), ("D", "3h", 2, 1), ("D", "3", 2, 4),
    ("W", "3h", 0, 5), ("C", "mm", 0, 2, "all"), ("W", "3", 1, 6), ("S", "3h", 1, 6), ("W", "3", 2, 6),
    ("S", "3h", 2, 6), ("C", "mm", 1, 3, "near"), ("C", "mm", 2, 3, "near"), ("W", "3h", 0, 6),
    ("C", "mm", 0, 3, "all"), ("W", "3h", 1, 5), ("C", "mm", 1, 2, "far"), ("W", "3h", 2, 5),
    ("C", "mm", 2, 2, "far"), ("W", "3h", 2, 6), ("C", "mm", 2, 3, "far"), ("D", "3h", 0, 4), ("D", "3h", 2, 2),
    ("D", "3h", 2, 3), ("D", "3", 2, 5), ("W", "3h", 1, 6), ("C", "mm", 1, 3, "far"),
)

THRESH = ((0.25, 0.5), (0.75, 1.0), (1.25, 1.5), (1.75, 2.0), (2.5, 3.0), (3.5, 4.0), (5.0, 6.0))


def mod4(v):
    return lax.rem(v + 8, 4)


def kernel(
    tokens, gain, frag, exps, base, mom,
    nb_out, nm_out, kv_out,
    w0, w1, w2, tok, acc, kv, fb, rl, bs, ms, gb, gf, gn, ex, eb, er, erl, sc, iv, ss,
    loc, a_snd, a_rcv, e_snd, e_rcv, t_snd, t_rcv, g_snd, g_rcv, o_sem,
):
    W = (w0, w1, w2)
    rep = lax.axis_index("replica")
    fs = lax.axis_index("fsdp")
    core = lax.axis_index("tensor")
    pos = {"x": lax.rem(fs, 4), "y": lax.div(fs, 4), "z": rep}

    def nbr(axis, step):
        c = dict(pos)
        c[axis] = mod4(pos[axis] + step)
        return (c["z"], c["y"] * 4 + c["x"], core)

    other = (rep, fs, 1 - core)

    def remote(src, dst, ss_, rs_, dev):
        return pltpu.make_async_remote_copy(
            src_ref=src, dst_ref=dst, send_sem=ss_, recv_sem=rs_, device_id=dev, device_id_type=MESH
        )

    pending = []

    def go(copy):
        copy.start()
        pending.append(copy)

    l_ex = pltpu.make_async_copy(exps, ex, loc.at[0])
    l_ex.start()
    l_fr = pltpu.make_async_copy(frag.at[rep], fb.at[0], loc.at[1])
    l_fr.start()
    l_bs = pltpu.make_async_copy(base, bs, loc.at[2])
    l_bs.start()
    l_ms = pltpu.make_async_copy(mom, ms, loc.at[3])
    l_ms.start()
    l_gn = pltpu.make_async_copy(gain, gb, loc.at[4])
    l_gn.start()

    barrier = pltpu.get_barrier_semaphore()
    peers = [nbr(a, s) for a in "xyz" for s in (1, -1)] + [other]
    for p in peers:
        pl.semaphore_signal(barrier, inc=1, device_id=p, device_id_type=MESH)

    l_ex.wait()
    eb[...] = ex[...].astype(F32).astype(BF16)

    pl.semaphore_wait(barrier, len(peers))

    up, down = nbr("z", 1), nbr("z", -1)
    zu, zd, zo = mod4(rep + 1), mod4(rep - 1), mod4(rep + 2)

    def window(d):
        return eb.at[:, pl.ds(pl.multiple_of(128 * lax.div(3 * d, 2), 128), 256)]

    e_cp = [
        remote(window(zo), erl, e_snd.at[0], e_rcv.at[0], up),
        remote(window(zu), er.at[1], e_snd.at[1], e_rcv.at[1], up),
        remote(window(zd), er.at[2], e_snd.at[2], e_rcv.at[2], down),
        remote(erl, er.at[3], e_snd.at[3], e_rcv.at[3], up),
    ]

    def cols(c):
        return pl.ds(CLS[c][0], CLS[c][1])

    H = ROWS // 2

    def a2a(c):
        k = 6 * c
        cc = cols(c)
        return [
            remote(frag.at[zo, pl.ds(0, H), cc], rl.at[0, :, cc], a_snd.at[k], a_rcv.at[k], up),
            remote(frag.at[zo, pl.ds(H, H), cc], rl.at[1, :, cc], a_snd.at[k + 1], a_rcv.at[k + 1], down),
            remote(frag.at[zu, :, cc], fb.at[1, :, cc], a_snd.at[k + 2], a_rcv.at[k + 2], up),
            remote(frag.at[zd, :, cc], fb.at[2, :, cc], a_snd.at[k + 3], a_rcv.at[k + 3], down),
            remote(rl.at[0, :, cc], fb.at[3, pl.ds(0, H), cc], a_snd.at[k + 4], a_rcv.at[k + 4], up),
            remote(rl.at[1, :, cc], fb.at[3, pl.ds(H, H), cc], a_snd.at[k + 5], a_rcv.at[k + 5], down),
        ]

    for m in e_cp[:3]:
        go(m)
    mine = pl.ds(pl.multiple_of(core * TOK, TOK), TOK)
    t_cp = remote(tokens, tok.at[mine, :], t_snd.at[0], t_rcv.at[0], other)
    l_tk = pltpu.make_async_copy(tokens, tok.at[mine, :], loc.at[5])

    off = 64 * lax.rem(rep, 2)

    def expand(slot):
        e = (window(rep)[...] if slot == 0 else er[slot]).astype(F32)
        j = lax.broadcasted_iota(jnp.int32, (BLOCK, KVW), 0)
        n = lax.broadcasted_iota(jnp.int32, (BLOCK, KVW), 1)
        pick = jnp.where(j == lax.div(n, BLOCK), 1.0, 0.0).astype(BF16)
        for ref, sign in ((sc, 1.0), (iv, -1.0)):
            small = jnp.exp2(sign * e).astype(BF16)
            full = lax.dot_general(small, pick, (((0,), (0,)), ((), ())), preferred_element_type=F32)
            ref[slot] = full.astype(BF16)

    def prepare():
        go(t_cp)
        l_tk.start()
        expand(0)
        e_cp[0].wait_recv()
        go(e_cp[3])
        l_gn.wait()
        gf[...] = gb[...].astype(F32)
        first = 6 * fs + lax.div(3 * rep, 2)
        i = lax.broadcasted_iota(jnp.int32, (128, 128), 0)
        l = lax.broadcasted_iota(jnp.int32, (128, 128), 1)
        for h in range(2):
            row = jnp.broadcast_to(gf[pl.ds(first + h, 1), :], (128, 128))
            column = jnp.sum(jnp.where(i == l, row, 0.0), axis=1, keepdims=True)
            gn[pl.ds(128 * h, 128), :] = jnp.broadcast_to(column, (128, 128))
        for s in (1, 2, 3):
            e_cp[s].wait_recv()
            expand(s)
        acc[...] = jnp.zeros_like(acc)
        l_fr.wait()
        l_bs.wait()
        l_ms.wait()

    def encode(c):
        lo, width = CLS[c]
        row0 = pl.multiple_of(rep * ROWS, ROWS)

        def step(t, carry):
            rr = pl.ds(pl.multiple_of(t * SLAB, SLAB), SLAB)
            wr = pl.ds(pl.multiple_of(row0 + t * SLAB, SLAB), SLAB)
            fr = pl.ds(pl.multiple_of(off + t * SLAB, 16), SLAB)
            g = gn[fr, :]
            for k in range(width // 128):
                cc = pl.ds(lo + 128 * k, 128)
                b = bs[rr, cc]
                total = jnp.zeros((SLAB, 128), F32)
                for s in range(4):
                    v = (b - fb[s, rr, cc].astype(F32)) * iv[s, fr, cc].astype(F32)
                    m = jnp.abs(v)
                    level = jnp.zeros_like(m)
                    for mid, val in THRESH:
                        level = jnp.where(m >= mid, val, level)
                    total = total + jnp.where(v < 0.0, -level, level) * sc[s, fr, cc].astype(F32)
                grad = total * 0.25
                nm = MOMENTUM_COEF * ms[rr, cc] + grad
                nb = b - OUTER_RATE * (grad + MOMENTUM_COEF * nm)
                ms[rr, cc] = nm
                bs[rr, cc] = nb
                W[c][pos["y"], pos["x"], wr, pl.ds(128 * k, 128)] = (nb * g).astype(BF16)
            return carry

        lax.fori_loop(0, ROWS // SLAB, step, 0)

    def place(c, **at):
        half = at.pop("half", None)
        xs, ys = at.get("x", slice(None)), at.get("y", slice(None))
        if "z" in at:
            r0, n = at["z"] * ROWS, ROWS
        else:
            r0, n = 0, FROWS
        if half is not None:
            n = n // 2
            r0 = r0 + half * n
        if not isinstance(r0, int):
            r0 = pl.multiple_of(r0, 96)
        return W[c].at[ys, xs, pl.ds(r0, n), :]

    M = {}
    OFF = (0, 1, -1, 2)
    for c in range(3):
        m = a2a(c)
        M["r", c], M["d", c], M["f", c] = m[:2], m[2:4], m[4:]

    def ring(level, c, i, k, axis, fixed):
        k = 48 * c + 4 * k
        key = (c,) if level == "1" else (c, i)
        here = place(c, **{**fixed, axis: pos[axis]})
        M[(level,) + key] = [
            remote(here, here, g_snd.at[k + j], g_rcv.at[k + j], nbr(axis, s)) for j, s in enumerate((1, -1))
        ]
        M[(level + "h",) + key] = []
        for j, s in enumerate((1, -1)):
            part = place(c, **{**fixed, axis: mod4(pos[axis] - s), "half": j})
            M[(level + "h",) + key].append(
                remote(part, part, g_snd.at[k + 2 + j], g_rcv.at[k + 2 + j], nbr(axis, s))
            )

    for c in range(3):
        a, b, l = ORDER[c]
        ring("1", c, 0, 0, a, {b: pos[b], l: pos[l]})
        for i in range(4):
            at = mod4(pos[a] + OFF[i])
            ring("2", c, i, 1 + i, b, {a: at, l: pos[l]})
            ring("3", c, i, 5 + i, l, {a: at, b: pos[b]})
        for i in range(1, 4):
            ring("3", c, 3 + i, 8 + i, l, {b: mod4(pos[b] + OFF[i])})

    def mm(c, count, coords):
        lo, width = CLS[c]
        cc = pl.ds(lo, width)

        def chunk(t, carry):
            yy, xx = coords(t)
            kk = pl.ds(pl.multiple_of((yy * 4 + xx) * FROWS, FROWS), FROWS)

            def block(m, carry):
                mr = pl.ds(pl.multiple_of(m * 256, 256), 256)
                acc[mr, cc] += jnp.dot(tok[mr, kk], W[c][yy, xx], preferred_element_type=F32)
                return carry

            return lax.fori_loop(0, 3, block, carry)

        lax.fori_loop(0, count, chunk, 0)

    def mm_near(c, i):
        if c == 1:
            yy = mod4(pos["y"] + OFF[i])
            mm(c, 3, lambda t: (yy, mod4(pos["x"] + t + lax.div(t, 2))))
        else:
            xx = mod4(pos["x"] + OFF[i])
            mm(c, 3, lambda t: (mod4(pos["y"] + t + lax.div(t, 2)), xx))

    def mm_far(c, i):
        if c == 0:
            yy = mod4(pos["y"] + OFF[i])
            mm(c, 4, lambda t: (yy, t))
        elif c == 1:
            yy = mod4(pos["y"] + OFF[i])
            mm(c, 1, lambda t: (yy, mod4(pos["x"] + 2)))
        else:
            xx = mod4(pos["x"] + OFF[i])
            mm(c, 1, lambda t: (mod4(pos["y"] + 2), xx))

    def squares(i):
        rr = pl.ds(i * 128, 128)

        def step(t, s):
            for k in range(4):
                v = tok[rr, pl.ds(pl.multiple_of(t * 512 + k * 128, 128), 128)].astype(F32)
                s = s + v * v
            return s

        s = lax.fori_loop(0, D // 512, step, jnp.zeros((128, 128), F32))
        mean = jnp.sum(s, axis=1, keepdims=True) * (1.0 / D)
        ss[rr, :] = jnp.broadcast_to(lax.rsqrt(mean + 1e-05) * (D ** -0.5), (128, 128))

    outs = []
    left = []
    encoded = 0
    squared = 0
    for kind, *key in SCHEDULE:
        key = tuple(key)
        if kind == "S":
            for m in M[key]:
                m.start()
            left.append(key)
        elif kind == "W":
            if key == ("d", 0):
                prepare()
            for m in M[key]:
                m.wait_recv()
        elif kind == "D":
            for m in M[key]:
                m.wait_send()
            left.remove(key)
        elif kind == "E":
            encode(*key)
            encoded += 1
            if encoded == 3:
                outs.append(pltpu.make_async_copy(bs, nb_out, o_sem.at[0]))
                outs.append(pltpu.make_async_copy(ms, nm_out, o_sem.at[1]))
                for o in outs:
                    o.start()
        elif key[0] == "sq":
            if squared == 0:
                l_tk.wait()
                t_cp.wait_recv()
            squared += 1
            squares(key[1])
        elif key[3] == "near":
            mm_near(key[1], key[2])
        else:
            mm_far(key[1], key[2])

    for m in range(3):
        mr = pl.ds(m * 256, 256)

        def scale(k, carry):
            cc = pl.ds(pl.multiple_of(k * 128, 128), 128)
            kv[mr, cc] = (acc[mr, cc] * ss[mr, :]).astype(BF16)
            return carry

        lax.fori_loop(0, KVW // 128, scale, 0)
        o = pltpu.make_async_copy(kv.at[mr, :], kv_out.at[mr, :], o_sem.at[2 + m])
        o.start()
        outs.append(o)
    for key in left:
        for m in M[key]:
            m.wait_send()
    for p in pending:
        p.wait_send()
    for o in outs:
        o.wait()


def body(tokens, norm_gain, fragment, exponents, base_weight, momentum):
    any_ = pl.BlockSpec(memory_space=pl.ANY)
    dma = pltpu.SemaphoreType.DMA
    vm = pltpu.VMEM
    return pl.pallas_call(
        kernel,
        out_shape=(
            jax.ShapeDtypeStruct((ROWS, KVW), F32),
            jax.ShapeDtypeStruct((ROWS, KVW), F32),
            jax.ShapeDtypeStruct((2 * TOK, KVW), BF16),
        ),
        in_specs=[any_] * 6,
        out_specs=[any_] * 3,
        scratch_shapes=[
            vm((4, 4, FROWS, CLS[0][1]), BF16),
            vm((4, 4, FROWS, CLS[1][1]), BF16),
            vm((4, 4, FROWS, CLS[2][1]), BF16),
            vm((2 * TOK, D), BF16),
            vm((2 * TOK, KVW), F32),
            vm((2 * TOK, KVW), BF16),
            vm((4, ROWS, KVW), BF16),
            vm((2, ROWS // 2, KVW), BF16),
            vm((ROWS, KVW), F32),
            vm((ROWS, KVW), F32),
            vm((D // 128, 128), BF16),
            vm((D // 128, 128), F32),
            vm((256, 128), F32),
            vm((BLOCK, 4 * ROWS), jnp.int32),
            vm((BLOCK, 4 * ROWS), BF16),
            vm((4, BLOCK, 256), BF16),
            vm((BLOCK, 256), BF16),
            vm((4, 256, KVW), BF16),
            vm((4, 256, KVW), BF16),
            vm((2 * TOK, 128), F32),
            dma((6,)),
            dma((18,)),
            dma((18,)),
            dma((4,)),
            dma((4,)),
            dma((1,)),
            dma((1,)),
            dma((144,)),
            dma((144,)),
            dma((5,)),
        ],
        compiler_params=pltpu.CompilerParams(
            collective_id=0, has_side_effects=True, vmem_limit_bytes=62 * 1024 * 1024
        ),
        cost_estimate=pl.CostEstimate(flops=2 * 768 * 12288 * 1024, bytes_accessed=30_000_000, transcendentals=0),
    )(
        tokens,
        norm_gain.reshape(D // 128, 128),
        fragment.reshape(4, ROWS, KVW),
        exponents[0].T,
        base_weight,
        momentum,
    )


def solution(mesh):
    in_specs = (
        P(("replica", "fsdp", "tensor"), None),
        P(),
        P("replica", "fsdp", "tensor"),
        P("replica", "fsdp", "tensor"),
        P(("fsdp", "replica"), "tensor"),
        P(("fsdp", "replica"), "tensor"),
    )
    out_specs = (
        P(("fsdp", "replica"), "tensor"),
        P(("fsdp", "replica"), "tensor"),
        P(("replica", "fsdp"), "tensor"),
    )
    return jax.shard_map(body, mesh=mesh, in_specs=in_specs, out_specs=out_specs, check_vma=False)
```

time: 157 us -> 139 us (0.89)
  Pallas kernels: 148 us -> 134 us
  local copies, waits for them, and re-layouts: 6.81 us -> 4.27 us
    pallas_call x1, Pallas kernels: 148 us -> 134 us  [body(): pl.pallas_call(kernel, out_shape=(jax.ShapeDtypeStruct((ROWS, KVW), F32),...]
    unnamed x8 -> x7, local copies, waits for them, and re-layouts: 6.08 us -> 4.27 us
where the time goes in v2:
time: 139 us
  Pallas kernels  134 us (96%)
  local copies, waits for them, and re-layouts  4.27 us (3%)
    pallas_call x1, Pallas kernels, body(): pl.pallas_call(kernel, out_shape=(jax.ShapeDtypeStruct((ROWS, KVW), F32),...  134 us
    unnamed x7, local copies, waits for them, and re-layouts  4.27 us

profile of v2, /device:TPU:0, one launch (start us, length us, event | category | flops | bytes accessed | tf_op | source)
XLA Modules:
  0.0 139.1 jit_solution(466565388412055018)
XLA Ops:
  0.6 134.2 %shard_map.85 = (f32[192,1024]{1,0:T(8,128)}, f32[192,1024]{1,0:T(8,128)}, bf16[768,1024]{1,0:T(8,128)(2,1)}) custom-call(bf16[384,12288]{1,0:T(8,128)(2,1)} %tokens.1, bf16[96,128]{1,0:T(8,128)(2,1)} %bitcast.7, bf16[4,192,1024]{2,1,0:T(8,128)(2,1)} %bitcast.5, s32[32,768]{1,0:T(8,128)} %bitcast.6, f32[192,1024]{1,0:T(8,128)} %base.1, f32[192,1024]{1,0:T(8,128)} %mom.1), custom_call_target="tpu_custom_call" | custom-call | flops 19327352832 | bytes 30000000 | tf_op jit(solution)/shard_map/pallas_call | solution.py:383
  134.8 0.0 copy-start.1
  134.8 0.0 copy-start
  134.8 2.2 %copy.12 = f32[192,1024]{1,0:T(8,128)} copy(f32[192,1024]{1,0:T(8,128)} %get-tuple-element.6) | data formatting | bytes 1572864
  137.1 0.0 copy-done.1
  137.1 0.9 copy.13
  137.9 0.0 copy-done
  137.9 1.1 copy.14
Async XLA Ops:
  134.8 2.3 %copy-start.1 = (f32[192,1024]{1,0:T(8,128)S(1)}, f32[192,1024]{1,0:T(8,128)}, u32[]{:S(2)}) copy-start(f32[192,1024]{1,0:T(8,128)} %get-tuple-element.7) | copy-start | bytes 2359300
  134.8 3.1 %copy-start = (bf16[768,1024]{1,0:T(8,128)(2,1)S(1)}, bf16[768,1024]{1,0:T(8,128)(2,1)}, u32[]{:S(2)}) copy-start(bf16[768,1024]{1,0:T(8,128)(2,1)} %get-tuple-element.8) | copy-start | bytes 4718596

commit v3 on v2

v3 whole, which is shorter than its diff:
```python
import jax
import jax.numpy as jnp
from jax import lax
from jax.experimental import pallas as pl
from jax.experimental.pallas import tpu as pltpu
from jax.sharding import PartitionSpec as P

MESH = pl.DeviceIdType.MESH
F32, BF16 = jnp.float32, jnp.bfloat16
D, KVW, BLOCK, TOK = 12288, 1024, 32, 384
ROWS = 192
FROWS = 768
SLAB = 48
OUTER_RATE = 0.7
MOMENTUM_COEF = 0.9
CLS = ((0, 256), (256, 384), (640, 384))
PARTS = (
    (0, 0, 128, ("x", "y", "z")),
    (0, 128, 128, ("y", "x", "z")),
    (1, 0, 128, ("z", "y", "x")),
    (2, 0, 128, ("z", "x", "y")),
    (1, 128, 256, ("y", "z", "x")),
    (2, 128, 256, ("x", "z", "y")),
)

SCHEDULE = (
    ("S", "r", 0), ("S", "d", 0), ("S", "r", 1), ("D", "r", 0), ("S", "d", 1), ("W", "r", 0), ("S", "f", 0),
    ("D", "r", 1), ("D", "d", 0), ("S", "r", 2), ("S", "d", 2), ("D", "f", 0), ("D", "d", 1), ("W", "r", 1),
    ("S", "f", 1), ("D", "r", 2), ("S", "r", 3), ("W", "d", 0), ("W", "f", 0), ("E", 0), ("S", "1", 0),
    ("S", "2", 0, 0), ("D", "f", 1), ("D", "d", 2), ("D", "r", 3), ("W", "r", 2), ("S", "f", 2), ("S", "d", 3),
    ("W", "d", 1), ("W", "f", 1), ("E", 1), ("D", "1", 0), ("S", "2", 1, 0), ("D", "2", 0, 0), ("S", "1", 1),
    ("D", "f", 2), ("W", "r", 3), ("S", "f", 3), ("D", "d", 3), ("S", "r", 4), ("W", "1", 0), ("S", "1h", 0),
    ("W", "2", 0, 0), ("S", "2h", 0, 0), ("S", "2", 0, 1), ("D", "f", 3), ("S", "d", 4), ("D", "1", 1),
    ("S", "2", 0, 2), ("W", "d", 2), ("W", "f", 2), ("E", 2), ("D", "2", 1, 0), ("D", "1h", 0), ("W", "2", 1, 0),
    ("S", "2h", 1, 0), ("W", "1", 1), ("S", "2", 1, 1), ("D", "2h", 0, 0), ("S", "1h", 1), ("D", "r", 4),
    ("S", "r", 5), ("S", "2", 1, 2), ("W", "1h", 0), ("S", "2", 0, 3), ("D", "2", 0, 1), ("S", "2", 2, 0),
    ("D", "2h", 1, 0), ("S", "3", 2, 0), ("W", "r", 4), ("S", "f", 4), ("W", "d", 3), ("W", "f", 3), ("E", 3),
    ("D", "d", 4), ("S", "d", 5), ("D", "2", 1, 1), ("S", "2", 3, 0), ("D", "2", 0, 2), ("D", "1h", 1),
    ("W", "2", 0, 1), ("S", "2h", 0, 1), ("W", "2", 0, 2), ("S", "2h", 0, 2), ("D", "2", 1, 2), ("W", "1h", 1),
    ("S", "2", 1, 3), ("D", "r", 5), ("S", "1", 2), ("W", "2", 1, 1), ("S", "2h", 1, 1), ("D", "2", 0, 3),
    ("D", "2", 2, 0), ("S", "3", 3, 0), ("D", "3", 2, 0), ("W", "2", 1, 2), ("S", "2h", 1, 2), ("D", "2h", 0, 1),
    ("D", "2h", 0, 2), ("W", "2", 0, 3), ("S", "2h", 0, 3), ("W", "2", 2, 0), ("S", "2h", 2, 0), ("D", "f", 4),
    ("W", "r", 5), ("S", "f", 5), ("S", "1", 3), ("W", "d", 4), ("W", "f", 4), ("E", 4), ("D", "3", 3, 0),
    ("D", "2h", 0, 3), ("D", "2h", 2, 0), ("S", "1", 4), ("D", "2h", 1, 1), ("D", "2", 3, 0), ("D", "2h", 1, 2),
    ("D", "2", 1, 3), ("W", "2", 3, 0), ("S", "2h", 3, 0), ("W", "2", 1, 3), ("S", "2h", 1, 3), ("D", "1", 2),
    ("D", "d", 5), ("W", "1", 2), ("S", "1h", 2), ("D", "f", 5), ("D", "1", 3), ("S", "2", 4, 0), ("S", "2", 2, 1),
    ("S", "2", 2, 2), ("D", "2h", 3, 0), ("D", "2h", 1, 3), ("S", "3", 4, 0), ("W", "d", 5), ("W", "f", 5), ("E", 5),
    ("D", "1h", 2), ("W", "1", 3), ("S", "1h", 3), ("S", "1", 5), ("D", "2", 4, 0), ("S", "2", 5, 0), ("D", "1", 4),
    ("W", "1h", 2), ("S", "2", 2, 3), ("D", "3", 4, 0), ("S", "2", 3, 1), ("D", "2", 2, 1), ("D", "2", 2, 2),
    ("W", "1", 4), ("S", "1h", 4), ("D", "1h", 3), ("W", "2", 4, 0), ("S", "2h", 4, 0), ("S", "2", 3, 2),
    ("S", "2", 4, 1), ("W", "2", 2, 1), ("S", "2h", 2, 1), ("W", "2", 2, 2), ("S", "2h", 2, 2), ("W", "1h", 3),
    ("S", "2", 3, 3), ("D", "2", 2, 3), ("S", "3", 5, 0), ("S", "2", 4, 2), ("W", "2", 2, 3), ("S", "2h", 2, 3),
    ("D", "2", 3, 1), ("S", "3", 2, 1), ("D", "2h", 2, 1), ("D", "1h", 4), ("D", "2h", 2, 2), ("D", "2h", 2, 3),
    ("S", "3", 3, 1), ("W", "2", 3, 1), ("S", "2h", 3, 1), ("D", "2h", 4, 0), ("D", "2", 5, 0), ("W", "1h", 4),
    ("S", "2", 4, 3), ("D", "2", 3, 2), ("D", "1", 5), ("S", "3", 4, 1), ("W", "2", 5, 0), ("S", "3", 5, 1),
    ("D", "2", 3, 3), ("W", "2", 3, 2), ("S", "2h", 3, 2), ("D", "2h", 3, 1), ("W", "1", 5), ("S", "1h", 5),
    ("S", "2h", 5, 0), ("D", "3", 5, 0), ("D", "3", 3, 1), ("S", "3", 3, 2), ("D", "3", 2, 1), ("W", "2", 3, 3),
    ("S", "2h", 3, 3), ("D", "2", 4, 1), ("S", "2", 5, 1), ("S", "3", 5, 2), ("D", "2h", 3, 2), ("S", "3", 2, 2),
    ("D", "2", 4, 2), ("W", "2", 4, 1), ("S", "2h", 4, 1), ("D", "2h", 3, 3), ("D", "1h", 5), ("S", "3", 4, 2),
    ("D", "3", 5, 1), ("D", "3", 3, 2), ("S", "3", 3, 3), ("D", "2h", 5, 0), ("W", "2", 4, 2), ("S", "2h", 4, 2),
    ("S", "3", 3, 4), ("D", "2", 4, 3), ("S", "2", 5, 2), ("D", "3", 4, 1), ("D", "3", 2, 2), ("S", "3", 2, 3),
    ("W", "2h", 4, 0), ("S", "3", 4, 3), ("D", "2h", 4, 1), ("W", "2", 4, 3), ("S", "2h", 4, 3), ("C", "sq", 0),
    ("D", "2h", 4, 2), ("W", "1h", 5), ("S", "2", 5, 3), ("D", "3", 4, 2), ("D", "3", 2, 3), ("S", "3", 2, 4),
    ("D", "3", 5, 2), ("D", "3", 3, 3), ("W", "2h", 5, 0), ("S", "3", 5, 3), ("C", "sq", 1), ("D", "2", 5, 1),
    ("W", "2", 5, 1), ("S", "2h", 5, 1), ("W", "3", 3, 0), ("W", "3", 3, 1), ("W", "3", 3, 2), ("W", "3", 3, 3),
    ("S", "3h", 3, 0), ("C", "sq", 2), ("D", "2h", 4, 3), ("S", "3", 0, 0), ("D", "3", 4, 3), ("W", "2h", 4, 1),
    ("S", "3", 4, 4), ("D", "3", 3, 4), ("S", "3", 3, 5), ("D", "2", 5, 2), ("S", "3", 1, 0), ("S", "3", 0, 1),
    ("W", "3", 2, 0), ("W", "3", 2, 1), ("W", "3", 2, 2), ("W", "3", 2, 3), ("W", "3", 4, 0), ("W", "3", 4, 1),
    ("W", "3", 4, 2), ("W", "3", 4, 3), ("C", "mm", 1, 0, "near"), ("D", "2h", 5, 1), ("D", "2", 5, 3),
    ("W", "2", 5, 2), ("S", "2h", 5, 2), ("D", "3", 0, 0), ("S", "3", 1, 1), ("D", "3", 5, 3), ("D", "3h", 3, 0),
    ("W", "2h", 5, 1), ("S", "3", 5, 4), ("W", "2", 5, 3), ("S", "2h", 5, 3), ("D", "3", 1, 0), ("D", "3", 0, 1),
    ("S", "3", 0, 2), ("W", "3", 5, 0), ("W", "3", 5, 1), ("W", "3", 5, 2), ("W", "3", 5, 3),
    ("C", "mm", 2, 0, "near"), ("S", "3", 1, 2), ("D", "2h", 5, 2), ("D", "3", 1, 1), ("S", "3", 0, 3),
    ("D", "3", 2, 4), ("S", "3h", 2, 0), ("D", "2h", 5, 3), ("D", "3", 0, 2), ("S", "3", 1, 3), ("S", "3", 0, 4),
    ("S", "3h", 4, 0), ("D", "3", 3, 5), ("S", "3h", 5, 0), ("W", "3", 2, 4), ("W", "3", 4, 4),
    ("C", "mm", 1, 1, "near"), ("D", "3", 1, 2), ("D", "3", 0, 3), ("D", "3", 1, 3), ("S", "3", 1, 4),
    ("D", "3", 4, 4), ("D", "3h", 2, 0), ("S", "3", 2, 5), ("D", "3", 5, 4), ("W", "2h", 5, 2), ("S", "3", 5, 5),
    ("D", "3", 0, 4), ("W", "3", 0, 0), ("W", "3", 0, 1), ("W", "3", 0, 2), ("W", "3", 0, 3), ("S", "3h", 0, 0),
    ("D", "3h", 4, 0), ("W", "2h", 4, 2), ("S", "3", 4, 5), ("W", "3", 3, 4), ("W", "3", 5, 4),
    ("C", "mm", 2, 1, "near"), ("W", "3", 1, 0), ("W", "3", 1, 1), ("W", "3", 1, 2), ("W", "3", 1, 3),
    ("S", "3h", 1, 0), ("W", "3h", 2, 0), ("W", "3h", 4, 0), ("C", "mm", 1, 0, "far"), ("W", "3h", 3, 0),
    ("W", "3h", 5, 0), ("C", "mm", 2, 0, "far"), ("D", "3h", 0, 0), ("D", "3", 1, 4), ("S", "3", 0, 5),
    ("D", "3h", 5, 0), ("S", "3h", 3, 1), ("W", "3h", 0, 0), ("W", "3h", 1, 0), ("C", "mm", 0, 0, "all"),
    ("D", "3h", 1, 0), ("S", "3", 1, 5), ("D", "3", 2, 5), ("S", "3h", 2, 1), ("S", "3h", 5, 1), ("S", "3h", 4, 1),
    ("W", "3", 3, 5), ("W", "3", 5, 5), ("C", "mm", 2, 2, "near"), ("D", "3", 0, 5), ("W", "3", 0, 4),
    ("S", "3h", 0, 1), ("D", "3", 5, 5), ("D", "3h", 3, 1), ("W", "2h", 3, 0), ("W", "2h", 3, 1), ("W", "2h", 3, 2),
    ("W", "2h", 3, 3), ("S", "3", 3, 6), ("W", "3", 1, 4), ("S", "3h", 1, 1), ("D", "3", 4, 5), ("D", "3h", 2, 1),
    ("W", "2h", 2, 0), ("W", "2h", 2, 1), ("W", "2h", 2, 2), ("W", "2h", 2, 3), ("S", "3", 2, 6), ("W", "3", 2, 5),
    ("W", "3", 4, 5), ("C", "mm", 1, 2, "near"), ("D", "3", 1, 5), ("W", "2h", 0, 0), ("W", "2h", 0, 1),
    ("W", "2h", 0, 2), ("W", "2h", 0, 3), ("S", "3", 0, 6), ("D", "3h", 5, 1), ("W", "2h", 5, 3), ("S", "3", 5, 6),
    ("W", "3h", 3, 1), ("W", "3h", 5, 1), ("C", "mm", 2, 1, "far"), ("D", "3h", 4, 1), ("W", "2h", 4, 3),
    ("S", "3", 4, 6), ("W", "3h", 2, 1), ("W", "3h", 4, 1), ("C", "mm", 1, 1, "far"), ("D", "3h", 0, 1),
    ("D", "3h", 1, 1), ("W", "2h", 1, 0), ("W", "2h", 1, 1), ("W", "2h", 1, 2), ("W", "2h", 1, 3), ("S", "3", 1, 6),
    ("W", "3h", 0, 1), ("W", "3h", 1, 1), ("C", "mm", 0, 1, "all"), ("D", "3", 0, 6), ("W", "3", 0, 5),
    ("S", "3h", 0, 2), ("D", "3", 3, 6), ("S", "3h", 3, 2), ("W", "3", 1, 5), ("S", "3h", 1, 2), ("D", "3", 2, 6),
    ("S", "3h", 2, 2), ("S", "3h", 5, 2), ("D", "3", 1, 6), ("W", "3", 0, 6), ("S", "3h", 0, 3), ("S", "3h", 4, 2),
    ("D", "3h", 0, 2), ("W", "3", 1, 6), ("S", "3h", 1, 3), ("W", "3", 3, 6), ("W", "3", 5, 6),
    ("C", "mm", 2, 3, "near"), ("D", "3", 5, 6), ("D", "3h", 3, 2), ("S", "3h", 3, 3), ("D", "3", 4, 6),
    ("D", "3h", 2, 2), ("W", "3", 2, 6), ("S", "3h", 2, 3), ("S", "3h", 5, 3), ("W", "3", 4, 6),
    ("C", "mm", 1, 3, "near"), ("S", "3h", 4, 3), ("W", "3h", 0, 2), ("W", "3h", 1, 2), ("C", "mm", 0, 2, "all"),
    ("W", "3h", 0, 3), ("W", "3h", 1, 3), ("C", "mm", 0, 3, "all"), ("W", "3h", 2, 2), ("W", "3h", 4, 2),
    ("C", "mm", 1, 2, "far"), ("W", "3h", 2, 3), ("W", "3h", 4, 3), ("C", "mm", 1, 3, "far"), ("W", "3h", 3, 2),
    ("W", "3h", 5, 2), ("C", "mm", 2, 2, "far"), ("W", "3h", 3, 3), ("W", "3h", 5, 3), ("C", "mm", 2, 3, "far"),
)

THRESH = ((0.25, 0.5), (0.75, 1.0), (1.25, 1.5), (1.75, 2.0), (2.5, 3.0), (3.5, 4.0), (5.0, 6.0))


def mod4(v):
    return lax.rem(v + 8, 4)


def kernel(
    tokens, gain, frag, exps, base, mom,
    nb_out, nm_out, kv_out,
    w0, w1, w2, tok, acc, kv, fb, rl, bs, ms, gb, gf, gn, ex, eb, er, erl, sc, iv, ss,
    loc, a_snd, a_rcv, e_snd, e_rcv, t_snd, t_rcv, g_snd, g_rcv, o_sem,
):
    W = (w0, w1, w2)
    rep = lax.axis_index("replica")
    fs = lax.axis_index("fsdp")
    core = lax.axis_index("tensor")
    pos = {"x": lax.rem(fs, 4), "y": lax.div(fs, 4), "z": rep}

    def nbr(axis, step):
        c = dict(pos)
        c[axis] = mod4(pos[axis] + step)
        return (c["z"], c["y"] * 4 + c["x"], core)

    other = (rep, fs, 1 - core)

    def remote(src, dst, ss_, rs_, dev):
        return pltpu.make_async_remote_copy(
            src_ref=src, dst_ref=dst, send_sem=ss_, recv_sem=rs_, device_id=dev, device_id_type=MESH
        )

    pending = []

    def go(copy):
        copy.start()
        pending.append(copy)

    l_ex = pltpu.make_async_copy(exps, ex, loc.at[0])
    l_ex.start()
    l_fr = pltpu.make_async_copy(frag.at[rep], fb.at[0], loc.at[1])
    l_fr.start()
    l_bs = pltpu.make_async_copy(base, bs, loc.at[2])
    l_bs.start()
    l_ms = pltpu.make_async_copy(mom, ms, loc.at[3])
    l_ms.start()
    l_gn = pltpu.make_async_copy(gain, gb, loc.at[4])
    l_gn.start()

    barrier = pltpu.get_barrier_semaphore()
    peers = [nbr(a, s) for a in "xyz" for s in (1, -1)] + [other]
    for p in peers:
        pl.semaphore_signal(barrier, inc=1, device_id=p, device_id_type=MESH)

    l_ex.wait()
    eb[...] = ex[...].astype(F32).astype(BF16)

    def window(d):
        return eb.at[:, pl.ds(pl.multiple_of(128 * lax.div(3 * d, 2), 128), 256)]

    off = 64 * lax.rem(rep, 2)

    def expand(slot):
        e = (window(rep)[...] if slot == 0 else er[slot]).astype(F32)
        j = lax.broadcasted_iota(jnp.int32, (BLOCK, KVW), 0)
        n = lax.broadcasted_iota(jnp.int32, (BLOCK, KVW), 1)
        pick = jnp.where(j == lax.div(n, BLOCK), 1.0, 0.0).astype(BF16)
        for ref, sign in ((sc, 1.0), (iv, -1.0)):
            small = jnp.exp2(sign * e).astype(BF16)
            full = lax.dot_general(small, pick, (((0,), (0,)), ((), ())), preferred_element_type=F32)
            ref[slot] = full.astype(BF16)

    expand(0)
    l_gn.wait()
    gf[...] = gb[...].astype(F32)
    first = 6 * fs + lax.div(3 * rep, 2)
    i = lax.broadcasted_iota(jnp.int32, (128, 128), 0)
    l = lax.broadcasted_iota(jnp.int32, (128, 128), 1)
    for h in range(2):
        row = jnp.broadcast_to(gf[pl.ds(first + h, 1), :], (128, 128))
        column = jnp.sum(jnp.where(i == l, row, 0.0), axis=1, keepdims=True)
        gn[pl.ds(128 * h, 128), :] = jnp.broadcast_to(column, (128, 128))
    acc[...] = jnp.zeros_like(acc)

    pl.semaphore_wait(barrier, len(peers))

    up, down = nbr("z", 1), nbr("z", -1)
    zu, zd, zo = mod4(rep + 1), mod4(rep - 1), mod4(rep + 2)

    e_cp = [
        remote(window(zo), erl, e_snd.at[0], e_rcv.at[0], up),
        remote(window(zu), er.at[1], e_snd.at[1], e_rcv.at[1], up),
        remote(window(zd), er.at[2], e_snd.at[2], e_rcv.at[2], down),
        remote(erl, er.at[3], e_snd.at[3], e_rcv.at[3], up),
    ]

    def cols(p):
        c, lo, width, _ = PARTS[p]
        return pl.ds(CLS[c][0] + lo, width)

    H = ROWS // 2

    def a2a(p):
        k = 6 * p
        cc = cols(p)
        return [
            remote(frag.at[zo, pl.ds(0, H), cc], rl.at[0, :, cc], a_snd.at[k], a_rcv.at[k], up),
            remote(frag.at[zo, pl.ds(H, H), cc], rl.at[1, :, cc], a_snd.at[k + 1], a_rcv.at[k + 1], down),
            remote(frag.at[zu, :, cc], fb.at[1, :, cc], a_snd.at[k + 2], a_rcv.at[k + 2], up),
            remote(frag.at[zd, :, cc], fb.at[2, :, cc], a_snd.at[k + 3], a_rcv.at[k + 3], down),
            remote(rl.at[0, :, cc], fb.at[3, pl.ds(0, H), cc], a_snd.at[k + 4], a_rcv.at[k + 4], up),
            remote(rl.at[1, :, cc], fb.at[3, pl.ds(H, H), cc], a_snd.at[k + 5], a_rcv.at[k + 5], down),
        ]

    for m in e_cp[:3]:
        go(m)
    mine = pl.ds(pl.multiple_of(core * TOK, TOK), TOK)
    t_cp = remote(tokens, tok.at[mine, :], t_snd.at[0], t_rcv.at[0], other)
    l_tk = pltpu.make_async_copy(tokens, tok.at[mine, :], loc.at[5])

    def prepare():
        for s in (1, 2, 3):
            e_cp[s].wait_recv()
            expand(s)
        l_fr.wait()
        l_bs.wait()
        l_ms.wait()

    def encode(p):
        c, sub, width, _ = PARTS[p]
        lo = CLS[c][0] + sub
        row0 = pl.multiple_of(rep * ROWS, ROWS)

        def step(t, carry):
            rr = pl.ds(pl.multiple_of(t * SLAB, SLAB), SLAB)
            wr = pl.ds(pl.multiple_of(row0 + t * SLAB, SLAB), SLAB)
            fr = pl.ds(pl.multiple_of(off + t * SLAB, 16), SLAB)
            g = gn[fr, :]
            for k in range(width // 128):
                cc = pl.ds(lo + 128 * k, 128)
                b = bs[rr, cc]
                total = jnp.zeros((SLAB, 128), F32)
                for s in range(4):
                    v = (b - fb[s, rr, cc].astype(F32)) * iv[s, fr, cc].astype(F32)
                    m = jnp.abs(v)
                    level = jnp.zeros_like(m)
                    for mid, val in THRESH:
                        level = jnp.where(m >= mid, val, level)
                    total = total + jnp.where(v < 0.0, -level, level) * sc[s, fr, cc].astype(F32)
                grad = total * 0.25
                nm = MOMENTUM_COEF * ms[rr, cc] + grad
                nb = b - OUTER_RATE * (grad + MOMENTUM_COEF * nm)
                ms[rr, cc] = nm
                bs[rr, cc] = nb
                W[c][pos["y"], pos["x"], wr, pl.ds(sub + 128 * k, 128)] = (nb * g).astype(BF16)
            return carry

        lax.fori_loop(0, ROWS // SLAB, step, 0)

    def place(p, **at):
        half = at.pop("half", None)
        xs, ys = at.get("x", slice(None)), at.get("y", slice(None))
        if "z" in at:
            r0, n = at["z"] * ROWS, ROWS
        else:
            r0, n = 0, FROWS
        if half is not None:
            n = n // 2
            r0 = r0 + half * n
        if not isinstance(r0, int):
            r0 = pl.multiple_of(r0, 96)
        c, lo, width, _ = PARTS[p]
        return W[c].at[ys, xs, pl.ds(r0, n), pl.ds(lo, width)]

    M = {}
    OFF = (0, 1, -1, 2)
    used = [0]

    def both(*pair):
        out = []
        for j, s in enumerate((1, -1)):
            axis, ref = pair[j]
            out.append(remote(ref, ref, g_snd.at[used[0]], g_rcv.at[used[0]], nbr(axis, s)))
            used[0] += 1
        return out

    def full(p, axis, **fixed):
        here = place(p, **fixed, **{axis: pos[axis]})
        return both((axis, here), (axis, here))

    def half(p, axis, **fixed):
        return both(
            *[(axis, place(p, **fixed, **{axis: mod4(pos[axis] - s), "half": j})) for j, s in enumerate((1, -1))]
        )

    for p in range(len(PARTS)):
        m = a2a(p)
        M["r", p], M["d", p], M["f", p] = m[:2], m[2:4], m[4:]
        a, b, l = PARTS[p][3]
        R, S = (a, b) if b == "z" else (b, a)
        at = {b: pos[b], l: pos[l]}
        M["1", p], M["1h", p] = full(p, a, **at), half(p, a, **at)
        for i in range(4):
            at = {a: mod4(pos[a] + OFF[i]), l: pos[l]}
            M["2", p, i], M["2h", p, i] = full(p, b, **at), half(p, b, **at)
            M["3", p, i] = full(p, l, **{R: pos[R], S: mod4(pos[S] + OFF[i])})
            M["3h", p, i] = half(p, l, **{R: mod4(pos[R] + OFF[i])})
            if i:
                M["3", p, 3 + i] = full(p, l, **{R: mod4(pos[R] + OFF[i])})

    def mm(c, count, coords):
        lo, width = CLS[c]
        cc = pl.ds(lo, width)

        def chunk(t, carry):
            yy, xx = coords(t)
            kk = pl.ds(pl.multiple_of((yy * 4 + xx) * FROWS, FROWS), FROWS)

            def block(m, carry):
                mr = pl.ds(pl.multiple_of(m * 256, 256), 256)
                acc[mr, cc] += jnp.dot(tok[mr, kk], W[c][yy, xx], preferred_element_type=F32)
                return carry

            return lax.fori_loop(0, 3, block, carry)

        lax.fori_loop(0, count, chunk, 0)

    def offset(i):
        return i + lax.div(i, 2) - 2 * lax.div(i, 3)

    def mm_near(c, i):
        if c == 1:
            yy = mod4(pos["y"] + OFF[i])
            mm(c, 3, lambda t: (yy, mod4(pos["x"] + offset(t))))
        else:
            xx = mod4(pos["x"] + OFF[i])
            mm(c, 3, lambda t: (mod4(pos["y"] + offset(t)), xx))

    def mm_far(c, i):
        if c == 1:
            mm(c, 1, lambda t: (mod4(pos["y"] + OFF[i]), mod4(pos["x"] + 2)))
        else:
            mm(c, 1, lambda t: (mod4(pos["y"] + 2), mod4(pos["x"] + OFF[i])))

    def mm_level(c, i):
        def coords(t):
            turn = lax.div(t, i + 1)
            iy = i * (1 - turn) + (t - i - 1) * turn
            ix = t * (1 - turn) + i * turn
            return mod4(pos["y"] + offset(iy)), mod4(pos["x"] + offset(ix))

        mm(c, 2 * i + 1, coords)

    def squares(i):
        rr = pl.ds(pl.multiple_of(core * TOK + i * 128, 128), 128)

        def step(t, s):
            for k in range(4):
                v = tok[rr, pl.ds(pl.multiple_of(t * 512 + k * 128, 128), 128)].astype(F32)
                s = s + v * v
            return s

        s = lax.fori_loop(0, D // 512, step, jnp.zeros((128, 128), F32))
        mean = jnp.sum(s, axis=1, keepdims=True) * (1.0 / D)
        ss[rr, :] = jnp.broadcast_to(lax.rsqrt(mean + 1e-05) * (D ** -0.5), (128, 128))

    s_cp = remote(ss.at[mine, :], ss.at[mine, :], t_snd.at[1], t_rcv.at[1], other)
    outs = []
    left = []
    seen = set()

    def once(name):
        new = name not in seen
        seen.add(name)
        return new

    for kind, *key in SCHEDULE:
        key = tuple(key)
        if kind == "S":
            for m in M[key]:
                m.start()
            left.append(key)
        elif kind == "W":
            if once("wait"):
                go(t_cp)
                l_tk.start()
                e_cp[0].wait_recv()
                go(e_cp[3])
            if key == ("d", 0):
                prepare()
            for m in M[key]:
                m.wait_recv()
        elif kind == "D":
            for m in M[key]:
                m.wait_send()
            left.remove(key)
        elif kind == "E":
            encode(*key)
            left_to_encode = len(PARTS) - 1 - key[0]
            if left_to_encode == 0:
                outs.append(pltpu.make_async_copy(bs, nb_out, o_sem.at[0]))
                outs.append(pltpu.make_async_copy(ms, nm_out, o_sem.at[1]))
                for o in outs:
                    o.start()
        elif key[0] == "sq":
            if once("own tokens"):
                l_tk.wait()
            squares(key[1])
            if key[1] == 2:
                go(s_cp)
        else:
            if once("all tokens"):
                t_cp.wait_recv()
            {"near": mm_near, "far": mm_far, "all": mm_level}[key[3]](key[1], key[2])
    s_cp.wait_recv()

    for m in range(3):
        mr = pl.ds(m * 256, 256)

        def scale(k, carry):
            cc = pl.ds(pl.multiple_of(k * 128, 128), 128)
            kv[mr, cc] = (acc[mr, cc] * ss[mr, :]).astype(BF16)
            return carry

        lax.fori_loop(0, KVW // 128, scale, 0)
        o = pltpu.make_async_copy(kv.at[mr, :], kv_out.at[mr, :], o_sem.at[2 + m])
        o.start()
        outs.append(o)
    for key in left:
        for m in M[key]:
            m.wait_send()
    for p in pending:
        p.wait_send()
    for o in outs:
        o.wait()


def body(tokens, norm_gain, fragment, exponents, base_weight, momentum):
    any_ = pl.BlockSpec(memory_space=pl.ANY)
    dma = pltpu.SemaphoreType.DMA
    vm = pltpu.VMEM
    return pl.pallas_call(
        kernel,
        out_shape=(
            jax.ShapeDtypeStruct((ROWS, KVW), F32),
            jax.ShapeDtypeStruct((ROWS, KVW), F32),
            jax.ShapeDtypeStruct((2 * TOK, KVW), BF16),
        ),
        in_specs=[any_] * 6,
        out_specs=[any_] * 3,
        scratch_shapes=[
            *[vm((4, 4, FROWS, width), BF16) for _, width in CLS],
            vm((2 * TOK, D), BF16),
            vm((2 * TOK, KVW), F32),
            vm((2 * TOK, KVW), BF16),
            vm((4, ROWS, KVW), BF16),
            vm((2, ROWS // 2, KVW), BF16),
            vm((ROWS, KVW), F32),
            vm((ROWS, KVW), F32),
            vm((D // 128, 128), BF16),
            vm((D // 128, 128), F32),
            vm((256, 128), F32),
            vm((BLOCK, 4 * ROWS), jnp.int32),
            vm((BLOCK, 4 * ROWS), BF16),
            vm((4, BLOCK, 256), BF16),
            vm((BLOCK, 256), BF16),
            vm((4, 256, KVW), BF16),
            vm((4, 256, KVW), BF16),
            vm((2 * TOK, 128), F32),
            dma((6,)),
            dma((6 * len(PARTS),)),
            dma((6 * len(PARTS),)),
            dma((4,)),
            dma((4,)),
            dma((2,)),
            dma((2,)),
            dma((42 * len(PARTS),)),
            dma((42 * len(PARTS),)),
            dma((5,)),
        ],
        compiler_params=pltpu.CompilerParams(
            collective_id=0, has_side_effects=True, vmem_limit_bytes=62 * 1024 * 1024
        ),
        cost_estimate=pl.CostEstimate(flops=2 * 768 * 12288 * 1024, bytes_accessed=30_000_000, transcendentals=0),
    )(
        tokens,
        norm_gain.reshape(D // 128, 128),
        fragment.reshape(4, ROWS, KVW),
        exponents[0].T,
        base_weight,
        momentum,
    )


def solution(mesh):
    in_specs = (
        P(("replica", "fsdp", "tensor"), None),
        P(),
        P("replica", "fsdp", "tensor"),
        P("replica", "fsdp", "tensor"),
        P(("fsdp", "replica"), "tensor"),
        P(("fsdp", "replica"), "tensor"),
    )
    out_specs = (
        P(("fsdp", "replica"), "tensor"),
        P(("fsdp", "replica"), "tensor"),
        P(("replica", "fsdp"), "tensor"),
    )
    return jax.shard_map(body, mesh=mesh, in_specs=in_specs, out_specs=out_specs, check_vma=False)
```

time: 139 us -> 137 us (0.986)
  Pallas kernels: 134 us -> 132 us
    pallas_call x1, Pallas kernels: 134 us -> 132 us  [body(): pl.pallas_call(kernel, out_shape=(jax.ShapeDtypeStruct((ROWS, KVW), F32),...]
where the time goes in v3:
time: 137 us
  Pallas kernels  132 us (96%)
  local copies, waits for them, and re-layouts  4.27 us (3%)
    pallas_call x1, Pallas kernels, body(): pl.pallas_call(kernel, out_shape=(jax.ShapeDtypeStruct((ROWS, KVW), F32),...  132 us
    unnamed x7, local copies, waits for them, and re-layouts  4.27 us

profile of v3, /device:TPU:0, one launch (start us, length us, event | category | flops | bytes accessed | tf_op | source)
XLA Modules:
  0.0 137.1 jit_solution(7651188655568046220)
XLA Ops:
  0.6 132.2 %shard_map.85 = (f32[192,1024]{1,0:T(8,128)}, f32[192,1024]{1,0:T(8,128)}, bf16[768,1024]{1,0:T(8,128)(2,1)}) custom-call(bf16[384,12288]{1,0:T(8,128)(2,1)} %tokens.1, bf16[96,128]{1,0:T(8,128)(2,1)} %bitcast.7, bf16[4,192,1024]{2,1,0:T(8,128)(2,1)} %bitcast.5, s32[32,768]{1,0:T(8,128)} %bitcast.6, f32[192,1024]{1,0:T(8,128)} %base.1, f32[192,1024]{1,0:T(8,128)} %mom.1), custom_call_target="tpu_custom_call" | custom-call | flops 19327352832 | bytes 30000000 | tf_op jit(solution)/shard_map/pallas_call | solution.py:446
  132.8 0.0 copy-start.1
  132.8 0.0 copy-start
  132.9 2.2 %copy.12 = f32[192,1024]{1,0:T(8,128)} copy(f32[192,1024]{1,0:T(8,128)} %get-tuple-element.6) | data formatting | bytes 1572864
  135.1 0.0 copy-done.1
  135.1 0.9 copy.13
  136.0 0.0 copy-done
  136.0 1.1 copy.14
Async XLA Ops:
  132.8 2.3 %copy-start.1 = (f32[192,1024]{1,0:T(8,128)S(1)}, f32[192,1024]{1,0:T(8,128)}, u32[]{:S(2)}) copy-start(f32[192,1024]{1,0:T(8,128)} %get-tuple-element.7) | copy-start | bytes 2359300
  132.8 3.1 %copy-start = (bf16[768,1024]{1,0:T(8,128)(2,1)S(1)}, bf16[768,1024]{1,0:T(8,128)(2,1)}, u32[]{:S(2)}) copy-start(bf16[768,1024]{1,0:T(8,128)(2,1)} %get-tuple-element.8) | copy-start | bytes 4718596

commit v4 on v3

--- a/solution.py
+++ b/solution.py
@@ -25,80 +25,79 @@
 
 SCHEDULE = (
     ("S", "r", 0), ("S", "d", 0), ("S", "r", 1), ("D", "r", 0), ("S", "d", 1), ("W", "r", 0), ("S", "f", 0),
-    ("D", "r", 1), ("D", "d", 0), ("S", "r", 2), ("S", "d", 2), ("D", "f", 0), ("D", "d", 1), ("W", "r", 1),
+    ("D", "d", 0), ("D", "r", 1), ("S", "r", 2), ("S", "d", 2), ("D", "d", 1), ("D", "f", 0), ("W", "r", 1),
     ("S", "f", 1), ("D", "r", 2), ("S", "r", 3), ("W", "d", 0), ("W", "f", 0), ("E", 0), ("S", "1", 0),
     ("S", "2", 0, 0), ("D", "f", 1), ("D", "d", 2), ("D", "r", 3), ("W", "r", 2), ("S", "f", 2), ("S", "d", 3),
     ("W", "d", 1), ("W", "f", 1), ("E", 1), ("D", "1", 0), ("S", "2", 1, 0), ("D", "2", 0, 0), ("S", "1", 1),
-    ("D", "f", 2), ("W", "r", 3), ("S", "f", 3), ("D", "d", 3), ("S", "r", 4), ("W", "1", 0), ("S", "1h", 0),
-    ("W", "2", 0, 0), ("S", "2h", 0, 0), ("S", "2", 0, 1), ("D", "f", 3), ("S", "d", 4), ("D", "1", 1),
-    ("S", "2", 0, 2), ("W", "d", 2), ("W", "f", 2), ("E", 2), ("D", "2", 1, 0), ("D", "1h", 0), ("W", "2", 1, 0),
-    ("S", "2h", 1, 0), ("W", "1", 1), ("S", "2", 1, 1), ("D", "2h", 0, 0), ("S", "1h", 1), ("D", "r", 4),
-    ("S", "r", 5), ("S", "2", 1, 2), ("W", "1h", 0), ("S", "2", 0, 3), ("D", "2", 0, 1), ("S", "2", 2, 0),
-    ("D", "2h", 1, 0), ("S", "3", 2, 0), ("W", "r", 4), ("S", "f", 4), ("W", "d", 3), ("W", "f", 3), ("E", 3),
-    ("D", "d", 4), ("S", "d", 5), ("D", "2", 1, 1), ("S", "2", 3, 0), ("D", "2", 0, 2), ("D", "1h", 1),
-    ("W", "2", 0, 1), ("S", "2h", 0, 1), ("W", "2", 0, 2), ("S", "2h", 0, 2), ("D", "2", 1, 2), ("W", "1h", 1),
-    ("S", "2", 1, 3), ("D", "r", 5), ("S", "1", 2), ("W", "2", 1, 1), ("S", "2h", 1, 1), ("D", "2", 0, 3),
-    ("D", "2", 2, 0), ("S", "3", 3, 0), ("D", "3", 2, 0), ("W", "2", 1, 2), ("S", "2h", 1, 2), ("D", "2h", 0, 1),
-    ("D", "2h", 0, 2), ("W", "2", 0, 3), ("S", "2h", 0, 3), ("W", "2", 2, 0), ("S", "2h", 2, 0), ("D", "f", 4),
-    ("W", "r", 5), ("S", "f", 5), ("S", "1", 3), ("W", "d", 4), ("W", "f", 4), ("E", 4), ("D", "3", 3, 0),
-    ("D", "2h", 0, 3), ("D", "2h", 2, 0), ("S", "1", 4), ("D", "2h", 1, 1), ("D", "2", 3, 0), ("D", "2h", 1, 2),
-    ("D", "2", 1, 3), ("W", "2", 3, 0), ("S", "2h", 3, 0), ("W", "2", 1, 3), ("S", "2h", 1, 3), ("D", "1", 2),
-    ("D", "d", 5), ("W", "1", 2), ("S", "1h", 2), ("D", "f", 5), ("D", "1", 3), ("S", "2", 4, 0), ("S", "2", 2, 1),
-    ("S", "2", 2, 2), ("D", "2h", 3, 0), ("D", "2h", 1, 3), ("S", "3", 4, 0), ("W", "d", 5), ("W", "f", 5), ("E", 5),
-    ("D", "1h", 2), ("W", "1", 3), ("S", "1h", 3), ("S", "1", 5), ("D", "2", 4, 0), ("S", "2", 5, 0), ("D", "1", 4),
-    ("W", "1h", 2), ("S", "2", 2, 3), ("D", "3", 4, 0), ("S", "2", 3, 1), ("D", "2", 2, 1), ("D", "2", 2, 2),
-    ("W", "1", 4), ("S", "1h", 4), ("D", "1h", 3), ("W", "2", 4, 0), ("S", "2h", 4, 0), ("S", "2", 3, 2),
-    ("S", "2", 4, 1), ("W", "2", 2, 1), ("S", "2h", 2, 1), ("W", "2", 2, 2), ("S", "2h", 2, 2), ("W", "1h", 3),
-    ("S", "2", 3, 3), ("D", "2", 2, 3), ("S", "3", 5, 0), ("S", "2", 4, 2), ("W", "2", 2, 3), ("S", "2h", 2, 3),
-    ("D", "2", 3, 1), ("S", "3", 2, 1), ("D", "2h", 2, 1), ("D", "1h", 4), ("D", "2h", 2, 2), ("D", "2h", 2, 3),
-    ("S", "3", 3, 1), ("W", "2", 3, 1), ("S", "2h", 3, 1), ("D", "2h", 4, 0), ("D", "2", 5, 0), ("W", "1h", 4),
-    ("S", "2", 4, 3), ("D", "2", 3, 2), ("D", "1", 5), ("S", "3", 4, 1), ("W", "2", 5, 0), ("S", "3", 5, 1),
-    ("D", "2", 3, 3), ("W", "2", 3, 2), ("S", "2h", 3, 2), ("D", "2h", 3, 1), ("W", "1", 5), ("S", "1h", 5),
-    ("S", "2h", 5, 0), ("D", "3", 5, 0), ("D", "3", 3, 1), ("S", "3", 3, 2), ("D", "3", 2, 1), ("W", "2", 3, 3),
-    ("S", "2h", 3, 3), ("D", "2", 4, 1), ("S", "2", 5, 1), ("S", "3", 5, 2), ("D", "2h", 3, 2), ("S", "3", 2, 2),
-    ("D", "2", 4, 2), ("W", "2", 4, 1), ("S", "2h", 4, 1), ("D", "2h", 3, 3), ("D", "1h", 5), ("S", "3", 4, 2),
-    ("D", "3", 5, 1), ("D", "3", 3, 2), ("S", "3", 3, 3), ("D", "2h", 5, 0), ("W", "2", 4, 2), ("S", "2h", 4, 2),
-    ("S", "3", 3, 4), ("D", "2", 4, 3), ("S", "2", 5, 2), ("D", "3", 4, 1), ("D", "3", 2, 2), ("S", "3", 2, 3),
-    ("W", "2h", 4, 0), ("S", "3", 4, 3), ("D", "2h", 4, 1), ("W", "2", 4, 3), ("S", "2h", 4, 3), ("C", "sq", 0),
-    ("D", "2h", 4, 2), ("W", "1h", 5), ("S", "2", 5, 3), ("D", "3", 4, 2), ("D", "3", 2, 3), ("S", "3", 2, 4),
-    ("D", "3", 5, 2), ("D", "3", 3, 3), ("W", "2h", 5, 0), ("S", "3", 5, 3), ("C", "sq", 1), ("D", "2", 5, 1),
-    ("W", "2", 5, 1), ("S", "2h", 5, 1), ("W", "3", 3, 0), ("W", "3", 3, 1), ("W", "3", 3, 2), ("W", "3", 3, 3),
-    ("S", "3h", 3, 0), ("C", "sq", 2), ("D", "2h", 4, 3), ("S", "3", 0, 0), ("D", "3", 4, 3), ("W", "2h", 4, 1),
-    ("S", "3", 4, 4), ("D", "3", 3, 4), ("S", "3", 3, 5), ("D", "2", 5, 2), ("S", "3", 1, 0), ("S", "3", 0, 1),
-    ("W", "3", 2, 0), ("W", "3", 2, 1), ("W", "3", 2, 2), ("W", "3", 2, 3), ("W", "3", 4, 0), ("W", "3", 4, 1),
-    ("W", "3", 4, 2), ("W", "3", 4, 3), ("C", "mm", 1, 0, "near"), ("D", "2h", 5, 1), ("D", "2", 5, 3),
-    ("W", "2", 5, 2), ("S", "2h", 5, 2), ("D", "3", 0, 0), ("S", "3", 1, 1), ("D", "3", 5, 3), ("D", "3h", 3, 0),
-    ("W", "2h", 5, 1), ("S", "3", 5, 4), ("W", "2", 5, 3), ("S", "2h", 5, 3), ("D", "3", 1, 0), ("D", "3", 0, 1),
-    ("S", "3", 0, 2), ("W", "3", 5, 0), ("W", "3", 5, 1), ("W", "3", 5, 2), ("W", "3", 5, 3),
-    ("C", "mm", 2, 0, "near"), ("S", "3", 1, 2), ("D", "2h", 5, 2), ("D", "3", 1, 1), ("S", "3", 0, 3),
-    ("D", "3", 2, 4), ("S", "3h", 2, 0), ("D", "2h", 5, 3), ("D", "3", 0, 2), ("S", "3", 1, 3), ("S", "3", 0, 4),
-    ("S", "3h", 4, 0), ("D", "3", 3, 5), ("S", "3h", 5, 0), ("W", "3", 2, 4), ("W", "3", 4, 4),
-    ("C", "mm", 1, 1, "near"), ("D", "3", 1, 2), ("D", "3", 0, 3), ("D", "3", 1, 3), ("S", "3", 1, 4),
-    ("D", "3", 4, 4), ("D", "3h", 2, 0), ("S", "3", 2, 5), ("D", "3", 5, 4), ("W", "2h", 5, 2), ("S", "3", 5, 5),
-    ("D", "3", 0, 4), ("W", "3", 0, 0), ("W", "3", 0, 1), ("W", "3", 0, 2), ("W", "3", 0, 3), ("S", "3h", 0, 0),
-    ("D", "3h", 4, 0), ("W", "2h", 4, 2), ("S", "3", 4, 5), ("W", "3", 3, 4), ("W", "3", 5, 4),
-    ("C", "mm", 2, 1, "near"), ("W", "3", 1, 0), ("W", "3", 1, 1), ("W", "3", 1, 2), ("W", "3", 1, 3),
-    ("S", "3h", 1, 0), ("W", "3h", 2, 0), ("W", "3h", 4, 0), ("C", "mm", 1, 0, "far"), ("W", "3h", 3, 0),
-    ("W", "3h", 5, 0), ("C", "mm", 2, 0, "far"), ("D", "3h", 0, 0), ("D", "3", 1, 4), ("S", "3", 0, 5),
-    ("D", "3h", 5, 0), ("S", "3h", 3, 1), ("W", "3h", 0, 0), ("W", "3h", 1, 0), ("C", "mm", 0, 0, "all"),
-    ("D", "3h", 1, 0), ("S", "3", 1, 5), ("D", "3", 2, 5), ("S", "3h", 2, 1), ("S", "3h", 5, 1), ("S", "3h", 4, 1),
-    ("W", "3", 3, 5), ("W", "3", 5, 5), ("C", "mm", 2, 2, "near"), ("D", "3", 0, 5), ("W", "3", 0, 4),
-    ("S", "3h", 0, 1), ("D", "3", 5, 5), ("D", "3h", 3, 1), ("W", "2h", 3, 0), ("W", "2h", 3, 1), ("W", "2h", 3, 2),
-    ("W", "2h", 3, 3), ("S", "3", 3, 6), ("W", "3", 1, 4), ("S", "3h", 1, 1), ("D", "3", 4, 5), ("D", "3h", 2, 1),
-    ("W", "2h", 2, 0), ("W", "2h", 2, 1), ("W", "2h", 2, 2), ("W", "2h", 2, 3), ("S", "3", 2, 6), ("W", "3", 2, 5),
-    ("W", "3", 4, 5), ("C", "mm", 1, 2, "near"), ("D", "3", 1, 5), ("W", "2h", 0, 0), ("W", "2h", 0, 1),
-    ("W", "2h", 0, 2), ("W", "2h", 0, 3), ("S", "3", 0, 6), ("D", "3h", 5, 1), ("W", "2h", 5, 3), ("S", "3", 5, 6),
-    ("W", "3h", 3, 1), ("W", "3h", 5, 1), ("C", "mm", 2, 1, "far"), ("D", "3h", 4, 1), ("W", "2h", 4, 3),
-    ("S", "3", 4, 6), ("W", "3h", 2, 1), ("W", "3h", 4, 1), ("C", "mm", 1, 1, "far"), ("D", "3h", 0, 1),
-    ("D", "3h", 1, 1), ("W", "2h", 1, 0), ("W", "2h", 1, 1), ("W", "2h", 1, 2), ("W", "2h", 1, 3), ("S", "3", 1, 6),
-    ("W", "3h", 0, 1), ("W", "3h", 1, 1), ("C", "mm", 0, 1, "all"), ("D", "3", 0, 6), ("W", "3", 0, 5),
-    ("S", "3h", 0, 2), ("D", "3", 3, 6), ("S", "3h", 3, 2), ("W", "3", 1, 5), ("S", "3h", 1, 2), ("D", "3", 2, 6),
-    ("S", "3h", 2, 2), ("S", "3h", 5, 2), ("D", "3", 1, 6), ("W", "3", 0, 6), ("S", "3h", 0, 3), ("S", "3h", 4, 2),
-    ("D", "3h", 0, 2), ("W", "3", 1, 6), ("S", "3h", 1, 3), ("W", "3", 3, 6), ("W", "3", 5, 6),
-    ("C", "mm", 2, 3, "near"), ("D", "3", 5, 6), ("D", "3h", 3, 2), ("S", "3h", 3, 3), ("D", "3", 4, 6),
-    ("D", "3h", 2, 2), ("W", "3", 2, 6), ("S", "3h", 2, 3), ("S", "3h", 5, 3), ("W", "3", 4, 6),
-    ("C", "mm", 1, 3, "near"), ("S", "3h", 4, 3), ("W", "3h", 0, 2), ("W", "3h", 1, 2), ("C", "mm", 0, 2, "all"),
-    ("W", "3h", 0, 3), ("W", "3h", 1, 3), ("C", "mm", 0, 3, "all"), ("W", "3h", 2, 2), ("W", "3h", 4, 2),
+    ("D", "f", 2), ("W", "r", 3), ("S", "f", 3), ("S", "r", 4), ("W", "1", 0), ("S", "1h", 0), ("W", "2", 0, 0),
+    ("S", "2h", 0, 0), ("S", "2", 0, 1), ("D", "d", 3), ("D", "f", 3), ("S", "d", 4), ("D", "1", 1), ("S", "2", 0, 2),
+    ("W", "d", 2), ("W", "f", 2), ("E", 2), ("D", "2", 1, 0), ("D", "1h", 0), ("W", "2", 1, 0), ("S", "2h", 1, 0),
+    ("W", "1", 1), ("S", "2", 1, 1), ("D", "2h", 0, 0), ("S", "1h", 1), ("S", "2", 1, 2), ("D", "r", 4),
+    ("S", "r", 5), ("W", "1h", 0), ("S", "2", 0, 3), ("S", "2", 2, 0), ("W", "d", 3), ("W", "f", 3), ("E", 3),
+    ("W", "r", 4), ("S", "f", 4), ("D", "2h", 1, 0), ("S", "2", 3, 0), ("D", "2", 1, 1), ("S", "3", 2, 0),
+    ("D", "2", 0, 1), ("D", "2", 0, 2), ("D", "1h", 1), ("W", "2", 0, 1), ("S", "2h", 0, 1), ("D", "d", 4),
+    ("D", "r", 5), ("S", "d", 5), ("S", "3", 3, 0), ("W", "2", 0, 2), ("S", "2h", 0, 2), ("D", "2", 1, 2),
+    ("W", "2", 1, 1), ("S", "2h", 1, 1), ("W", "1h", 1), ("S", "2", 1, 3), ("W", "2", 1, 2), ("S", "2h", 1, 2),
+    ("D", "f", 4), ("W", "r", 5), ("S", "f", 5), ("S", "1", 2), ("W", "d", 4), ("W", "f", 4), ("E", 4),
+    ("D", "2", 0, 3), ("D", "2", 2, 0), ("D", "2h", 0, 1), ("D", "2h", 0, 2), ("D", "3", 3, 0), ("S", "1", 4),
+    ("D", "2", 3, 0), ("D", "3", 2, 0), ("D", "2h", 1, 1), ("D", "2h", 1, 2), ("W", "2", 3, 0), ("S", "2h", 3, 0),
+    ("D", "d", 5), ("S", "1", 3), ("W", "2", 0, 3), ("S", "2h", 0, 3), ("S", "2", 4, 0), ("W", "2", 2, 0),
+    ("S", "2h", 2, 0), ("D", "2", 1, 3), ("D", "2h", 3, 0), ("S", "3", 4, 0), ("W", "2", 1, 3), ("S", "2h", 1, 3),
+    ("W", "d", 5), ("W", "f", 5), ("E", 5), ("D", "2h", 0, 3), ("D", "2h", 2, 0), ("D", "1", 4), ("W", "1", 2),
+    ("S", "2", 2, 1), ("D", "2h", 1, 3), ("S", "1", 5), ("D", "f", 5), ("D", "1", 2), ("D", "1", 3), ("S", "1h", 2),
+    ("S", "2", 2, 2), ("W", "1", 3), ("S", "1h", 3), ("D", "2", 4, 0), ("W", "1", 4), ("S", "2", 4, 1),
+    ("S", "1h", 4), ("D", "3", 4, 0), ("S", "2", 3, 1), ("S", "2", 3, 2), ("D", "1h", 2), ("S", "2", 4, 2),
+    ("D", "2", 2, 1), ("S", "3", 5, 0), ("D", "2", 2, 2), ("W", "2", 2, 1), ("S", "2h", 2, 1), ("W", "1h", 3),
+    ("S", "2", 3, 3), ("W", "1h", 2), ("S", "2", 2, 3), ("D", "1h", 3), ("W", "2", 4, 0), ("S", "2h", 4, 0),
+    ("S", "3", 2, 1), ("D", "1h", 4), ("W", "2", 2, 2), ("S", "2h", 2, 2), ("S", "2", 5, 0), ("D", "1", 5),
+    ("D", "2", 3, 1), ("D", "2", 3, 2), ("S", "3", 4, 1), ("D", "2h", 2, 1), ("S", "3", 3, 1), ("W", "1", 5),
+    ("S", "1h", 5), ("D", "2", 4, 1), ("W", "1h", 4), ("S", "2", 4, 3), ("D", "2h", 2, 2), ("D", "2", 2, 3),
+    ("S", "3", 3, 2), ("D", "2", 3, 3), ("D", "3", 2, 1), ("W", "2", 3, 1), ("S", "2h", 3, 1), ("D", "3", 5, 0),
+    ("S", "3", 3, 3), ("W", "2", 2, 3), ("S", "2h", 2, 3), ("W", "2", 3, 2), ("S", "2h", 3, 2), ("W", "2", 3, 3),
+    ("S", "2h", 3, 3), ("D", "2h", 4, 0), ("D", "2", 4, 2), ("W", "2", 4, 1), ("S", "2h", 4, 1), ("D", "3", 3, 1),
+    ("S", "3", 3, 4), ("W", "2", 4, 2), ("S", "2h", 4, 2), ("D", "2h", 3, 1), ("S", "3", 2, 2), ("S", "2", 5, 1),
+    ("D", "1h", 5), ("D", "2h", 3, 2), ("S", "3", 4, 2), ("D", "2", 5, 0), ("W", "2", 5, 0), ("S", "2h", 5, 0),
+    ("D", "2h", 3, 3), ("D", "3", 4, 1), ("D", "3", 2, 2), ("S", "3", 2, 3), ("D", "2h", 2, 3), ("D", "3", 3, 2),
+    ("D", "3", 3, 3), ("S", "3", 5, 1), ("C", "sq", 0), ("D", "2h", 4, 1), ("D", "2", 4, 3), ("D", "2h", 4, 2),
+    ("W", "2", 4, 3), ("S", "2h", 4, 3), ("W", "2h", 4, 0), ("S", "3", 4, 3), ("S", "2", 5, 2), ("C", "sq", 1),
+    ("D", "3", 3, 4), ("S", "3", 5, 2), ("D", "3", 2, 3), ("D", "3", 4, 2), ("S", "3", 2, 4), ("C", "sq", 2),
+    ("D", "2h", 5, 0), ("D", "2", 5, 1), ("W", "1h", 5), ("S", "2", 5, 3), ("D", "3", 5, 1), ("W", "2h", 5, 0),
+    ("S", "3", 5, 3), ("D", "2h", 4, 3), ("W", "2", 5, 1), ("S", "2h", 5, 1), ("W", "3", 3, 0), ("W", "3", 3, 1),
+    ("W", "3", 3, 2), ("W", "3", 3, 3), ("S", "3h", 3, 0), ("D", "3", 4, 3), ("W", "2h", 4, 1), ("S", "3", 4, 4),
+    ("S", "3", 0, 0), ("D", "3", 5, 2), ("S", "3", 3, 5), ("S", "3", 1, 0), ("W", "3", 2, 0), ("W", "3", 2, 1),
+    ("W", "3", 2, 2), ("W", "3", 2, 3), ("W", "3", 4, 0), ("W", "3", 4, 1), ("W", "3", 4, 2), ("W", "3", 4, 3),
+    ("C", "mm", 1, 0, "near"), ("D", "2", 5, 2), ("D", "2h", 5, 1), ("D", "2", 5, 3), ("W", "2", 5, 2),
+    ("S", "2h", 5, 2), ("D", "3", 0, 0), ("D", "3", 1, 0), ("S", "3", 0, 1), ("S", "3", 1, 1), ("D", "3", 5, 3),
+    ("W", "2h", 5, 1), ("S", "3", 5, 4), ("S", "3", 0, 2), ("W", "2", 5, 3), ("S", "2h", 5, 3), ("W", "3", 5, 0),
+    ("W", "3", 5, 1), ("W", "3", 5, 2), ("W", "3", 5, 3), ("C", "mm", 2, 0, "near"), ("D", "2h", 5, 2),
+    ("S", "3", 1, 2), ("D", "3", 2, 4), ("S", "3h", 2, 0), ("D", "3", 0, 1), ("D", "3", 1, 1), ("S", "3", 0, 3),
+    ("D", "3", 0, 2), ("D", "2h", 5, 3), ("S", "3", 1, 3), ("S", "3h", 4, 0), ("S", "3", 0, 4), ("W", "3", 2, 4),
+    ("W", "3", 4, 4), ("C", "mm", 1, 1, "near"), ("D", "3h", 3, 0), ("D", "3", 3, 5), ("S", "3h", 5, 0),
+    ("D", "3", 4, 4), ("D", "3h", 2, 0), ("S", "3", 2, 5), ("D", "3", 1, 2), ("D", "3", 0, 3), ("D", "3", 1, 3),
+    ("S", "3", 1, 4), ("D", "3", 5, 4), ("W", "2h", 5, 2), ("S", "3", 5, 5), ("D", "3h", 4, 0), ("W", "2h", 4, 2),
+    ("S", "3", 4, 5), ("W", "3", 0, 0), ("W", "3", 0, 1), ("W", "3", 0, 2), ("W", "3", 0, 3), ("S", "3h", 0, 0),
+    ("W", "3", 3, 4), ("W", "3", 5, 4), ("C", "mm", 2, 1, "near"), ("W", "3h", 2, 0), ("W", "3h", 4, 0),
+    ("C", "mm", 1, 0, "far"), ("D", "3", 0, 4), ("W", "3", 1, 0), ("W", "3", 1, 1), ("W", "3", 1, 2),
+    ("W", "3", 1, 3), ("S", "3h", 1, 0), ("W", "3h", 3, 0), ("W", "3h", 5, 0), ("C", "mm", 2, 0, "far"),
+    ("D", "3h", 0, 0), ("D", "3", 1, 4), ("S", "3", 0, 5), ("D", "3h", 5, 0), ("S", "3h", 3, 1), ("W", "3h", 0, 0),
+    ("W", "3h", 1, 0), ("C", "mm", 0, 0, "all"), ("D", "3", 2, 5), ("S", "3h", 2, 1), ("D", "3h", 1, 0),
+    ("S", "3", 1, 5), ("S", "3h", 5, 1), ("D", "3", 4, 5), ("S", "3h", 4, 1), ("W", "3", 0, 4), ("S", "3h", 0, 1),
+    ("W", "3", 2, 5), ("W", "3", 4, 5), ("C", "mm", 1, 2, "near"), ("D", "3", 5, 5), ("D", "3h", 3, 1),
+    ("W", "2h", 3, 0), ("W", "2h", 3, 1), ("W", "2h", 3, 2), ("W", "2h", 3, 3), ("S", "3", 3, 6), ("D", "3h", 2, 1),
+    ("W", "2h", 2, 0), ("W", "2h", 2, 1), ("W", "2h", 2, 2), ("W", "2h", 2, 3), ("S", "3", 2, 6), ("D", "3", 0, 5),
+    ("W", "3", 1, 4), ("S", "3h", 1, 1), ("W", "2h", 0, 0), ("W", "2h", 0, 1), ("W", "2h", 0, 2), ("W", "2h", 0, 3),
+    ("S", "3", 0, 6), ("D", "3h", 5, 1), ("W", "2h", 5, 3), ("S", "3", 5, 6), ("W", "3", 3, 5), ("W", "3", 5, 5),
+    ("C", "mm", 2, 2, "near"), ("D", "3h", 4, 1), ("W", "2h", 4, 3), ("S", "3", 4, 6), ("W", "3h", 2, 1),
+    ("W", "3h", 4, 1), ("C", "mm", 1, 1, "far"), ("W", "3h", 3, 1), ("W", "3h", 5, 1), ("C", "mm", 2, 1, "far"),
+    ("D", "3h", 0, 1), ("D", "3", 1, 5), ("D", "3h", 1, 1), ("W", "2h", 1, 0), ("W", "2h", 1, 1), ("W", "2h", 1, 2),
+    ("W", "2h", 1, 3), ("S", "3", 1, 6), ("W", "3h", 0, 1), ("W", "3h", 1, 1), ("C", "mm", 0, 1, "all"),
+    ("D", "3", 0, 6), ("W", "3", 0, 5), ("S", "3h", 0, 2), ("D", "3", 3, 6), ("S", "3h", 3, 2), ("D", "3", 2, 6),
+    ("S", "3h", 2, 2), ("W", "3", 1, 5), ("S", "3h", 1, 2), ("S", "3h", 5, 2), ("S", "3h", 4, 2), ("D", "3", 1, 6),
+    ("W", "3", 0, 6), ("S", "3h", 0, 3), ("D", "3h", 0, 2), ("W", "3", 1, 6), ("S", "3h", 1, 3), ("W", "3", 3, 6),
+    ("W", "3", 5, 6), ("C", "mm", 2, 3, "near"), ("D", "3", 5, 6), ("D", "3h", 3, 2), ("S", "3h", 3, 3),
+    ("D", "3", 4, 6), ("D", "3h", 2, 2), ("W", "3", 2, 6), ("S", "3h", 2, 3), ("S", "3h", 5, 3), ("W", "3", 4, 6),
+    ("S", "3h", 4, 3), ("W", "3h", 0, 2), ("W", "3h", 1, 2), ("C", "mm", 0, 2, "all"), ("W", "3h", 0, 3),
+    ("W", "3h", 1, 3), ("C", "mm", 0, 3, "all"), ("C", "mm", 1, 3, "near"), ("W", "3h", 2, 2), ("W", "3h", 4, 2),
     ("C", "mm", 1, 2, "far"), ("W", "3h", 2, 3), ("W", "3h", 4, 3), ("C", "mm", 1, 3, "far"), ("W", "3h", 3, 2),
     ("W", "3h", 5, 2), ("C", "mm", 2, 2, "far"), ("W", "3h", 3, 3), ("W", "3h", 5, 3), ("C", "mm", 2, 3, "far"),
 )
@@ -112,8 +111,8 @@
 
 def kernel(
     tokens, gain, frag, exps, base, mom,
-    nb_out, nm_out, kv_out,
-    w0, w1, w2, tok, acc, kv, fb, rl, bs, ms, gb, gf, gn, ex, eb, er, erl, sc, iv, ss,
+    grad_out, kv_out,
+    w0, w1, w2, tok, acc, kv, fb, rl, bs, ms, gr, gb, gf, gn, ex, eb, er, erl, sc, iv, ss,
     loc, a_snd, a_rcv, e_snd, e_rcv, t_snd, t_rcv, g_snd, g_rcv, o_sem,
 ):
     W = (w0, w1, w2)
@@ -254,8 +253,7 @@
                 grad = total * 0.25
                 nm = MOMENTUM_COEF * ms[rr, cc] + grad
                 nb = b - OUTER_RATE * (grad + MOMENTUM_COEF * nm)
-                ms[rr, cc] = nm
-                bs[rr, cc] = nb
+                gr[rr, cc] = grad
                 W[c][pos["y"], pos["x"], wr, pl.ds(sub + 128 * k, 128)] = (nb * g).astype(BF16)
             return carry
 
@@ -402,10 +400,8 @@
             encode(*key)
             left_to_encode = len(PARTS) - 1 - key[0]
             if left_to_encode == 0:
-                outs.append(pltpu.make_async_copy(bs, nb_out, o_sem.at[0]))
-                outs.append(pltpu.make_async_copy(ms, nm_out, o_sem.at[1]))
-                for o in outs:
-                    o.start()
+                outs.append(pltpu.make_async_copy(gr, grad_out, o_sem.at[0]))
+                outs[0].start()
         elif key[0] == "sq":
             if once("own tokens"):
                 l_tk.wait()
@@ -427,7 +423,7 @@
             return carry
 
         lax.fori_loop(0, KVW // 128, scale, 0)
-        o = pltpu.make_async_copy(kv.at[mr, :], kv_out.at[mr, :], o_sem.at[2 + m])
+        o = pltpu.make_async_copy(kv.at[mr, :], kv_out.at[mr, :], o_sem.at[1 + m])
         o.start()
         outs.append(o)
     for key in left:
@@ -443,15 +439,14 @@
     any_ = pl.BlockSpec(memory_space=pl.ANY)
     dma = pltpu.SemaphoreType.DMA
     vm = pltpu.VMEM
-    return pl.pallas_call(
+    grad, keys_values = pl.pallas_call(
         kernel,
         out_shape=(
-            jax.ShapeDtypeStruct((ROWS, KVW), F32),
             jax.ShapeDtypeStruct((ROWS, KVW), F32),
             jax.ShapeDtypeStruct((2 * TOK, KVW), BF16),
         ),
         in_specs=[any_] * 6,
-        out_specs=[any_] * 3,
+        out_specs=[any_] * 2,
         scratch_shapes=[
             *[vm((4, 4, FROWS, width), BF16) for _, width in CLS],
             vm((2 * TOK, D), BF16),
@@ -459,6 +454,7 @@
             vm((2 * TOK, KVW), BF16),
             vm((4, ROWS, KVW), BF16),
             vm((2, ROWS // 2, KVW), BF16),
+            vm((ROWS, KVW), F32),
             vm((ROWS, KVW), F32),
             vm((ROWS, KVW), F32),
             vm((D // 128, 128), BF16),
@@ -480,7 +476,7 @@
             dma((2,)),
             dma((42 * len(PARTS),)),
             dma((42 * len(PARTS),)),
-            dma((5,)),
+            dma((4,)),
         ],
         compiler_params=pltpu.CompilerParams(
             collective_id=0, has_side_effects=True, vmem_limit_bytes=62 * 1024 * 1024
@@ -494,6 +490,9 @@
         base_weight,
         momentum,
     )
+    new_momentum = MOMENTUM_COEF * momentum + grad
+    new_base = base_weight - OUTER_RATE * (grad + MOMENTUM_COEF * new_momentum)
+    return new_base, new_momentum, keys_values
 
 
 def solution(mesh):

time: 137 us -> 137 us (level)
  local copies, waits for them, and re-layouts: 4.27 us -> 1.16 us
  other arithmetic: 0 us -> 2.76 us
    unnamed x7, local copies, waits for them, and re-layouts: 4.27 us -> 1.16 us
    sub x0 -> x1, other arithmetic: none -> 2.76 us  [body(): new_base = base_weight - OUTER_RATE * (grad + MOMENTUM_COEF * new_momentum)]
where the time goes in v4:
time: 137 us
  Pallas kernels  133 us (97%)
  other arithmetic  2.76 us (2%)
    pallas_call x1, Pallas kernels, body(): pl.pallas_call(kernel, out_shape=(jax.ShapeDtypeStruct((ROWS, KVW), F32),...  133 us
    sub x1, other arithmetic, body(): new_base = base_weight - OUTER_RATE * (grad + MOMENTUM_COEF * new_momentum)  2.76 us

profile of v4, /device:TPU:0, one launch (start us, length us, event | category | flops | bytes accessed | tf_op | source)
XLA Modules:
  0.0 137.3 jit_solution(16842286720564751391)
XLA Ops:
  0.6 0.0 copy-start.1
  0.6 0.0 copy-start.2
  0.7 132.7 %shard_map.85 = (f32[192,1024]{1,0:T(8,128)}, bf16[768,1024]{1,0:T(8,128)(2,1)}) custom-call(bf16[384,12288]{1,0:T(8,128)(2,1)} %tokens.1, bf16[96,128]{1,0:T(8,128)(2,1)} %bitcast.7, bf16[4,192,1024]{2,1,0:T(8,128)(2,1)} %bitcast.5, s32[32,768]{1,0:T(8,128)} %bitcast.6, f32[192,1024]{1,0:T(8,128)} %base.1, f32[192,1024]{1,0:T(8,128)} %mom.1), custom_call_target="tpu_custom_call" | custom-call | flops 19327352832 | bytes 30000000 | tf_op jit(solution)/shard_map/pallas_call | solution.py:442
  133.4 0.0 copy-done.1
  133.4 0.0 copy-done.2
  133.4 0.0 copy-start
  133.4 2.8 %multiply_subtract_fusion = (f32[192,1024]{1,0:T(8,128)}, f32[192,1024]{1,0:T(8,128)}) fusion(f32[192,1024]{1,0:T(8,128)S(1)} %copy-done.1, f32[192,1024]{1,0:T(8,128)} %get-tuple-element.5, f32[192,1024]{1,0:T(8,128)S(1)} %copy-done.2), kind=kLoop, calls=%fused_computation | loop fusion | flops 1179648 | bytes 3932160 | tf_op jit(solution)/shard_map/sub | solution.py:494
  136.2 0.0 copy-done
  136.2 1.1 copy.10
Async XLA Ops:
  0.6 132.8 %copy-start.1 = (f32[192,1024]{1,0:T(8,128)S(1)}, f32[192,1024]{1,0:T(8,128)}, u32[]{:S(2)}) copy-start(f32[192,1024]{1,0:T(8,128)} %base.1) | copy-start | bytes 2359300
  0.6 132.8 %copy-start.2 = (f32[192,1024]{1,0:T(8,128)S(1)}, f32[192,1024]{1,0:T(8,128)}, u32[]{:S(2)}) copy-start(f32[192,1024]{1,0:T(8,128)} %mom.1) | copy-start | bytes 2359300
  133.4 2.8 %copy-start = (bf16[768,1024]{1,0:T(8,128)(2,1)S(1)}, bf16[768,1024]{1,0:T(8,128)(2,1)}, u32[]{:S(2)}) copy-start(bf16[768,1024]{1,0:T(8,128)(2,1)} %get-tuple-element.14) | copy-start | bytes 4718596

commit v5 on v4

--- a/solution.py
+++ b/solution.py
@@ -24,80 +24,81 @@
 )
 
 SCHEDULE = (
-    ("S", "r", 0), ("S", "d", 0), ("S", "r", 1), ("D", "r", 0), ("S", "d", 1), ("W", "r", 0), ("S", "f", 0),
-    ("D", "d", 0), ("D", "r", 1), ("S", "r", 2), ("S", "d", 2), ("D", "d", 1), ("D", "f", 0), ("W", "r", 1),
-    ("S", "f", 1), ("D", "r", 2), ("S", "r", 3), ("W", "d", 0), ("W", "f", 0), ("E", 0), ("S", "1", 0),
-    ("S", "2", 0, 0), ("D", "f", 1), ("D", "d", 2), ("D", "r", 3), ("W", "r", 2), ("S", "f", 2), ("S", "d", 3),
-    ("W", "d", 1), ("W", "f", 1), ("E", 1), ("D", "1", 0), ("S", "2", 1, 0), ("D", "2", 0, 0), ("S", "1", 1),
-    ("D", "f", 2), ("W", "r", 3), ("S", "f", 3), ("S", "r", 4), ("W", "1", 0), ("S", "1h", 0), ("W", "2", 0, 0),
-    ("S", "2h", 0, 0), ("S", "2", 0, 1), ("D", "d", 3), ("D", "f", 3), ("S", "d", 4), ("D", "1", 1), ("S", "2", 0, 2),
-    ("W", "d", 2), ("W", "f", 2), ("E", 2), ("D", "2", 1, 0), ("D", "1h", 0), ("W", "2", 1, 0), ("S", "2h", 1, 0),
-    ("W", "1", 1), ("S", "2", 1, 1), ("D", "2h", 0, 0), ("S", "1h", 1), ("S", "2", 1, 2), ("D", "r", 4),
-    ("S", "r", 5), ("W", "1h", 0), ("S", "2", 0, 3), ("S", "2", 2, 0), ("W", "d", 3), ("W", "f", 3), ("E", 3),
-    ("W", "r", 4), ("S", "f", 4), ("D", "2h", 1, 0), ("S", "2", 3, 0), ("D", "2", 1, 1), ("S", "3", 2, 0),
-    ("D", "2", 0, 1), ("D", "2", 0, 2), ("D", "1h", 1), ("W", "2", 0, 1), ("S", "2h", 0, 1), ("D", "d", 4),
-    ("D", "r", 5), ("S", "d", 5), ("S", "3", 3, 0), ("W", "2", 0, 2), ("S", "2h", 0, 2), ("D", "2", 1, 2),
-    ("W", "2", 1, 1), ("S", "2h", 1, 1), ("W", "1h", 1), ("S", "2", 1, 3), ("W", "2", 1, 2), ("S", "2h", 1, 2),
-    ("D", "f", 4), ("W", "r", 5), ("S", "f", 5), ("S", "1", 2), ("W", "d", 4), ("W", "f", 4), ("E", 4),
-    ("D", "2", 0, 3), ("D", "2", 2, 0), ("D", "2h", 0, 1), ("D", "2h", 0, 2), ("D", "3", 3, 0), ("S", "1", 4),
-    ("D", "2", 3, 0), ("D", "3", 2, 0), ("D", "2h", 1, 1), ("D", "2h", 1, 2), ("W", "2", 3, 0), ("S", "2h", 3, 0),
-    ("D", "d", 5), ("S", "1", 3), ("W", "2", 0, 3), ("S", "2h", 0, 3), ("S", "2", 4, 0), ("W", "2", 2, 0),
-    ("S", "2h", 2, 0), ("D", "2", 1, 3), ("D", "2h", 3, 0), ("S", "3", 4, 0), ("W", "2", 1, 3), ("S", "2h", 1, 3),
-    ("W", "d", 5), ("W", "f", 5), ("E", 5), ("D", "2h", 0, 3), ("D", "2h", 2, 0), ("D", "1", 4), ("W", "1", 2),
-    ("S", "2", 2, 1), ("D", "2h", 1, 3), ("S", "1", 5), ("D", "f", 5), ("D", "1", 2), ("D", "1", 3), ("S", "1h", 2),
-    ("S", "2", 2, 2), ("W", "1", 3), ("S", "1h", 3), ("D", "2", 4, 0), ("W", "1", 4), ("S", "2", 4, 1),
-    ("S", "1h", 4), ("D", "3", 4, 0), ("S", "2", 3, 1), ("S", "2", 3, 2), ("D", "1h", 2), ("S", "2", 4, 2),
-    ("D", "2", 2, 1), ("S", "3", 5, 0), ("D", "2", 2, 2), ("W", "2", 2, 1), ("S", "2h", 2, 1), ("W", "1h", 3),
-    ("S", "2", 3, 3), ("W", "1h", 2), ("S", "2", 2, 3), ("D", "1h", 3), ("W", "2", 4, 0), ("S", "2h", 4, 0),
-    ("S", "3", 2, 1), ("D", "1h", 4), ("W", "2", 2, 2), ("S", "2h", 2, 2), ("S", "2", 5, 0), ("D", "1", 5),
-    ("D", "2", 3, 1), ("D", "2", 3, 2), ("S", "3", 4, 1), ("D", "2h", 2, 1), ("S", "3", 3, 1), ("W", "1", 5),
-    ("S", "1h", 5), ("D", "2", 4, 1), ("W", "1h", 4), ("S", "2", 4, 3), ("D", "2h", 2, 2), ("D", "2", 2, 3),
-    ("S", "3", 3, 2), ("D", "2", 3, 3), ("D", "3", 2, 1), ("W", "2", 3, 1), ("S", "2h", 3, 1), ("D", "3", 5, 0),
-    ("S", "3", 3, 3), ("W", "2", 2, 3), ("S", "2h", 2, 3), ("W", "2", 3, 2), ("S", "2h", 3, 2), ("W", "2", 3, 3),
-    ("S", "2h", 3, 3), ("D", "2h", 4, 0), ("D", "2", 4, 2), ("W", "2", 4, 1), ("S", "2h", 4, 1), ("D", "3", 3, 1),
-    ("S", "3", 3, 4), ("W", "2", 4, 2), ("S", "2h", 4, 2), ("D", "2h", 3, 1), ("S", "3", 2, 2), ("S", "2", 5, 1),
-    ("D", "1h", 5), ("D", "2h", 3, 2), ("S", "3", 4, 2), ("D", "2", 5, 0), ("W", "2", 5, 0), ("S", "2h", 5, 0),
-    ("D", "2h", 3, 3), ("D", "3", 4, 1), ("D", "3", 2, 2), ("S", "3", 2, 3), ("D", "2h", 2, 3), ("D", "3", 3, 2),
-    ("D", "3", 3, 3), ("S", "3", 5, 1), ("C", "sq", 0), ("D", "2h", 4, 1), ("D", "2", 4, 3), ("D", "2h", 4, 2),
-    ("W", "2", 4, 3), ("S", "2h", 4, 3), ("W", "2h", 4, 0), ("S", "3", 4, 3), ("S", "2", 5, 2), ("C", "sq", 1),
-    ("D", "3", 3, 4), ("S", "3", 5, 2), ("D", "3", 2, 3), ("D", "3", 4, 2), ("S", "3", 2, 4), ("C", "sq", 2),
-    ("D", "2h", 5, 0), ("D", "2", 5, 1), ("W", "1h", 5), ("S", "2", 5, 3), ("D", "3", 5, 1), ("W", "2h", 5, 0),
-    ("S", "3", 5, 3), ("D", "2h", 4, 3), ("W", "2", 5, 1), ("S", "2h", 5, 1), ("W", "3", 3, 0), ("W", "3", 3, 1),
-    ("W", "3", 3, 2), ("W", "3", 3, 3), ("S", "3h", 3, 0), ("D", "3", 4, 3), ("W", "2h", 4, 1), ("S", "3", 4, 4),
-    ("S", "3", 0, 0), ("D", "3", 5, 2), ("S", "3", 3, 5), ("S", "3", 1, 0), ("W", "3", 2, 0), ("W", "3", 2, 1),
-    ("W", "3", 2, 2), ("W", "3", 2, 3), ("W", "3", 4, 0), ("W", "3", 4, 1), ("W", "3", 4, 2), ("W", "3", 4, 3),
-    ("C", "mm", 1, 0, "near"), ("D", "2", 5, 2), ("D", "2h", 5, 1), ("D", "2", 5, 3), ("W", "2", 5, 2),
-    ("S", "2h", 5, 2), ("D", "3", 0, 0), ("D", "3", 1, 0), ("S", "3", 0, 1), ("S", "3", 1, 1), ("D", "3", 5, 3),
-    ("W", "2h", 5, 1), ("S", "3", 5, 4), ("S", "3", 0, 2), ("W", "2", 5, 3), ("S", "2h", 5, 3), ("W", "3", 5, 0),
-    ("W", "3", 5, 1), ("W", "3", 5, 2), ("W", "3", 5, 3), ("C", "mm", 2, 0, "near"), ("D", "2h", 5, 2),
-    ("S", "3", 1, 2), ("D", "3", 2, 4), ("S", "3h", 2, 0), ("D", "3", 0, 1), ("D", "3", 1, 1), ("S", "3", 0, 3),
-    ("D", "3", 0, 2), ("D", "2h", 5, 3), ("S", "3", 1, 3), ("S", "3h", 4, 0), ("S", "3", 0, 4), ("W", "3", 2, 4),
-    ("W", "3", 4, 4), ("C", "mm", 1, 1, "near"), ("D", "3h", 3, 0), ("D", "3", 3, 5), ("S", "3h", 5, 0),
-    ("D", "3", 4, 4), ("D", "3h", 2, 0), ("S", "3", 2, 5), ("D", "3", 1, 2), ("D", "3", 0, 3), ("D", "3", 1, 3),
-    ("S", "3", 1, 4), ("D", "3", 5, 4), ("W", "2h", 5, 2), ("S", "3", 5, 5), ("D", "3h", 4, 0), ("W", "2h", 4, 2),
-    ("S", "3", 4, 5), ("W", "3", 0, 0), ("W", "3", 0, 1), ("W", "3", 0, 2), ("W", "3", 0, 3), ("S", "3h", 0, 0),
-    ("W", "3", 3, 4), ("W", "3", 5, 4), ("C", "mm", 2, 1, "near"), ("W", "3h", 2, 0), ("W", "3h", 4, 0),
-    ("C", "mm", 1, 0, "far"), ("D", "3", 0, 4), ("W", "3", 1, 0), ("W", "3", 1, 1), ("W", "3", 1, 2),
-    ("W", "3", 1, 3), ("S", "3h", 1, 0), ("W", "3h", 3, 0), ("W", "3h", 5, 0), ("C", "mm", 2, 0, "far"),
-    ("D", "3h", 0, 0), ("D", "3", 1, 4), ("S", "3", 0, 5), ("D", "3h", 5, 0), ("S", "3h", 3, 1), ("W", "3h", 0, 0),
-    ("W", "3h", 1, 0), ("C", "mm", 0, 0, "all"), ("D", "3", 2, 5), ("S", "3h", 2, 1), ("D", "3h", 1, 0),
-    ("S", "3", 1, 5), ("S", "3h", 5, 1), ("D", "3", 4, 5), ("S", "3h", 4, 1), ("W", "3", 0, 4), ("S", "3h", 0, 1),
-    ("W", "3", 2, 5), ("W", "3", 4, 5), ("C", "mm", 1, 2, "near"), ("D", "3", 5, 5), ("D", "3h", 3, 1),
-    ("W", "2h", 3, 0), ("W", "2h", 3, 1), ("W", "2h", 3, 2), ("W", "2h", 3, 3), ("S", "3", 3, 6), ("D", "3h", 2, 1),
-    ("W", "2h", 2, 0), ("W", "2h", 2, 1), ("W", "2h", 2, 2), ("W", "2h", 2, 3), ("S", "3", 2, 6), ("D", "3", 0, 5),
-    ("W", "3", 1, 4), ("S", "3h", 1, 1), ("W", "2h", 0, 0), ("W", "2h", 0, 1), ("W", "2h", 0, 2), ("W", "2h", 0, 3),
-    ("S", "3", 0, 6), ("D", "3h", 5, 1), ("W", "2h", 5, 3), ("S", "3", 5, 6), ("W", "3", 3, 5), ("W", "3", 5, 5),
-    ("C", "mm", 2, 2, "near"), ("D", "3h", 4, 1), ("W", "2h", 4, 3), ("S", "3", 4, 6), ("W", "3h", 2, 1),
-    ("W", "3h", 4, 1), ("C", "mm", 1, 1, "far"), ("W", "3h", 3, 1), ("W", "3h", 5, 1), ("C", "mm", 2, 1, "far"),
-    ("D", "3h", 0, 1), ("D", "3", 1, 5), ("D", "3h", 1, 1), ("W", "2h", 1, 0), ("W", "2h", 1, 1), ("W", "2h", 1, 2),
+    ("S", "r", 0), ("S", "d", 0), ("S", "r", 1), ("S", "d", 1), ("W", "r", 0), ("S", "f", 0), ("S", "r", 2),
+    ("W", "r", 1), ("S", "f", 1), ("S", "d", 2), ("S", "r", 3), ("W", "d", 0), ("W", "f", 0), ("E", 0), ("S", "1", 0),
+    ("S", "2", 0, 0), ("D", "r", 0), ("W", "r", 2), ("S", "f", 2), ("S", "d", 3), ("W", "d", 1), ("W", "f", 1),
+    ("E", 1), ("S", "2", 1, 0), ("S", "1", 1), ("D", "r", 1), ("D", "d", 0), ("W", "r", 3), ("S", "f", 3),
+    ("S", "r", 4), ("W", "1", 0), ("S", "1h", 0), ("W", "2", 0, 0), ("S", "2h", 0, 0), ("S", "2", 0, 1),
+    ("S", "2", 0, 2), ("D", "d", 1), ("D", "f", 0), ("S", "d", 4), ("W", "d", 2), ("W", "f", 2), ("E", 2),
+    ("W", "2", 1, 0), ("S", "2h", 1, 0), ("W", "1", 1), ("S", "2", 1, 1), ("S", "1h", 1), ("S", "2", 1, 2),
+    ("W", "1h", 0), ("S", "2", 0, 3), ("S", "2", 2, 0), ("S", "3", 2, 0), ("D", "r", 2), ("D", "f", 1), ("D", "d", 2),
+    ("D", "r", 3), ("W", "r", 4), ("S", "f", 4), ("W", "d", 3), ("W", "f", 3), ("E", 3), ("S", "r", 5),
+    ("S", "2", 3, 0), ("S", "3", 3, 0), ("D", "f", 2), ("S", "d", 5), ("D", "2", 0, 0), ("W", "2", 0, 1),
+    ("S", "2h", 0, 1), ("S", "1", 2), ("D", "1", 0), ("W", "1h", 1), ("S", "2", 1, 3), ("D", "1", 1),
+    ("W", "2", 0, 2), ("S", "2h", 0, 2), ("D", "d", 3), ("D", "f", 3), ("S", "1", 3), ("D", "2", 1, 0),
+    ("D", "1h", 0), ("W", "2", 1, 1), ("S", "2h", 1, 1), ("W", "d", 4), ("W", "f", 4), ("E", 4), ("D", "2h", 0, 0),
+    ("S", "1", 4), ("W", "2", 1, 2), ("S", "2h", 1, 2), ("S", "3", 4, 0), ("W", "2", 0, 3), ("S", "2h", 0, 3),
+    ("W", "2", 2, 0), ("S", "2h", 2, 0), ("C", "tk", 0), ("D", "2h", 1, 0), ("W", "2", 3, 0), ("S", "2h", 3, 0),
+    ("D", "r", 4), ("D", "d", 4), ("W", "r", 5), ("S", "f", 5), ("S", "2", 4, 0), ("C", "tk", 1), ("W", "2", 1, 3),
+    ("S", "2h", 1, 3), ("D", "2", 0, 1), ("D", "2", 0, 2), ("D", "1h", 1), ("W", "1", 2), ("S", "2", 2, 1),
+    ("S", "2", 2, 2), ("D", "2", 1, 1), ("W", "1", 3), ("S", "2", 3, 1), ("S", "2", 3, 2), ("D", "f", 4),
+    ("S", "1h", 2), ("S", "1h", 3), ("S", "3", 3, 1), ("C", "tk", 2), ("D", "2", 1, 2), ("D", "3", 2, 0),
+    ("S", "3", 2, 1), ("D", "r", 5), ("S", "3", 0, 0), ("D", "2", 0, 3), ("D", "2", 2, 0), ("S", "3", 3, 2),
+    ("D", "2", 3, 0), ("D", "2h", 1, 1), ("S", "3", 2, 2), ("S", "3", 1, 0), ("C", "tk", 3), ("W", "d", 5),
+    ("W", "f", 5), ("E", 5), ("D", "2h", 0, 1), ("D", "2h", 0, 2), ("D", "3", 3, 0), ("W", "1", 4), ("S", "1h", 4),
+    ("D", "2", 1, 3), ("D", "2h", 1, 2), ("S", "1", 5), ("D", "1", 2), ("D", "1", 3), ("S", "2", 4, 1),
+    ("D", "2h", 0, 3), ("D", "2h", 2, 0), ("W", "2", 2, 1), ("S", "2h", 2, 1), ("W", "2", 2, 2), ("S", "2h", 2, 2),
+    ("W", "1h", 2), ("S", "2", 2, 3), ("D", "2h", 3, 0), ("W", "2", 3, 1), ("S", "2h", 3, 1), ("D", "d", 5),
+    ("S", "2", 4, 2), ("D", "2h", 1, 3), ("W", "2", 3, 2), ("S", "2h", 3, 2), ("W", "1h", 3), ("S", "2", 3, 3),
+    ("S", "2", 5, 0), ("S", "3", 5, 0), ("C", "tk", 4), ("C", "tk", 5), ("W", "2", 4, 0), ("S", "3", 4, 1),
+    ("D", "1", 4), ("S", "3", 3, 3), ("D", "f", 5), ("D", "1h", 2), ("D", "1h", 3), ("S", "2h", 4, 0), ("W", "1h", 4),
+    ("S", "2", 4, 3), ("C", "tk", 6), ("D", "2", 2, 1), ("D", "2", 2, 2), ("D", "3", 3, 1), ("W", "2", 2, 3),
+    ("S", "2h", 2, 3), ("D", "3", 4, 0), ("D", "2", 3, 1), ("D", "2", 3, 2), ("S", "3", 4, 2), ("D", "3", 2, 1),
+    ("W", "2", 3, 3), ("S", "2h", 3, 3), ("D", "3", 3, 2), ("S", "3", 3, 4), ("C", "tk", 7), ("D", "3", 2, 2),
+    ("W", "1", 5), ("S", "1h", 5), ("D", "3", 0, 0), ("D", "2", 4, 0), ("D", "3", 1, 0), ("S", "2", 5, 1),
+    ("W", "2", 4, 1), ("S", "2h", 4, 1), ("D", "2h", 3, 1), ("D", "2h", 3, 2), ("S", "3", 2, 3), ("D", "2h", 2, 1),
+    ("D", "1h", 4), ("D", "2h", 2, 2), ("D", "2", 2, 3), ("W", "3", 3, 0), ("W", "3", 3, 1), ("W", "3", 3, 2),
+    ("W", "3", 3, 3), ("S", "3h", 3, 0), ("S", "2", 5, 2), ("W", "2h", 4, 0), ("S", "3", 4, 3), ("D", "3", 3, 3),
+    ("S", "3", 3, 5), ("W", "2", 4, 2), ("S", "2h", 4, 2), ("D", "2", 3, 3), ("D", "1", 5), ("S", "3", 2, 4),
+    ("D", "2", 4, 1), ("W", "2", 5, 0), ("S", "2h", 5, 0), ("D", "2h", 4, 0), ("W", "1h", 5), ("S", "2", 5, 3),
+    ("D", "2h", 2, 3), ("D", "3", 5, 0), ("S", "3", 5, 1), ("C", "sq", 0), ("D", "2", 4, 2), ("D", "2", 5, 0),
+    ("W", "2", 4, 3), ("S", "2h", 4, 3), ("D", "2h", 3, 3), ("D", "3", 4, 1), ("D", "1h", 5), ("W", "2h", 4, 1),
+    ("S", "3", 4, 4), ("S", "3", 5, 2), ("W", "3", 2, 0), ("W", "3", 2, 1), ("W", "3", 2, 2), ("W", "3", 2, 3),
+    ("W", "3", 4, 0), ("W", "3", 4, 1), ("W", "3", 4, 2), ("W", "3", 4, 3), ("C", "mm", 1, 0, "near"),
+    ("D", "2h", 4, 1), ("D", "2", 4, 3), ("W", "2", 5, 1), ("S", "2h", 5, 1), ("D", "3", 3, 4), ("D", "3h", 3, 0),
+    ("W", "2h", 5, 0), ("S", "3", 5, 3), ("S", "3", 0, 1), ("W", "2", 5, 2), ("S", "2h", 5, 2), ("C", "sq", 1),
+    ("W", "3", 3, 4), ("S", "3h", 3, 1), ("C", "sq", 2), ("D", "2h", 4, 2), ("S", "3", 1, 1), ("D", "2", 5, 1),
+    ("W", "2", 5, 3), ("S", "2h", 5, 3), ("W", "2h", 3, 0), ("W", "2h", 3, 1), ("W", "2h", 3, 2), ("W", "2h", 3, 3),
+    ("S", "3", 3, 6), ("D", "2h", 5, 0), ("S", "3", 0, 2), ("D", "3", 4, 2), ("D", "3", 2, 3), ("D", "3", 4, 3),
+    ("D", "3", 2, 4), ("S", "3h", 2, 0), ("D", "2", 5, 2), ("S", "3", 1, 2), ("D", "2h", 4, 3), ("S", "3", 0, 3),
+    ("S", "3h", 4, 0), ("S", "3", 1, 3), ("W", "3", 5, 0), ("W", "3", 5, 1), ("W", "3", 5, 2), ("W", "3", 5, 3),
+    ("C", "mm", 2, 0, "near"), ("D", "3", 3, 5), ("D", "3", 5, 1), ("D", "3", 5, 2), ("W", "2h", 5, 1),
+    ("S", "3", 5, 4), ("D", "2", 5, 3), ("D", "2h", 5, 1), ("S", "3", 0, 4), ("W", "3", 2, 4), ("W", "3", 4, 4),
+    ("C", "mm", 1, 1, "near"), ("S", "3", 2, 5), ("D", "3", 0, 1), ("D", "2h", 5, 2), ("S", "3", 1, 4),
+    ("W", "3h", 2, 0), ("W", "3h", 4, 0), ("C", "mm", 1, 0, "far"), ("D", "3", 4, 4), ("D", "3h", 2, 0),
+    ("W", "2h", 4, 2), ("S", "3", 4, 5), ("D", "3", 5, 3), ("D", "3h", 3, 1), ("D", "3", 3, 6), ("S", "3h", 5, 0),
+    ("D", "3", 1, 1), ("D", "2h", 5, 3), ("D", "3", 0, 2), ("D", "3", 1, 2), ("D", "3", 0, 3), ("D", "3", 1, 3),
+    ("W", "3", 0, 0), ("W", "3", 0, 1), ("W", "3", 0, 2), ("W", "3", 0, 3), ("S", "3h", 0, 0), ("W", "3", 1, 0),
+    ("W", "3", 1, 1), ("W", "3", 1, 2), ("W", "3", 1, 3), ("S", "3h", 1, 0), ("W", "2h", 5, 2), ("S", "3", 5, 5),
+    ("S", "3", 0, 5), ("W", "3", 5, 4), ("C", "mm", 2, 1, "near"), ("D", "3h", 4, 0), ("S", "3h", 2, 1),
+    ("D", "3", 0, 4), ("S", "3", 1, 5), ("W", "3h", 0, 0), ("W", "3h", 1, 0), ("C", "mm", 0, 0, "all"),
+    ("D", "3", 2, 5), ("S", "3h", 4, 1), ("W", "3h", 3, 0), ("W", "3h", 5, 0), ("C", "mm", 2, 0, "far"),
+    ("D", "3", 5, 4), ("S", "3h", 5, 1), ("D", "3", 1, 4), ("D", "3h", 0, 0), ("W", "3", 0, 4), ("S", "3h", 0, 1),
+    ("W", "2h", 2, 0), ("W", "2h", 2, 1), ("W", "2h", 2, 2), ("W", "2h", 2, 3), ("S", "3", 2, 6), ("W", "3", 2, 5),
+    ("W", "3", 4, 5), ("C", "mm", 1, 2, "near"), ("D", "3h", 1, 0), ("W", "3", 1, 4), ("S", "3h", 1, 1),
+    ("D", "3h", 5, 0), ("W", "2h", 5, 3), ("S", "3", 5, 6), ("W", "2h", 0, 0), ("W", "2h", 0, 1), ("W", "2h", 0, 2),
+    ("W", "2h", 0, 3), ("S", "3", 0, 6), ("D", "3", 4, 5), ("D", "3h", 2, 1), ("W", "2h", 4, 3), ("S", "3", 4, 6),
+    ("W", "3", 3, 5), ("W", "3", 5, 5), ("C", "mm", 2, 2, "near"), ("W", "3h", 2, 1), ("W", "3h", 4, 1),
+    ("C", "mm", 1, 1, "far"), ("D", "3", 0, 5), ("W", "2h", 1, 0), ("W", "2h", 1, 1), ("W", "2h", 1, 2),
     ("W", "2h", 1, 3), ("S", "3", 1, 6), ("W", "3h", 0, 1), ("W", "3h", 1, 1), ("C", "mm", 0, 1, "all"),
-    ("D", "3", 0, 6), ("W", "3", 0, 5), ("S", "3h", 0, 2), ("D", "3", 3, 6), ("S", "3h", 3, 2), ("D", "3", 2, 6),
-    ("S", "3h", 2, 2), ("W", "3", 1, 5), ("S", "3h", 1, 2), ("S", "3h", 5, 2), ("S", "3h", 4, 2), ("D", "3", 1, 6),
-    ("W", "3", 0, 6), ("S", "3h", 0, 3), ("D", "3h", 0, 2), ("W", "3", 1, 6), ("S", "3h", 1, 3), ("W", "3", 3, 6),
-    ("W", "3", 5, 6), ("C", "mm", 2, 3, "near"), ("D", "3", 5, 6), ("D", "3h", 3, 2), ("S", "3h", 3, 3),
-    ("D", "3", 4, 6), ("D", "3h", 2, 2), ("W", "3", 2, 6), ("S", "3h", 2, 3), ("S", "3h", 5, 3), ("W", "3", 4, 6),
-    ("S", "3h", 4, 3), ("W", "3h", 0, 2), ("W", "3h", 1, 2), ("C", "mm", 0, 2, "all"), ("W", "3h", 0, 3),
-    ("W", "3h", 1, 3), ("C", "mm", 0, 3, "all"), ("C", "mm", 1, 3, "near"), ("W", "3h", 2, 2), ("W", "3h", 4, 2),
+    ("W", "3h", 3, 1), ("W", "3h", 5, 1), ("C", "mm", 2, 1, "far"), ("D", "3", 5, 5), ("S", "3h", 3, 2),
+    ("D", "3h", 0, 1), ("D", "3", 1, 5), ("W", "3", 0, 5), ("S", "3h", 0, 2), ("D", "3h", 4, 1), ("S", "3h", 2, 2),
+    ("D", "3h", 5, 1), ("S", "3h", 5, 2), ("D", "3h", 1, 1), ("W", "3", 1, 5), ("S", "3h", 1, 2), ("D", "3", 2, 6),
+    ("S", "3h", 4, 2), ("W", "3", 0, 6), ("S", "3h", 0, 3), ("W", "3", 3, 6), ("W", "3", 5, 6),
+    ("C", "mm", 2, 3, "near"), ("S", "3h", 3, 3), ("D", "3", 0, 6), ("W", "3", 1, 6), ("S", "3h", 1, 3),
+    ("W", "3", 2, 6), ("S", "3h", 2, 3), ("S", "3h", 5, 3), ("W", "3", 4, 6), ("C", "mm", 1, 3, "near"),
+    ("D", "3", 4, 6), ("S", "3h", 4, 3), ("W", "3h", 0, 2), ("W", "3h", 1, 2), ("C", "mm", 0, 2, "all"),
+    ("W", "3h", 0, 3), ("W", "3h", 1, 3), ("C", "mm", 0, 3, "all"), ("W", "3h", 2, 2), ("W", "3h", 4, 2),
     ("C", "mm", 1, 2, "far"), ("W", "3h", 2, 3), ("W", "3h", 4, 3), ("C", "mm", 1, 3, "far"), ("W", "3h", 3, 2),
     ("W", "3h", 5, 2), ("C", "mm", 2, 2, "far"), ("W", "3h", 3, 3), ("W", "3h", 5, 3), ("C", "mm", 2, 3, "far"),
 )
@@ -139,6 +140,11 @@
         copy.start()
         pending.append(copy)
 
+    barrier = pltpu.get_barrier_semaphore()
+    peers = [nbr(a, s) for a in "xyz" for s in (1, -1)] + [other]
+    for p in peers:
+        pl.semaphore_signal(barrier, inc=1, device_id=p, device_id_type=MESH)
+
     l_ex = pltpu.make_async_copy(exps, ex, loc.at[0])
     l_ex.start()
     l_fr = pltpu.make_async_copy(frag.at[rep], fb.at[0], loc.at[1])
@@ -150,13 +156,10 @@
     l_gn = pltpu.make_async_copy(gain, gb, loc.at[4])
     l_gn.start()
 
-    barrier = pltpu.get_barrier_semaphore()
-    peers = [nbr(a, s) for a in "xyz" for s in (1, -1)] + [other]
-    for p in peers:
-        pl.semaphore_signal(barrier, inc=1, device_id=p, device_id_type=MESH)
-
-    l_ex.wait()
-    eb[...] = ex[...].astype(F32).astype(BF16)
+    pl.semaphore_wait(barrier, len(peers))
+
+    up, down = nbr("z", 1), nbr("z", -1)
+    zu, zd, zo = mod4(rep + 1), mod4(rep - 1), mod4(rep + 2)
 
     def window(d):
         return eb.at[:, pl.ds(pl.multiple_of(128 * lax.div(3 * d, 2), 128), 256)]
@@ -172,23 +175,6 @@
             small = jnp.exp2(sign * e).astype(BF16)
             full = lax.dot_general(small, pick, (((0,), (0,)), ((), ())), preferred_element_type=F32)
             ref[slot] = full.astype(BF16)
-
-    expand(0)
-    l_gn.wait()
-    gf[...] = gb[...].astype(F32)
-    first = 6 * fs + lax.div(3 * rep, 2)
-    i = lax.broadcasted_iota(jnp.int32, (128, 128), 0)
-    l = lax.broadcasted_iota(jnp.int32, (128, 128), 1)
-    for h in range(2):
-        row = jnp.broadcast_to(gf[pl.ds(first + h, 1), :], (128, 128))
-        column = jnp.sum(jnp.where(i == l, row, 0.0), axis=1, keepdims=True)
-        gn[pl.ds(128 * h, 128), :] = jnp.broadcast_to(column, (128, 128))
-    acc[...] = jnp.zeros_like(acc)
-
-    pl.semaphore_wait(barrier, len(peers))
-
-    up, down = nbr("z", 1), nbr("z", -1)
-    zu, zd, zo = mod4(rep + 1), mod4(rep - 1), mod4(rep + 2)
 
     e_cp = [
         remote(window(zo), erl, e_snd.at[0], e_rcv.at[0], up),
@@ -215,11 +201,31 @@
             remote(rl.at[1, :, cc], fb.at[3, pl.ds(H, H), cc], a_snd.at[k + 5], a_rcv.at[k + 5], down),
         ]
 
-    for m in e_cp[:3]:
-        go(m)
     mine = pl.ds(pl.multiple_of(core * TOK, TOK), TOK)
-    t_cp = remote(tokens, tok.at[mine, :], t_snd.at[0], t_rcv.at[0], other)
-    l_tk = pltpu.make_async_copy(tokens, tok.at[mine, :], loc.at[5])
+    t_cp, l_tk = [], []
+    for i in range(8):
+        src = tokens.at[pl.ds(i * SLAB, SLAB), :]
+        dst = tok.at[pl.ds(pl.multiple_of(core * TOK + i * SLAB, SLAB), SLAB), :]
+        t_cp.append(remote(src, dst, t_snd.at[i], t_rcv.at[i], other))
+        l_tk.append(pltpu.make_async_copy(src, dst, loc.at[5 + i]))
+
+    def early():
+        l_ex.wait()
+        eb[...] = ex[...].astype(F32).astype(BF16)
+        for m in e_cp[:3]:
+            go(m)
+        expand(0)
+        l_gn.wait()
+        gf[...] = gb[...].astype(F32)
+        first = 6 * fs + lax.div(3 * rep, 2)
+        i = lax.broadcasted_iota(jnp.int32, (128, 128), 0)
+        l = lax.broadcasted_iota(jnp.int32, (128, 128), 1)
+        for h in range(2):
+            row = jnp.broadcast_to(gf[pl.ds(first + h, 1), :], (128, 128))
+            column = jnp.sum(jnp.where(i == l, row, 0.0), axis=1, keepdims=True)
+            gn[pl.ds(128 * h, 128), :] = jnp.broadcast_to(column, (128, 128))
+        e_cp[0].wait_recv()
+        go(e_cp[3])
 
     def prepare():
         for s in (1, 2, 3):
@@ -366,7 +372,7 @@
         mean = jnp.sum(s, axis=1, keepdims=True) * (1.0 / D)
         ss[rr, :] = jnp.broadcast_to(lax.rsqrt(mean + 1e-05) * (D ** -0.5), (128, 128))
 
-    s_cp = remote(ss.at[mine, :], ss.at[mine, :], t_snd.at[1], t_rcv.at[1], other)
+    s_cp = remote(ss.at[mine, :], ss.at[mine, :], t_snd.at[8], t_rcv.at[8], other)
     outs = []
     left = []
     seen = set()
@@ -384,10 +390,7 @@
             left.append(key)
         elif kind == "W":
             if once("wait"):
-                go(t_cp)
-                l_tk.start()
-                e_cp[0].wait_recv()
-                go(e_cp[3])
+                early()
             if key == ("d", 0):
                 prepare()
             for m in M[key]:
@@ -402,15 +405,22 @@
             if left_to_encode == 0:
                 outs.append(pltpu.make_async_copy(gr, grad_out, o_sem.at[0]))
                 outs[0].start()
+        elif key[0] == "tk":
+            l_tk[key[1]].start()
+            go(t_cp[key[1]])
+            if once("total"):
+                acc[...] = jnp.zeros_like(acc)
         elif key[0] == "sq":
             if once("own tokens"):
-                l_tk.wait()
+                for t in l_tk:
+                    t.wait()
             squares(key[1])
             if key[1] == 2:
                 go(s_cp)
         else:
             if once("all tokens"):
-                t_cp.wait_recv()
+                for t in t_cp:
+                    t.wait_recv()
             {"near": mm_near, "far": mm_far, "all": mm_level}[key[3]](key[1], key[2])
     s_cp.wait_recv()
 
@@ -467,13 +477,13 @@
             vm((4, 256, KVW), BF16),
             vm((4, 256, KVW), BF16),
             vm((2 * TOK, 128), F32),
-            dma((6,)),
+            dma((13,)),
             dma((6 * len(PARTS),)),
             dma((6 * len(PARTS),)),
             dma((4,)),
             dma((4,)),
-            dma((2,)),
-            dma((2,)),
+            dma((9,)),
+            dma((9,)),
             dma((42 * len(PARTS),)),
             dma((42 * len(PARTS),)),
             dma((4,)),

time: 137 us -> 137 us (level)
  no operation moved by 1% of the time
where the time goes in v5:
time: 137 us
  Pallas kernels  132 us (96%)
  other arithmetic  2.76 us (2%)
    pallas_call x1, Pallas kernels, body(): pl.pallas_call(kernel, out_shape=(jax.ShapeDtypeStruct((ROWS, KVW), F32),...  132 us
    sub x1, other arithmetic, body(): new_base = base_weight - OUTER_RATE * (grad + MOMENTUM_COEF * new_momentum)  2.76 us

profile of v5, /device:TPU:0, one launch (start us, length us, event | category | flops | bytes accessed | tf_op | source)
XLA Modules:
  0.0 136.9 jit_solution(9560474702922440322)
XLA Ops:
  0.6 0.0 copy-start.1
  0.6 0.0 copy-start.2
  0.7 132.3 %shard_map.85 = (f32[192,1024]{1,0:T(8,128)}, bf16[768,1024]{1,0:T(8,128)(2,1)}) custom-call(bf16[384,12288]{1,0:T(8,128)(2,1)} %tokens.1, bf16[96,128]{1,0:T(8,128)(2,1)} %bitcast.7, bf16[4,192,1024]{2,1,0:T(8,128)(2,1)} %bitcast.5, s32[32,768]{1,0:T(8,128)} %bitcast.6, f32[192,1024]{1,0:T(8,128)} %base.1, f32[192,1024]{1,0:T(8,128)} %mom.1), custom_call_target="tpu_custom_call" | custom-call | flops 19327352832 | bytes 30000000 | tf_op jit(solution)/shard_map/pallas_call | solution.py:452
  133.0 0.0 copy-done.1
  133.0 0.0 copy-done.2
  133.0 0.0 copy-start
  133.0 2.8 %multiply_subtract_fusion = (f32[192,1024]{1,0:T(8,128)}, f32[192,1024]{1,0:T(8,128)}) fusion(f32[192,1024]{1,0:T(8,128)S(1)} %copy-done.1, f32[192,1024]{1,0:T(8,128)} %get-tuple-element.5, f32[192,1024]{1,0:T(8,128)S(1)} %copy-done.2), kind=kLoop, calls=%fused_computation | loop fusion | flops 1179648 | bytes 3932160 | tf_op jit(solution)/shard_map/sub | solution.py:504
  135.7 0.0 copy-done
  135.7 1.1 copy.10
Async XLA Ops:
  0.6 132.3 %copy-start.1 = (f32[192,1024]{1,0:T(8,128)S(1)}, f32[192,1024]{1,0:T(8,128)}, u32[]{:S(2)}) copy-start(f32[192,1024]{1,0:T(8,128)} %base.1) | copy-start | bytes 2359300
  0.6 132.3 %copy-start.2 = (f32[192,1024]{1,0:T(8,128)S(1)}, f32[192,1024]{1,0:T(8,128)}, u32[]{:S(2)}) copy-start(f32[192,1024]{1,0:T(8,128)} %mom.1) | copy-start | bytes 2359300
  133.0 2.8 %copy-start = (bf16[768,1024]{1,0:T(8,128)(2,1)S(1)}, bf16[768,1024]{1,0:T(8,128)(2,1)}, u32[]{:S(2)}) copy-start(bf16[768,1024]{1,0:T(8,128)(2,1)} %get-tuple-element.14) | copy-start | bytes 4718596

commit v6 on v5

v6 whole, which is shorter than its diff:
```python
import jax
import jax.numpy as jnp
from jax import lax
from jax.experimental import pallas as pl
from jax.experimental.pallas import tpu as pltpu
from jax.sharding import PartitionSpec as P

MESH = pl.DeviceIdType.MESH
F32, BF16 = jnp.float32, jnp.bfloat16
D, KVW, BLOCK, TOK = 12288, 1024, 32, 384
ROWS = 192
FROWS = 768
SLAB = 48
OUTER_RATE = 0.7
MOMENTUM_COEF = 0.9
CLS = ((0, 256), (256, 384), (640, 384))
PARTS = (
    (0, 0, 128, ("x", "y", "z")),
    (0, 128, 128, ("y", "x", "z")),
    (1, 0, 128, ("z", "y", "x")),
    (2, 0, 128, ("z", "x", "y")),
    (1, 128, 256, ("y", "z", "x")),
    (2, 128, 256, ("x", "z", "y")),
)

SCHEDULE = (
    ("S", "r", 0), ("S", "d", 0), ("S", "r", 1), ("D", "r", 0), ("S", "d", 1), ("D", "d", 0), ("D", "r", 1),
    ("W", "r", 0), ("S", "f", 0), ("S", "r", 2), ("W", "r", 1), ("S", "f", 1), ("D", "d", 1), ("S", "d", 2),
    ("W", "d", 0), ("W", "f", 0), ("E", 0), ("S", "1", 0), ("S", "2", 0, 0), ("D", "f", 0), ("D", "r", 2),
    ("D", "f", 1), ("D", "d", 2), ("W", "r", 2), ("S", "f", 2), ("S", "r", 3), ("W", "d", 1), ("W", "f", 1), ("E", 1),
    ("D", "1", 0), ("S", "2", 1, 0), ("D", "2", 0, 0), ("S", "1", 1), ("D", "f", 2), ("D", "r", 3), ("S", "d", 3),
    ("W", "1", 0), ("S", "1h", 0), ("W", "2", 0, 0), ("S", "2h", 0, 0), ("W", "r", 3), ("S", "f", 3),
    ("S", "2", 0, 1), ("S", "r", 4), ("S", "2", 0, 2), ("W", "d", 2), ("W", "f", 2), ("E", 2), ("D", "d", 3),
    ("D", "f", 3), ("S", "d", 4), ("D", "2", 1, 0), ("D", "1h", 0), ("W", "2", 1, 0), ("S", "2h", 1, 0),
    ("W", "1", 1), ("S", "2", 1, 1), ("D", "1", 1), ("D", "2h", 0, 0), ("S", "1h", 1), ("S", "2", 1, 2),
    ("W", "1h", 0), ("S", "2", 0, 3), ("S", "2", 2, 0), ("D", "2h", 1, 0), ("S", "3", 2, 0), ("W", "d", 3),
    ("W", "f", 3), ("E", 3), ("D", "r", 4), ("W", "r", 4), ("S", "f", 4), ("S", "2", 3, 0), ("D", "2", 0, 1),
    ("D", "2", 0, 2), ("S", "3", 3, 0), ("D", "1h", 1), ("W", "2", 0, 1), ("S", "2h", 0, 1), ("D", "d", 4),
    ("S", "r", 5), ("W", "2", 0, 2), ("S", "2h", 0, 2), ("D", "2", 1, 1), ("W", "1h", 1), ("S", "2", 1, 3),
    ("S", "d", 5), ("D", "f", 4), ("S", "1", 2), ("S", "1", 3), ("D", "2", 1, 2), ("W", "2", 1, 1), ("S", "2h", 1, 1),
    ("W", "d", 4), ("W", "f", 4), ("E", 4), ("D", "3", 2, 0), ("D", "2", 3, 0), ("D", "2h", 1, 1), ("W", "2", 1, 2),
    ("S", "2h", 1, 2), ("D", "2h", 0, 1), ("D", "2", 0, 3), ("D", "2", 2, 0), ("D", "2h", 0, 2), ("D", "3", 3, 0),
    ("S", "1", 4), ("W", "2", 0, 3), ("S", "2h", 0, 3), ("D", "2", 1, 3), ("D", "2h", 1, 2), ("W", "2", 3, 0),
    ("S", "2h", 3, 0), ("W", "2", 2, 0), ("S", "2h", 2, 0), ("W", "2", 1, 3), ("S", "2h", 1, 3), ("S", "3", 4, 0),
    ("C", "tk", 0), ("D", "r", 5), ("D", "1", 2), ("D", "1", 3), ("W", "r", 5), ("S", "f", 5), ("S", "2", 4, 0),
    ("C", "tk", 1), ("D", "2h", 0, 3), ("W", "1", 2), ("S", "2", 2, 1), ("D", "2h", 3, 0), ("D", "2h", 1, 3),
    ("W", "1", 3), ("S", "2", 3, 1), ("D", "2h", 2, 0), ("S", "2", 2, 2), ("S", "2", 3, 2), ("D", "d", 5),
    ("S", "1h", 2), ("S", "1h", 3), ("C", "tk", 2), ("S", "3", 3, 1), ("S", "3", 2, 1), ("S", "3", 0, 0),
    ("S", "3", 3, 2), ("C", "tk", 3), ("S", "3", 2, 2), ("D", "f", 5), ("D", "1h", 2), ("D", "1h", 3),
    ("S", "3", 1, 0), ("W", "d", 5), ("W", "f", 5), ("E", 5), ("D", "1", 4), ("D", "2", 2, 1), ("D", "2", 2, 2),
    ("W", "1", 4), ("S", "1h", 4), ("D", "2", 3, 1), ("D", "3", 4, 0), ("D", "2", 3, 2), ("S", "1", 5),
    ("S", "2", 4, 1), ("D", "3", 3, 1), ("D", "3", 3, 2), ("W", "2", 2, 1), ("S", "2h", 2, 1), ("W", "2", 2, 2),
    ("S", "2h", 2, 2), ("W", "1h", 2), ("S", "2", 2, 3), ("D", "3", 2, 1), ("D", "3", 2, 2), ("W", "2", 3, 1),
    ("S", "2h", 3, 1), ("D", "3", 0, 0), ("D", "2", 4, 0), ("D", "3", 1, 0), ("S", "2", 4, 2), ("W", "2", 3, 2),
    ("S", "2h", 3, 2), ("W", "1h", 3), ("S", "2", 3, 3), ("W", "2", 4, 0), ("S", "2h", 4, 0), ("D", "1h", 4),
    ("S", "3", 5, 0), ("C", "tk", 4), ("S", "2", 5, 0), ("C", "tk", 5), ("D", "2h", 3, 1), ("S", "3", 4, 1),
    ("D", "2h", 2, 1), ("D", "2h", 2, 2), ("S", "3", 3, 3), ("C", "tk", 6), ("W", "1h", 4), ("S", "2", 4, 3),
    ("D", "2", 2, 3), ("W", "2", 2, 3), ("S", "2h", 2, 3), ("D", "2h", 3, 2), ("S", "3", 4, 2), ("C", "tk", 7),
    ("D", "1", 5), ("D", "2", 3, 3), ("W", "1", 5), ("S", "1h", 5), ("W", "2", 3, 3), ("S", "2h", 3, 3),
    ("D", "3", 3, 3), ("D", "2h", 2, 3), ("S", "3", 3, 4), ("D", "2h", 4, 0), ("D", "2", 4, 1), ("S", "2", 5, 1),
    ("S", "3", 2, 3), ("W", "2", 4, 1), ("S", "2h", 4, 1), ("D", "3", 5, 0), ("W", "3", 3, 0), ("W", "3", 3, 1),
    ("W", "3", 3, 2), ("W", "3", 3, 3), ("S", "3h", 3, 0), ("D", "2h", 3, 3), ("W", "2h", 4, 0), ("S", "3", 4, 3),
    ("D", "2", 4, 2), ("S", "2", 5, 2), ("S", "3", 3, 5), ("D", "3", 4, 1), ("D", "1h", 5), ("S", "3", 2, 4),
    ("D", "2", 5, 0), ("W", "2", 4, 2), ("S", "2h", 4, 2), ("W", "2", 5, 0), ("S", "2h", 5, 0), ("W", "1h", 5),
    ("S", "2", 5, 3), ("C", "sq", 0), ("C", "sq", 1), ("D", "3", 3, 4), ("D", "3h", 3, 0), ("S", "3", 5, 1),
    ("D", "3", 4, 2), ("D", "3", 2, 3), ("D", "3", 4, 3), ("W", "2h", 4, 1), ("S", "3", 4, 4), ("D", "2h", 4, 1),
    ("D", "2", 4, 3), ("W", "2", 4, 3), ("S", "2h", 4, 3), ("W", "3", 2, 0), ("W", "3", 2, 1), ("W", "3", 2, 2),
    ("W", "3", 2, 3), ("W", "3", 4, 0), ("W", "3", 4, 1), ("W", "3", 4, 2), ("W", "3", 4, 3),
    ("C", "mm", 1, 0, "near"), ("D", "2", 5, 1), ("D", "2h", 4, 2), ("D", "2h", 5, 0), ("W", "2", 5, 1),
    ("S", "2h", 5, 1), ("D", "3", 3, 5), ("D", "3", 5, 1), ("S", "3", 5, 2), ("C", "sq", 2), ("D", "2", 5, 2),
    ("S", "3", 0, 1), ("W", "2h", 5, 0), ("S", "3", 5, 3), ("D", "2h", 4, 3), ("W", "2", 5, 2), ("S", "2h", 5, 2),
    ("S", "3", 1, 1), ("W", "3", 3, 4), ("S", "3h", 3, 1), ("D", "2", 5, 3), ("S", "3", 0, 2), ("D", "2h", 5, 1),
    ("W", "2", 5, 3), ("S", "2h", 5, 3), ("D", "3", 5, 2), ("W", "2h", 5, 1), ("S", "3", 5, 4), ("D", "3", 2, 4),
    ("S", "3h", 2, 0), ("D", "3", 0, 1), ("S", "3", 1, 2), ("D", "2h", 5, 2), ("S", "3", 0, 3), ("S", "3h", 4, 0),
    ("S", "3", 1, 3), ("W", "3", 5, 0), ("W", "3", 5, 1), ("W", "3", 5, 2), ("W", "3", 5, 3),
    ("C", "mm", 2, 0, "near"), ("D", "3", 1, 1), ("D", "3", 0, 2), ("D", "2h", 5, 3), ("S", "3", 0, 4),
    ("W", "3", 2, 4), ("W", "3", 4, 4), ("C", "mm", 1, 1, "near"), ("D", "3", 4, 4), ("D", "3h", 2, 0),
    ("S", "3", 2, 5), ("D", "3", 1, 2), ("D", "3", 0, 3), ("D", "3", 1, 3), ("S", "3", 1, 4), ("D", "3", 5, 3),
    ("D", "3h", 3, 1), ("S", "3h", 5, 0), ("W", "3h", 2, 0), ("W", "3h", 4, 0), ("C", "mm", 1, 0, "far"),
    ("D", "3h", 4, 0), ("W", "2h", 4, 2), ("S", "3", 4, 5), ("D", "3", 0, 4), ("W", "3", 0, 0), ("W", "3", 0, 1),
    ("W", "3", 0, 2), ("W", "3", 0, 3), ("S", "3h", 0, 0), ("D", "3", 5, 4), ("W", "2h", 5, 2), ("S", "3", 5, 5),
    ("W", "3", 5, 4), ("C", "mm", 2, 1, "near"), ("W", "3", 1, 0), ("W", "3", 1, 1), ("W", "3", 1, 2),
    ("W", "3", 1, 3), ("S", "3h", 1, 0), ("D", "3", 1, 4), ("S", "3", 0, 5), ("W", "3h", 3, 0), ("W", "3h", 5, 0),
    ("C", "mm", 2, 0, "far"), ("D", "3", 2, 5), ("S", "3h", 2, 1), ("D", "3h", 0, 0), ("D", "3h", 1, 0),
    ("S", "3", 1, 5), ("D", "3h", 5, 0), ("S", "3h", 5, 1), ("S", "3h", 4, 1), ("W", "3h", 0, 0), ("W", "3h", 1, 0),
    ("C", "mm", 0, 0, "all"), ("W", "3", 2, 5), ("W", "3", 4, 5), ("C", "mm", 1, 2, "near"), ("D", "3", 0, 5),
    ("W", "3", 0, 4), ("S", "3h", 0, 1), ("D", "3", 5, 5), ("W", "2h", 3, 0), ("W", "2h", 3, 1), ("W", "2h", 3, 2),
    ("W", "2h", 3, 3), ("S", "3", 3, 6), ("D", "3", 4, 5), ("D", "3h", 2, 1), ("W", "2h", 2, 0), ("W", "2h", 2, 1),
    ("W", "2h", 2, 2), ("W", "2h", 2, 3), ("S", "3", 2, 6), ("W", "3", 1, 4), ("S", "3h", 1, 1), ("W", "3", 3, 5),
    ("W", "3", 5, 5), ("C", "mm", 2, 2, "near"), ("D", "3", 1, 5), ("W", "2h", 0, 0), ("W", "2h", 0, 1),
    ("W", "2h", 0, 2), ("W", "2h", 0, 3), ("S", "3", 0, 6), ("D", "3h", 5, 1), ("W", "2h", 5, 3), ("S", "3", 5, 6),
    ("D", "3h", 4, 1), ("W", "2h", 4, 3), ("S", "3", 4, 6), ("W", "3h", 2, 1), ("W", "3h", 4, 1),
    ("C", "mm", 1, 1, "far"), ("W", "3h", 3, 1), ("W", "3h", 5, 1), ("C", "mm", 2, 1, "far"), ("W", "3h", 0, 1),
    ("W", "3h", 1, 1), ("C", "mm", 0, 1, "all"), ("D", "3h", 0, 1), ("D", "3h", 1, 1), ("W", "2h", 1, 0),
    ("W", "2h", 1, 1), ("W", "2h", 1, 2), ("W", "2h", 1, 3), ("S", "3", 1, 6), ("D", "3", 0, 6), ("W", "3", 0, 5),
    ("S", "3h", 0, 2), ("D", "3", 3, 6), ("S", "3h", 3, 2), ("D", "3", 2, 6), ("S", "3h", 2, 2), ("W", "3", 1, 5),
    ("S", "3h", 1, 2), ("S", "3h", 5, 2), ("S", "3h", 4, 2), ("D", "3", 1, 6), ("W", "3", 0, 6), ("S", "3h", 0, 3),
    ("W", "3", 2, 6), ("W", "3", 4, 6), ("C", "mm", 1, 3, "near"), ("D", "3h", 0, 2), ("W", "3", 1, 6),
    ("S", "3h", 1, 3), ("D", "3", 5, 6), ("D", "3h", 3, 2), ("W", "3", 3, 6), ("S", "3h", 3, 3), ("D", "3", 4, 6),
    ("D", "3h", 2, 2), ("S", "3h", 2, 3), ("W", "3", 5, 6), ("C", "mm", 2, 3, "near"), ("D", "3h", 5, 2),
    ("S", "3h", 5, 3), ("D", "3h", 4, 2), ("S", "3h", 4, 3), ("W", "3h", 0, 2), ("W", "3h", 1, 2),
    ("C", "mm", 0, 2, "all"), ("W", "3h", 0, 3), ("W", "3h", 1, 3), ("C", "mm", 0, 3, "all"), ("W", "3h", 2, 2),
    ("W", "3h", 4, 2), ("C", "mm", 1, 2, "far"), ("W", "3h", 2, 3), ("W", "3h", 4, 3), ("C", "mm", 1, 3, "far"),
    ("W", "3h", 3, 2), ("W", "3h", 5, 2), ("C", "mm", 2, 2, "far"), ("W", "3h", 3, 3), ("W", "3h", 5, 3),
    ("C", "mm", 2, 3, "far"), ("C", "fin", 1), ("C", "fin", 2), ("C", "fin", 0),
)

THRESH = ((0.25, 0.5), (0.75, 1.0), (1.25, 1.5), (1.75, 2.0), (2.5, 3.0), (3.5, 4.0), (5.0, 6.0))


def mod4(v):
    return lax.rem(v + 8, 4)


def kernel(
    tokens, gain, frag, exps, base, mom,
    grad_out, kv_out,
    w0, w1, w2, tok, acc, kv, fv, fb, rl, bs, ms, gr, gb, gf, gn, ex, eb, er, erl, sc, iv, ss,
    loc, a_snd, a_rcv, e_snd, e_rcv, t_snd, t_rcv, g_snd, g_rcv, o_sem,
):
    W = (w0, w1, w2)
    rep = lax.axis_index("replica")
    fs = lax.axis_index("fsdp")
    core = lax.axis_index("tensor")
    pos = {"x": lax.rem(fs, 4), "y": lax.div(fs, 4), "z": rep}

    def nbr(axis, step):
        c = dict(pos)
        c[axis] = mod4(pos[axis] + step)
        return (c["z"], c["y"] * 4 + c["x"], core)

    other = (rep, fs, 1 - core)

    def remote(src, dst, ss_, rs_, dev):
        return pltpu.make_async_remote_copy(
            src_ref=src, dst_ref=dst, send_sem=ss_, recv_sem=rs_, device_id=dev, device_id_type=MESH
        )

    pending = []

    def go(copy):
        copy.start()
        pending.append(copy)

    barrier = pltpu.get_barrier_semaphore()
    peers = [nbr(a, s) for a in "xyz" for s in (1, -1)] + [other]
    for p in peers:
        pl.semaphore_signal(barrier, inc=1, device_id=p, device_id_type=MESH)

    l_ex = pltpu.make_async_copy(exps, ex, loc.at[0])
    l_ex.start()
    l_fr = pltpu.make_async_copy(frag, fv, loc.at[1])
    l_fr.start()
    l_bs = pltpu.make_async_copy(base, bs, loc.at[2])
    l_bs.start()
    l_ms = pltpu.make_async_copy(mom, ms, loc.at[3])
    l_ms.start()
    l_gn = pltpu.make_async_copy(gain, gb, loc.at[4])
    l_gn.start()

    pl.semaphore_wait(barrier, len(peers))
    l_fr.wait()

    up, down = nbr("z", 1), nbr("z", -1)
    zu, zd, zo = mod4(rep + 1), mod4(rep - 1), mod4(rep + 2)

    def window(d):
        return eb.at[:, pl.ds(pl.multiple_of(128 * lax.div(3 * d, 2), 128), 256)]

    off = 64 * lax.rem(rep, 2)

    def expand(p):
        c, sub, width, _ = PARTS[p]
        lo = CLS[c][0] + sub
        j = lax.broadcasted_iota(jnp.int32, (BLOCK, width), 0)
        n = lax.broadcasted_iota(jnp.int32, (BLOCK, width), 1)
        pick = jnp.where(j == lax.div(n + lo, BLOCK), 1.0, 0.0).astype(BF16)
        for slot in range(4):
            e = (window(rep)[...] if slot == 0 else er[slot]).astype(F32)
            for ref, sign in ((sc, 1.0), (iv, -1.0)):
                small = jnp.exp2(sign * e).astype(BF16)
                full = lax.dot_general(small, pick, (((0,), (0,)), ((), ())), preferred_element_type=F32)
                ref[slot, :, pl.ds(lo, width)] = full.astype(BF16)

    e_cp = [
        remote(window(zo), erl, e_snd.at[0], e_rcv.at[0], up),
        remote(window(zu), er.at[1], e_snd.at[1], e_rcv.at[1], up),
        remote(window(zd), er.at[2], e_snd.at[2], e_rcv.at[2], down),
        remote(erl, er.at[3], e_snd.at[3], e_rcv.at[3], up),
    ]

    def cols(p):
        c, lo, width, _ = PARTS[p]
        return pl.ds(CLS[c][0] + lo, width)

    H = ROWS // 2

    def a2a(p):
        k = 6 * p
        cc = cols(p)
        return [
            remote(fv.at[zo, pl.ds(0, H), cc], rl.at[0, :, cc], a_snd.at[k], a_rcv.at[k], up),
            remote(fv.at[zo, pl.ds(H, H), cc], rl.at[1, :, cc], a_snd.at[k + 1], a_rcv.at[k + 1], down),
            remote(fv.at[zu, :, cc], fb.at[1, :, cc], a_snd.at[k + 2], a_rcv.at[k + 2], up),
            remote(fv.at[zd, :, cc], fb.at[2, :, cc], a_snd.at[k + 3], a_rcv.at[k + 3], down),
            remote(rl.at[0, :, cc], fb.at[3, pl.ds(0, H), cc], a_snd.at[k + 4], a_rcv.at[k + 4], up),
            remote(rl.at[1, :, cc], fb.at[3, pl.ds(H, H), cc], a_snd.at[k + 5], a_rcv.at[k + 5], down),
        ]

    mine = pl.ds(pl.multiple_of(core * TOK, TOK), TOK)
    t_cp, l_tk = [], []
    for i in range(8):
        src = tokens.at[pl.ds(i * SLAB, SLAB), :]
        dst = tok.at[pl.ds(pl.multiple_of(core * TOK + i * SLAB, SLAB), SLAB), :]
        t_cp.append(remote(src, dst, t_snd.at[i], t_rcv.at[i], other))
        l_tk.append(pltpu.make_async_copy(src, dst, loc.at[5 + i]))

    def early():
        l_ex.wait()
        eb[...] = ex[...].astype(F32).astype(BF16)
        for m in e_cp[:3]:
            go(m)
        l_gn.wait()
        gf[...] = gb[...].astype(F32)
        first = 6 * fs + lax.div(3 * rep, 2)
        i = lax.broadcasted_iota(jnp.int32, (128, 128), 0)
        l = lax.broadcasted_iota(jnp.int32, (128, 128), 1)
        for h in range(2):
            row = jnp.broadcast_to(gf[pl.ds(first + h, 1), :], (128, 128))
            column = jnp.sum(jnp.where(i == l, row, 0.0), axis=1, keepdims=True)
            gn[pl.ds(128 * h, 128), :] = jnp.broadcast_to(column, (128, 128))
        e_cp[0].wait_recv()
        go(e_cp[3])

    def prepare():
        for s in (1, 2, 3):
            e_cp[s].wait_recv()
        l_bs.wait()
        l_ms.wait()

    def encode(p):
        c, sub, width, _ = PARTS[p]
        lo = CLS[c][0] + sub
        row0 = pl.multiple_of(rep * ROWS, ROWS)

        def step(t, carry):
            rr = pl.ds(pl.multiple_of(t * SLAB, SLAB), SLAB)
            wr = pl.ds(pl.multiple_of(row0 + t * SLAB, SLAB), SLAB)
            fr = pl.ds(pl.multiple_of(off + t * SLAB, 16), SLAB)
            g = gn[fr, :]
            for k in range(width // 128):
                cc = pl.ds(lo + 128 * k, 128)
                b = bs[rr, cc]
                total = jnp.zeros((SLAB, 128), F32)
                for s in range(4):
                    v = (b - (fv[rep, rr, cc] if s == 0 else fb[s, rr, cc]).astype(F32)) * iv[s, fr, cc].astype(F32)
                    m = jnp.abs(v)
                    level = jnp.zeros_like(m)
                    for mid, val in THRESH:
                        level = jnp.where(m >= mid, val, level)
                    total = total + jnp.where(v < 0.0, -level, level) * sc[s, fr, cc].astype(F32)
                grad = total * 0.25
                nm = MOMENTUM_COEF * ms[rr, cc] + grad
                nb = b - OUTER_RATE * (grad + MOMENTUM_COEF * nm)
                gr[rr, cc] = grad
                W[c][pos["y"], pos["x"], wr, pl.ds(sub + 128 * k, 128)] = (nb * g).astype(BF16)
            return carry

        lax.fori_loop(0, ROWS // SLAB, step, 0)

    def place(p, **at):
        half = at.pop("half", None)
        xs, ys = at.get("x", slice(None)), at.get("y", slice(None))
        if "z" in at:
            r0, n = at["z"] * ROWS, ROWS
        else:
            r0, n = 0, FROWS
        if half is not None:
            n = n // 2
            r0 = r0 + half * n
        if not isinstance(r0, int):
            r0 = pl.multiple_of(r0, 96)
        c, lo, width, _ = PARTS[p]
        return W[c].at[ys, xs, pl.ds(r0, n), pl.ds(lo, width)]

    M = {}
    OFF = (0, 1, -1, 2)
    used = [0]

    def both(*pair):
        out = []
        for j, s in enumerate((1, -1)):
            axis, ref = pair[j]
            out.append(remote(ref, ref, g_snd.at[used[0]], g_rcv.at[used[0]], nbr(axis, s)))
            used[0] += 1
        return out

    def full(p, axis, **fixed):
        here = place(p, **fixed, **{axis: pos[axis]})
        return both((axis, here), (axis, here))

    def half(p, axis, **fixed):
        return both(
            *[(axis, place(p, **fixed, **{axis: mod4(pos[axis] - s), "half": j})) for j, s in enumerate((1, -1))]
        )

    for p in range(len(PARTS)):
        m = a2a(p)
        M["r", p], M["d", p], M["f", p] = m[:2], m[2:4], m[4:]
        a, b, l = PARTS[p][3]
        R, S = (a, b) if b == "z" else (b, a)
        at = {b: pos[b], l: pos[l]}
        M["1", p], M["1h", p] = full(p, a, **at), half(p, a, **at)
        for i in range(4):
            at = {a: mod4(pos[a] + OFF[i]), l: pos[l]}
            M["2", p, i], M["2h", p, i] = full(p, b, **at), half(p, b, **at)
            M["3", p, i] = full(p, l, **{R: pos[R], S: mod4(pos[S] + OFF[i])})
            M["3h", p, i] = half(p, l, **{R: mod4(pos[R] + OFF[i])})
            if i:
                M["3", p, 3 + i] = full(p, l, **{R: mod4(pos[R] + OFF[i])})

    def mm(c, count, coords):
        lo, width = CLS[c]
        cc = pl.ds(lo, width)

        def chunk(t, carry):
            yy, xx = coords(t)
            kk = pl.ds(pl.multiple_of((yy * 4 + xx) * FROWS, FROWS), FROWS)

            def block(m, carry):
                mr = pl.ds(pl.multiple_of(m * 256, 256), 256)
                acc[mr, cc] += jnp.dot(tok[mr, kk], W[c][yy, xx], preferred_element_type=F32)
                return carry

            return lax.fori_loop(0, 3, block, carry)

        lax.fori_loop(0, count, chunk, 0)

    def offset(i):
        return i + lax.div(i, 2) - 2 * lax.div(i, 3)

    def mm_near(c, i):
        if c == 1:
            yy = mod4(pos["y"] + OFF[i])
            mm(c, 3, lambda t: (yy, mod4(pos["x"] + offset(t))))
        else:
            xx = mod4(pos["x"] + OFF[i])
            mm(c, 3, lambda t: (mod4(pos["y"] + offset(t)), xx))

    def mm_far(c, i):
        if c == 1:
            mm(c, 1, lambda t: (mod4(pos["y"] + OFF[i]), mod4(pos["x"] + 2)))
        else:
            mm(c, 1, lambda t: (mod4(pos["y"] + 2), mod4(pos["x"] + OFF[i])))

    same = len({p[3] for p in PARTS if p[0] == 0}) == 1

    def mm_row(c, i):
        by_y = PARTS[[p[0] for p in PARTS].index(0)][3][1] == "y"
        at = mod4(pos["y" if by_y else "x"] + OFF[i])
        mm(c, 4, (lambda t: (at, t)) if by_y else (lambda t: (t, at)))

    def mm_level(c, i):
        def coords(t):
            turn = lax.div(t, i + 1)
            iy = i * (1 - turn) + (t - i - 1) * turn
            ix = t * (1 - turn) + i * turn
            return mod4(pos["y"] + offset(iy)), mod4(pos["x"] + offset(ix))

        mm(c, 2 * i + 1, coords)

    def squares(i):
        rr = pl.ds(pl.multiple_of(core * TOK + i * 128, 128), 128)

        def step(t, s):
            for k in range(4):
                v = tok[rr, pl.ds(pl.multiple_of(t * 512 + k * 128, 128), 128)].astype(F32)
                s = s + v * v
            return s

        s = lax.fori_loop(0, D // 512, step, jnp.zeros((128, 128), F32))
        mean = jnp.sum(s, axis=1, keepdims=True) * (1.0 / D)
        ss[rr, :] = jnp.broadcast_to(lax.rsqrt(mean + 1e-05) * (D ** -0.5), (128, 128))

    def finish(c):
        lo, width = CLS[c]
        cc = pl.ds(lo, width)

        def scale(m, carry):
            mr = pl.ds(pl.multiple_of(m * 64, 64), 64)
            for k in range(width // 128):
                at = pl.ds(lo + 128 * k, 128)
                kv[mr, at] = (acc[mr, at] * ss[mr, :]).astype(BF16)
            return carry

        lax.fori_loop(0, 2 * TOK // 64, scale, 0)
        outs.append(pltpu.make_async_copy(kv.at[:, cc], kv_out.at[:, cc], o_sem.at[1 + c]))
        outs[-1].start()

    s_cp = remote(ss.at[mine, :], ss.at[mine, :], t_snd.at[8], t_rcv.at[8], other)
    outs = []
    left = []
    late = []
    seen = set()

    def once(name):
        new = name not in seen
        seen.add(name)
        return new

    for kind, *key in SCHEDULE:
        key = tuple(key)
        if kind == "S":
            for m in M[key]:
                m.start()
            left.append(key)
        elif kind == "W":
            if once("wait"):
                early()
            if key[0] == "d":
                if once("prepare"):
                    prepare()
                expand(key[1])
            for m in M[key]:
                m.wait_recv()
        elif kind == "D":

            @pl.when(core == 1)
            def _():
                for m in M[key]:
                    m.wait_send()

            left.remove(key)
            late.append(key)
        elif kind == "E":
            encode(*key)
            left_to_encode = len(PARTS) - 1 - key[0]
            if left_to_encode == 0:
                outs.append(pltpu.make_async_copy(gr, grad_out, o_sem.at[0]))
                outs[0].start()
        elif key[0] == "tk":
            l_tk[key[1]].start()
            go(t_cp[key[1]])
            if once("total"):
                acc[...] = jnp.zeros_like(acc)
        elif key[0] == "sq":
            if once("own tokens"):
                for t in l_tk:
                    t.wait()
            squares(key[1])
            if key[1] == 2:
                go(s_cp)
        elif key[0] == "fin":
            if once("factors"):
                s_cp.wait_recv()
            finish(key[1])
        else:
            if once("all tokens"):
                for t in t_cp:
                    t.wait_recv()
            {"near": mm_near, "far": mm_far, "all": mm_row if same else mm_level}[key[3]](key[1], key[2])
    for key in left:
        for m in M[key]:
            m.wait_send()

    @pl.when(core == 0)
    def _():
        for key in late:
            for m in M[key]:
                m.wait_send()

    for p in pending:
        p.wait_send()
    for o in outs:
        o.wait()


def write_kernel(grad, base, mom, kv, nb_out, nm_out, kv_out, gr, bs, ms, ks, in_sem, out_sem, kv_in, kv_sem):
    loads, stores, moves = [], [], []
    for q in range(4):
        rr = pl.ds(q * SLAB, SLAB)
        for i, (src, dst) in enumerate(((grad, gr), (base, bs), (mom, ms))):
            loads.append(pltpu.make_async_copy(src.at[rr, :], dst.at[rr, :], in_sem.at[3 * q + i]))
            loads[-1].start()
    for q in range(4):
        rr = pl.ds(q * 192, 192)
        moves.append(pltpu.make_async_copy(kv.at[rr, :], ks.at[rr, :], kv_in.at[q]))
        moves[-1].start()
    for q in range(4):
        rr = pl.ds(q * SLAB, SLAB)
        for i in range(3):
            loads[3 * q + i].wait()
        g = gr[rr, :]
        nm = MOMENTUM_COEF * ms[rr, :] + g
        ms[rr, :] = nm
        bs[rr, :] = bs[rr, :] - OUTER_RATE * (g + MOMENTUM_COEF * nm)
        stores.append(pltpu.make_async_copy(bs.at[rr, :], nb_out.at[rr, :], out_sem.at[2 * q]))
        stores.append(pltpu.make_async_copy(ms.at[rr, :], nm_out.at[rr, :], out_sem.at[2 * q + 1]))
        stores[-2].start()
        stores[-1].start()
    for q in range(4):
        rr = pl.ds(q * 192, 192)
        moves[q].wait()
        stores.append(pltpu.make_async_copy(ks.at[rr, :], kv_out.at[rr, :], kv_sem.at[q]))
        stores[-1].start()
    for copy in stores:
        copy.wait()


def body(tokens, norm_gain, fragment, exponents, base_weight, momentum):
    any_ = pl.BlockSpec(memory_space=pl.ANY)
    dma = pltpu.SemaphoreType.DMA
    vm = pltpu.VMEM
    grad, keys_values = pl.pallas_call(
        kernel,
        out_shape=(
            jax.ShapeDtypeStruct((ROWS, KVW), F32),
            jax.ShapeDtypeStruct((2 * TOK, KVW), BF16),
        ),
        in_specs=[any_] * 6,
        out_specs=[any_] * 2,
        scratch_shapes=[
            *[vm((4, 4, FROWS, width), BF16) for _, width in CLS],
            vm((2 * TOK, D), BF16),
            vm((2 * TOK, KVW), F32),
            vm((2 * TOK, KVW), BF16),
            vm((4, ROWS, KVW), BF16),
            vm((4, ROWS, KVW), BF16),
            vm((2, ROWS // 2, KVW), BF16),
            vm((ROWS, KVW), F32),
            vm((ROWS, KVW), F32),
            vm((ROWS, KVW), F32),
            vm((D // 128, 128), BF16),
            vm((D // 128, 128), F32),
            vm((256, 128), F32),
            vm((BLOCK, 4 * ROWS), jnp.int32),
            vm((BLOCK, 4 * ROWS), BF16),
            vm((4, BLOCK, 256), BF16),
            vm((BLOCK, 256), BF16),
            vm((4, 256, KVW), BF16),
            vm((4, 256, KVW), BF16),
            vm((2 * TOK, 128), F32),
            dma((13,)),
            dma((6 * len(PARTS),)),
            dma((6 * len(PARTS),)),
            dma((4,)),
            dma((4,)),
            dma((9,)),
            dma((9,)),
            dma((42 * len(PARTS),)),
            dma((42 * len(PARTS),)),
            dma((4,)),
        ],
        compiler_params=pltpu.CompilerParams(
            collective_id=0, has_side_effects=True, vmem_limit_bytes=62 * 1024 * 1024
        ),
        cost_estimate=pl.CostEstimate(flops=2 * 768 * 12288 * 1024, bytes_accessed=30_000_000, transcendentals=0),
    )(
        tokens,
        norm_gain.reshape(D // 128, 128),
        fragment.reshape(4, ROWS, KVW),
        exponents[0].T,
        base_weight,
        momentum,
    )
    return pl.pallas_call(
        write_kernel,
        out_shape=(
            jax.ShapeDtypeStruct((ROWS, KVW), F32),
            jax.ShapeDtypeStruct((ROWS, KVW), F32),
            jax.ShapeDtypeStruct((2 * TOK, KVW), BF16),
        ),
        in_specs=[any_] * 4,
        out_specs=[any_] * 3,
        scratch_shapes=[vm((ROWS, KVW), F32)] * 3
        + [vm((2 * TOK, KVW), BF16), dma((12,)), dma((8,)), dma((4,)), dma((4,))],
        compiler_params=pltpu.CompilerParams(vmem_limit_bytes=62 * 1024 * 1024),
        cost_estimate=pl.CostEstimate(flops=6 * ROWS * KVW, bytes_accessed=7_000_000, transcendentals=0),
    )(grad, base_weight, momentum, keys_values)


def solution(mesh):
    in_specs = (
        P(("replica", "fsdp", "tensor"), None),
        P(),
        P("replica", "fsdp", "tensor"),
        P("replica", "fsdp", "tensor"),
        P(("fsdp", "replica"), "tensor"),
        P(("fsdp", "replica"), "tensor"),
    )
    out_specs = (
        P(("fsdp", "replica"), "tensor"),
        P(("fsdp", "replica"), "tensor"),
        P(("replica", "fsdp"), "tensor"),
    )
    return jax.shard_map(body, mesh=mesh, in_specs=in_specs, out_specs=out_specs, check_vma=False)
```

time: 137 us -> 139 us (1.015)
  Pallas kernels: 132 us -> 138 us
  other arithmetic: 2.76 us -> 0 us
    pallas_call x0 -> x1, Pallas kernels: none -> 3.61 us  [body(): pl.pallas_call(write_kernel, out_shape=(jax.ShapeDtypeStruct((ROWS, KVW),...]
    sub x1 -> x0, other arithmetic: 2.76 us -> none  [body(): new_base = base_weight - OUTER_RATE * (grad + MOMENTUM_COEF * new_momentum)]
    pallas_call x1, Pallas kernels: 132 us -> 134 us  [body(): pl.pallas_call(kernel, out_shape=(jax.ShapeDtypeStruct((ROWS, KVW), F32),...]
where the time goes in v6:
time: 139 us
  Pallas kernels  138 us (99%)
    pallas_call x1, Pallas kernels, body(): pl.pallas_call(kernel, out_shape=(jax.ShapeDtypeStruct((ROWS, KVW), F32),...  134 us
    pallas_call x1, Pallas kernels, body(): pl.pallas_call(write_kernel, out_shape=(jax.ShapeDtypeStruct((ROWS, KVW),...  3.61 us

profile of v6, /device:TPU:0, one launch (start us, length us, event | category | flops | bytes accessed | tf_op | source)
XLA Modules:
  0.0 138.7 jit_solution(12427088772953750616)
XLA Ops:
  0.6 134.4 %shard_map.85 = (f32[192,1024]{1,0:T(8,128)}, bf16[768,1024]{1,0:T(8,128)(2,1)}) custom-call(bf16[384,12288]{1,0:T(8,128)(2,1)} %tokens.1, bf16[96,128]{1,0:T(8,128)(2,1)} %bitcast.7, bf16[4,192,1024]{2,1,0:T(8,128)(2,1)} %bitcast.5, s32[32,768]{1,0:T(8,128)} %bitcast.6, f32[192,1024]{1,0:T(8,128)} %base.3, f32[192,1024]{1,0:T(8,128)} %mom.3), custom_call_target="tpu_custom_call" | custom-call | flops 19327352832 | bytes 30000000 | tf_op jit(solution)/shard_map/pallas_call | solution.py:514
  135.0 3.6 %shard_map.86 = (f32[192,1024]{1,0:T(8,128)}, f32[192,1024]{1,0:T(8,128)}, bf16[768,1024]{1,0:T(8,128)(2,1)}) custom-call(f32[192,1024]{1,0:T(8,128)} %get-tuple-element.5.grad, f32[192,1024]{1,0:T(8,128)} %base.3, f32[192,1024]{1,0:T(8,128)} %mom.3, bf16[768,1024]{1,0:T(8,128)(2,1)} %get-tuple-element.6.kv), custom_call_target="tpu_custom_call" | custom-call | flops 1179648 | bytes 7000000 | tf_op jit(solution)/shard_map/pallas_call | solution.py:566

commit v7 on v6

--- a/solution.py
+++ b/solution.py
@@ -24,88 +24,96 @@
 )
 
 SCHEDULE = (
-    ("S", "r", 0), ("S", "d", 0), ("S", "r", 1), ("D", "r", 0), ("S", "d", 1), ("D", "d", 0), ("D", "r", 1),
-    ("W", "r", 0), ("S", "f", 0), ("S", "r", 2), ("W", "r", 1), ("S", "f", 1), ("D", "d", 1), ("S", "d", 2),
-    ("W", "d", 0), ("W", "f", 0), ("E", 0), ("S", "1", 0), ("S", "2", 0, 0), ("D", "f", 0), ("D", "r", 2),
-    ("D", "f", 1), ("D", "d", 2), ("W", "r", 2), ("S", "f", 2), ("S", "r", 3), ("W", "d", 1), ("W", "f", 1), ("E", 1),
-    ("D", "1", 0), ("S", "2", 1, 0), ("D", "2", 0, 0), ("S", "1", 1), ("D", "f", 2), ("D", "r", 3), ("S", "d", 3),
-    ("W", "1", 0), ("S", "1h", 0), ("W", "2", 0, 0), ("S", "2h", 0, 0), ("W", "r", 3), ("S", "f", 3),
-    ("S", "2", 0, 1), ("S", "r", 4), ("S", "2", 0, 2), ("W", "d", 2), ("W", "f", 2), ("E", 2), ("D", "d", 3),
-    ("D", "f", 3), ("S", "d", 4), ("D", "2", 1, 0), ("D", "1h", 0), ("W", "2", 1, 0), ("S", "2h", 1, 0),
-    ("W", "1", 1), ("S", "2", 1, 1), ("D", "1", 1), ("D", "2h", 0, 0), ("S", "1h", 1), ("S", "2", 1, 2),
-    ("W", "1h", 0), ("S", "2", 0, 3), ("S", "2", 2, 0), ("D", "2h", 1, 0), ("S", "3", 2, 0), ("W", "d", 3),
-    ("W", "f", 3), ("E", 3), ("D", "r", 4), ("W", "r", 4), ("S", "f", 4), ("S", "2", 3, 0), ("D", "2", 0, 1),
-    ("D", "2", 0, 2), ("S", "3", 3, 0), ("D", "1h", 1), ("W", "2", 0, 1), ("S", "2h", 0, 1), ("D", "d", 4),
-    ("S", "r", 5), ("W", "2", 0, 2), ("S", "2h", 0, 2), ("D", "2", 1, 1), ("W", "1h", 1), ("S", "2", 1, 3),
-    ("S", "d", 5), ("D", "f", 4), ("S", "1", 2), ("S", "1", 3), ("D", "2", 1, 2), ("W", "2", 1, 1), ("S", "2h", 1, 1),
-    ("W", "d", 4), ("W", "f", 4), ("E", 4), ("D", "3", 2, 0), ("D", "2", 3, 0), ("D", "2h", 1, 1), ("W", "2", 1, 2),
-    ("S", "2h", 1, 2), ("D", "2h", 0, 1), ("D", "2", 0, 3), ("D", "2", 2, 0), ("D", "2h", 0, 2), ("D", "3", 3, 0),
-    ("S", "1", 4), ("W", "2", 0, 3), ("S", "2h", 0, 3), ("D", "2", 1, 3), ("D", "2h", 1, 2), ("W", "2", 3, 0),
-    ("S", "2h", 3, 0), ("W", "2", 2, 0), ("S", "2h", 2, 0), ("W", "2", 1, 3), ("S", "2h", 1, 3), ("S", "3", 4, 0),
-    ("C", "tk", 0), ("D", "r", 5), ("D", "1", 2), ("D", "1", 3), ("W", "r", 5), ("S", "f", 5), ("S", "2", 4, 0),
-    ("C", "tk", 1), ("D", "2h", 0, 3), ("W", "1", 2), ("S", "2", 2, 1), ("D", "2h", 3, 0), ("D", "2h", 1, 3),
-    ("W", "1", 3), ("S", "2", 3, 1), ("D", "2h", 2, 0), ("S", "2", 2, 2), ("S", "2", 3, 2), ("D", "d", 5),
-    ("S", "1h", 2), ("S", "1h", 3), ("C", "tk", 2), ("S", "3", 3, 1), ("S", "3", 2, 1), ("S", "3", 0, 0),
-    ("S", "3", 3, 2), ("C", "tk", 3), ("S", "3", 2, 2), ("D", "f", 5), ("D", "1h", 2), ("D", "1h", 3),
-    ("S", "3", 1, 0), ("W", "d", 5), ("W", "f", 5), ("E", 5), ("D", "1", 4), ("D", "2", 2, 1), ("D", "2", 2, 2),
-    ("W", "1", 4), ("S", "1h", 4), ("D", "2", 3, 1), ("D", "3", 4, 0), ("D", "2", 3, 2), ("S", "1", 5),
-    ("S", "2", 4, 1), ("D", "3", 3, 1), ("D", "3", 3, 2), ("W", "2", 2, 1), ("S", "2h", 2, 1), ("W", "2", 2, 2),
-    ("S", "2h", 2, 2), ("W", "1h", 2), ("S", "2", 2, 3), ("D", "3", 2, 1), ("D", "3", 2, 2), ("W", "2", 3, 1),
-    ("S", "2h", 3, 1), ("D", "3", 0, 0), ("D", "2", 4, 0), ("D", "3", 1, 0), ("S", "2", 4, 2), ("W", "2", 3, 2),
-    ("S", "2h", 3, 2), ("W", "1h", 3), ("S", "2", 3, 3), ("W", "2", 4, 0), ("S", "2h", 4, 0), ("D", "1h", 4),
-    ("S", "3", 5, 0), ("C", "tk", 4), ("S", "2", 5, 0), ("C", "tk", 5), ("D", "2h", 3, 1), ("S", "3", 4, 1),
-    ("D", "2h", 2, 1), ("D", "2h", 2, 2), ("S", "3", 3, 3), ("C", "tk", 6), ("W", "1h", 4), ("S", "2", 4, 3),
-    ("D", "2", 2, 3), ("W", "2", 2, 3), ("S", "2h", 2, 3), ("D", "2h", 3, 2), ("S", "3", 4, 2), ("C", "tk", 7),
-    ("D", "1", 5), ("D", "2", 3, 3), ("W", "1", 5), ("S", "1h", 5), ("W", "2", 3, 3), ("S", "2h", 3, 3),
-    ("D", "3", 3, 3), ("D", "2h", 2, 3), ("S", "3", 3, 4), ("D", "2h", 4, 0), ("D", "2", 4, 1), ("S", "2", 5, 1),
-    ("S", "3", 2, 3), ("W", "2", 4, 1), ("S", "2h", 4, 1), ("D", "3", 5, 0), ("W", "3", 3, 0), ("W", "3", 3, 1),
-    ("W", "3", 3, 2), ("W", "3", 3, 3), ("S", "3h", 3, 0), ("D", "2h", 3, 3), ("W", "2h", 4, 0), ("S", "3", 4, 3),
-    ("D", "2", 4, 2), ("S", "2", 5, 2), ("S", "3", 3, 5), ("D", "3", 4, 1), ("D", "1h", 5), ("S", "3", 2, 4),
-    ("D", "2", 5, 0), ("W", "2", 4, 2), ("S", "2h", 4, 2), ("W", "2", 5, 0), ("S", "2h", 5, 0), ("W", "1h", 5),
-    ("S", "2", 5, 3), ("C", "sq", 0), ("C", "sq", 1), ("D", "3", 3, 4), ("D", "3h", 3, 0), ("S", "3", 5, 1),
-    ("D", "3", 4, 2), ("D", "3", 2, 3), ("D", "3", 4, 3), ("W", "2h", 4, 1), ("S", "3", 4, 4), ("D", "2h", 4, 1),
-    ("D", "2", 4, 3), ("W", "2", 4, 3), ("S", "2h", 4, 3), ("W", "3", 2, 0), ("W", "3", 2, 1), ("W", "3", 2, 2),
-    ("W", "3", 2, 3), ("W", "3", 4, 0), ("W", "3", 4, 1), ("W", "3", 4, 2), ("W", "3", 4, 3),
-    ("C", "mm", 1, 0, "near"), ("D", "2", 5, 1), ("D", "2h", 4, 2), ("D", "2h", 5, 0), ("W", "2", 5, 1),
-    ("S", "2h", 5, 1), ("D", "3", 3, 5), ("D", "3", 5, 1), ("S", "3", 5, 2), ("C", "sq", 2), ("D", "2", 5, 2),
-    ("S", "3", 0, 1), ("W", "2h", 5, 0), ("S", "3", 5, 3), ("D", "2h", 4, 3), ("W", "2", 5, 2), ("S", "2h", 5, 2),
-    ("S", "3", 1, 1), ("W", "3", 3, 4), ("S", "3h", 3, 1), ("D", "2", 5, 3), ("S", "3", 0, 2), ("D", "2h", 5, 1),
-    ("W", "2", 5, 3), ("S", "2h", 5, 3), ("D", "3", 5, 2), ("W", "2h", 5, 1), ("S", "3", 5, 4), ("D", "3", 2, 4),
-    ("S", "3h", 2, 0), ("D", "3", 0, 1), ("S", "3", 1, 2), ("D", "2h", 5, 2), ("S", "3", 0, 3), ("S", "3h", 4, 0),
-    ("S", "3", 1, 3), ("W", "3", 5, 0), ("W", "3", 5, 1), ("W", "3", 5, 2), ("W", "3", 5, 3),
-    ("C", "mm", 2, 0, "near"), ("D", "3", 1, 1), ("D", "3", 0, 2), ("D", "2h", 5, 3), ("S", "3", 0, 4),
-    ("W", "3", 2, 4), ("W", "3", 4, 4), ("C", "mm", 1, 1, "near"), ("D", "3", 4, 4), ("D", "3h", 2, 0),
-    ("S", "3", 2, 5), ("D", "3", 1, 2), ("D", "3", 0, 3), ("D", "3", 1, 3), ("S", "3", 1, 4), ("D", "3", 5, 3),
-    ("D", "3h", 3, 1), ("S", "3h", 5, 0), ("W", "3h", 2, 0), ("W", "3h", 4, 0), ("C", "mm", 1, 0, "far"),
-    ("D", "3h", 4, 0), ("W", "2h", 4, 2), ("S", "3", 4, 5), ("D", "3", 0, 4), ("W", "3", 0, 0), ("W", "3", 0, 1),
-    ("W", "3", 0, 2), ("W", "3", 0, 3), ("S", "3h", 0, 0), ("D", "3", 5, 4), ("W", "2h", 5, 2), ("S", "3", 5, 5),
-    ("W", "3", 5, 4), ("C", "mm", 2, 1, "near"), ("W", "3", 1, 0), ("W", "3", 1, 1), ("W", "3", 1, 2),
-    ("W", "3", 1, 3), ("S", "3h", 1, 0), ("D", "3", 1, 4), ("S", "3", 0, 5), ("W", "3h", 3, 0), ("W", "3h", 5, 0),
-    ("C", "mm", 2, 0, "far"), ("D", "3", 2, 5), ("S", "3h", 2, 1), ("D", "3h", 0, 0), ("D", "3h", 1, 0),
-    ("S", "3", 1, 5), ("D", "3h", 5, 0), ("S", "3h", 5, 1), ("S", "3h", 4, 1), ("W", "3h", 0, 0), ("W", "3h", 1, 0),
-    ("C", "mm", 0, 0, "all"), ("W", "3", 2, 5), ("W", "3", 4, 5), ("C", "mm", 1, 2, "near"), ("D", "3", 0, 5),
-    ("W", "3", 0, 4), ("S", "3h", 0, 1), ("D", "3", 5, 5), ("W", "2h", 3, 0), ("W", "2h", 3, 1), ("W", "2h", 3, 2),
-    ("W", "2h", 3, 3), ("S", "3", 3, 6), ("D", "3", 4, 5), ("D", "3h", 2, 1), ("W", "2h", 2, 0), ("W", "2h", 2, 1),
-    ("W", "2h", 2, 2), ("W", "2h", 2, 3), ("S", "3", 2, 6), ("W", "3", 1, 4), ("S", "3h", 1, 1), ("W", "3", 3, 5),
-    ("W", "3", 5, 5), ("C", "mm", 2, 2, "near"), ("D", "3", 1, 5), ("W", "2h", 0, 0), ("W", "2h", 0, 1),
-    ("W", "2h", 0, 2), ("W", "2h", 0, 3), ("S", "3", 0, 6), ("D", "3h", 5, 1), ("W", "2h", 5, 3), ("S", "3", 5, 6),
-    ("D", "3h", 4, 1), ("W", "2h", 4, 3), ("S", "3", 4, 6), ("W", "3h", 2, 1), ("W", "3h", 4, 1),
-    ("C", "mm", 1, 1, "far"), ("W", "3h", 3, 1), ("W", "3h", 5, 1), ("C", "mm", 2, 1, "far"), ("W", "3h", 0, 1),
-    ("W", "3h", 1, 1), ("C", "mm", 0, 1, "all"), ("D", "3h", 0, 1), ("D", "3h", 1, 1), ("W", "2h", 1, 0),
-    ("W", "2h", 1, 1), ("W", "2h", 1, 2), ("W", "2h", 1, 3), ("S", "3", 1, 6), ("D", "3", 0, 6), ("W", "3", 0, 5),
-    ("S", "3h", 0, 2), ("D", "3", 3, 6), ("S", "3h", 3, 2), ("D", "3", 2, 6), ("S", "3h", 2, 2), ("W", "3", 1, 5),
-    ("S", "3h", 1, 2), ("S", "3h", 5, 2), ("S", "3h", 4, 2), ("D", "3", 1, 6), ("W", "3", 0, 6), ("S", "3h", 0, 3),
-    ("W", "3", 2, 6), ("W", "3", 4, 6), ("C", "mm", 1, 3, "near"), ("D", "3h", 0, 2), ("W", "3", 1, 6),
-    ("S", "3h", 1, 3), ("D", "3", 5, 6), ("D", "3h", 3, 2), ("W", "3", 3, 6), ("S", "3h", 3, 3), ("D", "3", 4, 6),
-    ("D", "3h", 2, 2), ("S", "3h", 2, 3), ("W", "3", 5, 6), ("C", "mm", 2, 3, "near"), ("D", "3h", 5, 2),
-    ("S", "3h", 5, 3), ("D", "3h", 4, 2), ("S", "3h", 4, 3), ("W", "3h", 0, 2), ("W", "3h", 1, 2),
-    ("C", "mm", 0, 2, "all"), ("W", "3h", 0, 3), ("W", "3h", 1, 3), ("C", "mm", 0, 3, "all"), ("W", "3h", 2, 2),
-    ("W", "3h", 4, 2), ("C", "mm", 1, 2, "far"), ("W", "3h", 2, 3), ("W", "3h", 4, 3), ("C", "mm", 1, 3, "far"),
-    ("W", "3h", 3, 2), ("W", "3h", 5, 2), ("C", "mm", 2, 2, "far"), ("W", "3h", 3, 3), ("W", "3h", 5, 3),
-    ("C", "mm", 2, 3, "far"), ("C", "fin", 1), ("C", "fin", 2), ("C", "fin", 0),
+    ("S", "r", 0), ("S", "d", 0), ("S", "r", 1), ("S", "d", 1), ("W", "r", 0), ("S", "f", 0), ("S", "r", 2),
+    ("W", "r", 1), ("S", "f", 1), ("S", "d", 2), ("S", "r", 3), ("W", "d", 0), ("W", "f", 0), ("E", 0), ("S", "1", 0),
+    ("S", "2", 0, 0), ("D", "r", 0), ("W", "r", 2), ("S", "f", 2), ("S", "d", 3), ("W", "d", 1), ("W", "f", 1),
+    ("E", 1), ("S", "2", 1, 0), ("S", "1", 1), ("D", "d", 0), ("D", "r", 1), ("W", "r", 3), ("S", "f", 3),
+    ("S", "r", 4), ("W", "1", 0), ("S", "1h", 0), ("W", "2", 0, 0), ("S", "2h", 0, 0), ("S", "2", 0, 1),
+    ("S", "2", 0, 2), ("D", "d", 1), ("D", "f", 0), ("S", "d", 4), ("W", "d", 2), ("W", "f", 2), ("E", 2),
+    ("W", "2", 1, 0), ("S", "2h", 1, 0), ("W", "1", 1), ("S", "2", 1, 1), ("S", "1h", 1), ("S", "2", 1, 2),
+    ("W", "1h", 0), ("S", "2", 0, 3), ("S", "2", 2, 0), ("D", "r", 2), ("D", "f", 1), ("D", "d", 2), ("D", "r", 3),
+    ("W", "r", 4), ("S", "f", 4), ("S", "3", 2, 0), ("W", "d", 3), ("W", "f", 3), ("E", 3), ("S", "r", 5),
+    ("D", "1", 0), ("S", "2", 3, 0), ("D", "2", 0, 0), ("S", "3", 3, 0), ("D", "f", 2), ("S", "d", 5), ("D", "d", 3),
+    ("S", "1", 2), ("W", "2", 0, 1), ("S", "2h", 0, 1), ("W", "2", 0, 2), ("S", "2h", 0, 2), ("W", "1h", 1),
+    ("S", "2", 1, 3), ("D", "f", 3), ("S", "1", 3), ("D", "2", 1, 0), ("W", "2", 1, 1), ("S", "2h", 1, 1),
+    ("W", "d", 4), ("W", "f", 4), ("E", 4), ("D", "1", 1), ("D", "2h", 0, 0), ("S", "1", 4), ("D", "1h", 0),
+    ("W", "2", 1, 2), ("S", "2h", 1, 2), ("W", "2", 0, 3), ("S", "2h", 0, 3), ("W", "2", 2, 0), ("S", "2h", 2, 0),
+    ("D", "2h", 1, 0), ("S", "3", 4, 0), ("C", "tk", 0), ("W", "2", 3, 0), ("S", "2h", 3, 0), ("D", "r", 4),
+    ("D", "d", 4), ("W", "r", 5), ("S", "f", 5), ("S", "2", 4, 0), ("W", "2", 1, 3), ("S", "2h", 1, 3),
+    ("D", "2", 0, 1), ("D", "2", 0, 2), ("D", "1h", 1), ("W", "1", 2), ("S", "2", 2, 1), ("S", "2", 2, 2),
+    ("D", "2", 1, 1), ("W", "1", 3), ("S", "2", 3, 1), ("D", "f", 4), ("S", "1h", 2), ("S", "2", 3, 2),
+    ("S", "1h", 3), ("C", "tk", 1), ("C", "tk", 2), ("S", "3", 3, 1), ("D", "r", 5), ("S", "3", 0, 0),
+    ("D", "2", 1, 2), ("D", "3", 2, 0), ("S", "3", 2, 1), ("D", "2", 0, 3), ("D", "2", 2, 0), ("S", "3", 3, 2),
+    ("S", "3", 1, 0), ("D", "2", 3, 0), ("D", "2h", 1, 1), ("S", "3", 2, 2), ("C", "tk", 3), ("D", "2h", 0, 1),
+    ("D", "2h", 0, 2), ("D", "3", 3, 0), ("W", "1h", 2), ("S", "2", 2, 3), ("W", "d", 5), ("W", "f", 5), ("E", 5),
+    ("D", "1", 2), ("D", "1", 3), ("W", "1", 4), ("S", "2", 4, 1), ("D", "2", 1, 3), ("D", "2h", 1, 2),
+    ("D", "2h", 3, 0), ("S", "1", 5), ("D", "2h", 0, 3), ("D", "2h", 2, 0), ("S", "1h", 4), ("W", "2", 2, 1),
+    ("S", "2h", 2, 1), ("W", "2", 2, 2), ("S", "2h", 2, 2), ("D", "d", 5), ("S", "2", 4, 2), ("D", "2h", 1, 3),
+    ("W", "2", 3, 1), ("S", "2h", 3, 1), ("W", "2", 3, 2), ("S", "2h", 3, 2), ("W", "1h", 3), ("S", "2", 3, 3),
+    ("W", "2", 4, 0), ("S", "2h", 4, 0), ("S", "3", 5, 0), ("S", "2", 5, 0), ("W", "2", 2, 3), ("S", "2h", 2, 3),
+    ("C", "tk", 4), ("C", "tk", 5), ("S", "3", 4, 1), ("D", "2", 2, 1), ("D", "1", 4), ("S", "3", 3, 3),
+    ("C", "tk", 6), ("D", "1h", 2), ("D", "f", 5), ("D", "1h", 3), ("W", "1h", 4), ("S", "2", 4, 3), ("D", "2", 3, 1),
+    ("D", "2", 3, 2), ("D", "3", 4, 0), ("S", "3", 4, 2), ("C", "tk", 7), ("D", "3", 2, 1), ("D", "3", 2, 2),
+    ("W", "2", 3, 3), ("S", "2h", 3, 3), ("W", "1", 5), ("S", "1h", 5), ("D", "3", 0, 0), ("D", "2", 4, 0),
+    ("D", "3", 1, 0), ("S", "2", 5, 1), ("D", "2", 2, 2), ("D", "3", 3, 1), ("D", "3", 3, 2), ("D", "2", 2, 3),
+    ("S", "3", 3, 4), ("W", "2", 4, 1), ("S", "2h", 4, 1), ("D", "2h", 3, 1), ("S", "3", 2, 3), ("S", "2", 5, 2),
+    ("D", "2h", 3, 2), ("W", "2h", 4, 0), ("S", "3", 4, 3), ("D", "2h", 2, 1), ("D", "2h", 2, 2), ("D", "1h", 4),
+    ("D", "2h", 2, 3), ("W", "3", 3, 0), ("W", "3", 3, 1), ("W", "3", 3, 2), ("W", "3", 3, 3), ("S", "3h", 3, 0),
+    ("D", "2", 4, 1), ("D", "2h", 4, 0), ("W", "2", 4, 2), ("S", "2h", 4, 2), ("D", "2", 3, 3), ("D", "1", 5),
+    ("S", "3", 2, 4), ("D", "3", 3, 3), ("D", "3", 5, 0), ("W", "2", 5, 0), ("S", "3", 5, 1), ("S", "2h", 5, 0),
+    ("D", "2", 4, 2), ("W", "1h", 5), ("S", "2", 5, 3), ("S", "3", 5, 2), ("C", "sq", 0), ("D", "2", 5, 0),
+    ("W", "2", 4, 3), ("S", "2h", 4, 3), ("D", "2h", 3, 3), ("D", "3", 4, 1), ("D", "1h", 5), ("W", "2h", 4, 1),
+    ("S", "3", 4, 4), ("S", "3", 3, 5), ("W", "3", 2, 0), ("W", "3", 2, 1), ("W", "3", 2, 2), ("W", "3", 2, 3),
+    ("W", "3", 4, 0), ("W", "3", 4, 1), ("W", "3", 4, 2), ("W", "3", 4, 3), ("C", "mm", 1, 0, "near"),
+    ("D", "2h", 4, 1), ("D", "2", 4, 3), ("W", "2", 5, 1), ("S", "2h", 5, 1), ("S", "3", 0, 1), ("C", "sq", 1),
+    ("W", "2", 5, 2), ("S", "2h", 5, 2), ("D", "3", 3, 4), ("D", "3h", 3, 0), ("W", "2h", 5, 0), ("S", "3", 5, 3),
+    ("C", "sq", 2), ("S", "3", 1, 1), ("W", "3", 3, 4), ("S", "3h", 3, 1), ("D", "2", 5, 1), ("D", "2h", 4, 2),
+    ("S", "3", 0, 2), ("W", "2", 5, 3), ("S", "2h", 5, 3), ("D", "3", 4, 2), ("D", "3", 2, 3), ("D", "3", 4, 3),
+    ("D", "3", 2, 4), ("S", "3h", 2, 0), ("D", "3", 5, 1), ("D", "3", 5, 2), ("W", "2h", 5, 1), ("S", "3", 5, 4),
+    ("D", "2h", 5, 0), ("D", "2", 5, 2), ("S", "3", 1, 2), ("D", "2h", 4, 3), ("S", "3", 0, 3), ("S", "3h", 4, 0),
+    ("S", "3", 1, 3), ("D", "2", 5, 3), ("S", "3", 0, 4), ("W", "3", 5, 0), ("W", "3", 5, 1), ("W", "3", 5, 2),
+    ("W", "3", 5, 3), ("C", "mm", 2, 0, "near"), ("W", "3", 2, 4), ("W", "3", 4, 4), ("C", "mm", 1, 1, "near"),
+    ("S", "3", 2, 5), ("D", "2h", 5, 1), ("D", "3", 0, 1), ("D", "2h", 5, 2), ("S", "3", 1, 4), ("D", "3", 3, 5),
+    ("D", "3", 5, 3), ("D", "3h", 3, 1), ("S", "3h", 5, 0), ("W", "3h", 2, 0), ("W", "3h", 4, 0),
+    ("C", "mm", 1, 0, "far"), ("D", "3", 4, 4), ("D", "3h", 2, 0), ("W", "2h", 4, 2), ("S", "3", 4, 5),
+    ("D", "3", 1, 1), ("D", "3", 0, 2), ("D", "2h", 5, 3), ("D", "3", 1, 2), ("D", "3", 0, 3), ("D", "3", 1, 3),
+    ("W", "3", 0, 0), ("W", "3", 0, 1), ("W", "3", 0, 2), ("W", "3", 0, 3), ("S", "3h", 0, 0), ("W", "2h", 5, 2),
+    ("S", "3", 5, 5), ("W", "3", 5, 4), ("C", "mm", 2, 1, "near"), ("W", "3", 1, 0), ("W", "3", 1, 1),
+    ("W", "3", 1, 2), ("W", "3", 1, 3), ("S", "3h", 1, 0), ("S", "3", 0, 5), ("W", "3h", 3, 0), ("W", "3h", 5, 0),
+    ("C", "mm", 2, 0, "far"), ("D", "3h", 4, 0), ("S", "3h", 2, 1), ("D", "3", 0, 4), ("S", "3", 1, 5),
+    ("W", "3h", 0, 0), ("W", "3h", 1, 0), ("C", "mm", 0, 0, "all"), ("D", "3", 2, 5), ("S", "3h", 4, 1),
+    ("D", "3", 5, 4), ("D", "3h", 5, 0), ("S", "3h", 5, 1), ("D", "3", 1, 4), ("D", "3h", 0, 0), ("W", "3", 0, 4),
+    ("S", "3h", 0, 1), ("W", "3", 2, 5), ("W", "3", 4, 5), ("C", "mm", 1, 2, "near"), ("W", "2h", 2, 0),
+    ("W", "2h", 2, 1), ("W", "2h", 2, 2), ("W", "2h", 2, 3), ("S", "3", 2, 6), ("W", "2h", 3, 0), ("W", "2h", 3, 1),
+    ("W", "2h", 3, 2), ("W", "2h", 3, 3), ("S", "3", 3, 6), ("D", "3h", 1, 0), ("W", "3", 1, 4), ("S", "3h", 1, 1),
+    ("W", "3", 3, 5), ("W", "3", 5, 5), ("C", "mm", 2, 2, "near"), ("D", "3", 0, 5), ("W", "2h", 0, 0),
+    ("W", "2h", 0, 1), ("W", "2h", 0, 2), ("W", "2h", 0, 3), ("S", "3", 0, 6), ("D", "3", 4, 5), ("D", "3h", 2, 1),
+    ("W", "2h", 4, 3), ("S", "3", 4, 6), ("D", "3", 5, 5), ("W", "2h", 5, 3), ("S", "3", 5, 6), ("W", "3h", 2, 1),
+    ("W", "3h", 4, 1), ("C", "mm", 1, 1, "far"), ("W", "3h", 3, 1), ("W", "3h", 5, 1), ("C", "mm", 2, 1, "far"),
+    ("W", "3h", 0, 1), ("W", "3h", 1, 1), ("C", "mm", 0, 1, "all"), ("D", "3h", 0, 1), ("W", "2h", 1, 0),
+    ("W", "2h", 1, 1), ("W", "2h", 1, 2), ("W", "2h", 1, 3), ("S", "3", 1, 6), ("D", "3", 1, 5), ("D", "3h", 1, 1),
+    ("W", "3", 0, 5), ("S", "3h", 0, 2), ("D", "3h", 4, 1), ("D", "3", 2, 6), ("S", "3h", 2, 2), ("D", "3h", 5, 1),
+    ("D", "3", 3, 6), ("S", "3h", 3, 2), ("W", "3", 1, 5), ("S", "3h", 1, 2), ("S", "3h", 4, 2), ("S", "3h", 5, 2),
+    ("D", "3", 0, 6), ("W", "3", 0, 6), ("S", "3h", 0, 3), ("W", "3", 1, 6), ("S", "3h", 1, 3), ("W", "3", 2, 6),
+    ("S", "3h", 2, 3), ("W", "3", 3, 6), ("S", "3h", 3, 3), ("W", "3", 4, 6), ("C", "mm", 1, 3, "near"),
+    ("S", "3h", 4, 3), ("W", "3", 5, 6), ("S", "3h", 5, 3), ("C", "mm", 2, 3, "near"), ("W", "3h", 0, 2),
+    ("W", "3h", 1, 2), ("C", "mm", 0, 2, "all"), ("W", "3h", 0, 3), ("W", "3h", 1, 3), ("C", "mm", 0, 3, "all"),
+    ("W", "3h", 2, 2), ("W", "3h", 4, 2), ("C", "mm", 1, 2, "far"), ("W", "3h", 2, 3), ("W", "3h", 4, 3),
+    ("C", "mm", 1, 3, "far"), ("W", "3h", 3, 2), ("W", "3h", 5, 2), ("C", "mm", 2, 2, "far"), ("W", "3h", 3, 3),
+    ("W", "3h", 5, 3), ("C", "mm", 2, 3, "far"), ("C", "fin", 1), ("C", "fin", 2), ("C", "fin", 0),
 )
 
 THRESH = ((0.25, 0.5), (0.75, 1.0), (1.25, 1.5), (1.75, 2.0), (2.5, 3.0), (3.5, 4.0), (5.0, 6.0))
+
+
+class Message:
+    def __init__(self, whole, copies):
+        self.copies = copies
+        self.wait_recv, self.wait_send = whole.wait_recv, whole.wait_send
+
+    def start(self):
+        for copy in self.copies:
+            copy.start()
 
 
 def mod4(v):
@@ -281,7 +289,17 @@
         if not isinstance(r0, int):
             r0 = pl.multiple_of(r0, 96)
         c, lo, width, _ = PARTS[p]
-        return W[c].at[ys, xs, pl.ds(r0, n), pl.ds(lo, width)]
+        cc = pl.ds(lo, width)
+        if isinstance(ys, slice) or isinstance(xs, slice):
+            pieces = [(t, xs) if isinstance(ys, slice) else (ys, t) for t in range(4)]
+            pieces = [W[c].at[yy, xx, pl.ds(r0, n), cc] for yy, xx in pieces]
+        else:
+            step = n // 4 if n > ROWS else n // 2
+            starts = [r0 + t * step for t in range(n // step)]
+            if not isinstance(r0, int):
+                starts = [pl.multiple_of(t, SLAB) for t in starts]
+            pieces = [W[c].at[ys, xs, pl.ds(t, step), cc] for t in starts]
+        return W[c].at[ys, xs, pl.ds(r0, n), cc], pieces
 
     M = {}
     OFF = (0, 1, -1, 2)
@@ -290,8 +308,9 @@
     def both(*pair):
         out = []
         for j, s in enumerate((1, -1)):
-            axis, ref = pair[j]
-            out.append(remote(ref, ref, g_snd.at[used[0]], g_rcv.at[used[0]], nbr(axis, s)))
+            axis, (ref, pieces) = pair[j]
+            sems = g_snd.at[used[0]], g_rcv.at[used[0]], nbr(axis, s)
+            out.append(Message(remote(ref, ref, *sems), [remote(r, r, *sems) for r in pieces]))
             used[0] += 1
         return out
 
@@ -400,7 +419,6 @@
     s_cp = remote(ss.at[mine, :], ss.at[mine, :], t_snd.at[8], t_rcv.at[8], other)
     outs = []
     left = []
-    late = []
     seen = set()
 
     def once(name):
@@ -424,14 +442,9 @@
             for m in M[key]:
                 m.wait_recv()
         elif kind == "D":
-
-            @pl.when(core == 1)
-            def _():
-                for m in M[key]:
-                    m.wait_send()
-
+            for m in M[key]:
+                m.wait_send()
             left.remove(key)
-            late.append(key)
         elif kind == "E":
             encode(*key)
             left_to_encode = len(PARTS) - 1 - key[0]
@@ -462,12 +475,6 @@
     for key in left:
         for m in M[key]:
             m.wait_send()
-
-    @pl.when(core == 0)
-    def _():
-        for key in late:
-            for m in M[key]:
-                m.wait_send()
 
     for p in pending:
         p.wait_send()

time: 139 us -> 138 us (level)
  no operation moved by 1% of the time
where the time goes in v7:
time: 138 us
  Pallas kernels  137 us (99%)
    pallas_call x1, Pallas kernels, body(): pl.pallas_call(kernel, out_shape=(jax.ShapeDtypeStruct((ROWS, KVW), F32),...  133 us
    pallas_call x1, Pallas kernels, body(): pl.pallas_call(write_kernel, out_shape=(jax.ShapeDtypeStruct((ROWS, KVW),...  3.61 us

profile of v7, /device:TPU:0, one launch (start us, length us, event | category | flops | bytes accessed | tf_op | source)
XLA Modules:
  0.0 137.7 jit_solution(14266844105066716039)
XLA Ops:
  0.6 133.4 %shard_map.85 = (f32[192,1024]{1,0:T(8,128)}, bf16[768,1024]{1,0:T(8,128)(2,1)}) custom-call(bf16[384,12288]{1,0:T(8,128)(2,1)} %tokens.1, bf16[96,128]{1,0:T(8,128)(2,1)} %bitcast.7, bf16[4,192,1024]{2,1,0:T(8,128)(2,1)} %bitcast.5, s32[32,768]{1,0:T(8,128)} %bitcast.6, f32[192,1024]{1,0:T(8,128)} %base.3, f32[192,1024]{1,0:T(8,128)} %mom.3), custom_call_target="tpu_custom_call" | custom-call | flops 19327352832 | bytes 30000000 | tf_op jit(solution)/shard_map/pallas_call | solution.py:521
  134.1 3.6 %shard_map.86 = (f32[192,1024]{1,0:T(8,128)}, f32[192,1024]{1,0:T(8,128)}, bf16[768,1024]{1,0:T(8,128)(2,1)}) custom-call(f32[192,1024]{1,0:T(8,128)} %get-tuple-element.5.grad, f32[192,1024]{1,0:T(8,128)} %base.3, f32[192,1024]{1,0:T(8,128)} %mom.3, bf16[768,1024]{1,0:T(8,128)(2,1)} %get-tuple-element.6.kv), custom_call_target="tpu_custom_call" | custom-call | flops 1179648 | bytes 7000000 | tf_op jit(solution)/shard_map/pallas_call | solution.py:573

commit v8 on v6

v8 whole, which is shorter than its diff:
```python
import jax
import jax.numpy as jnp
from jax import lax
from jax.experimental import pallas as pl
from jax.experimental.pallas import tpu as pltpu
from jax.sharding import PartitionSpec as P

MESH = pl.DeviceIdType.MESH
F32, BF16 = jnp.float32, jnp.bfloat16
D, KVW, BLOCK, TOK = 12288, 1024, 32, 384
ROWS = 192
FROWS = 768
SLAB = 48
OUTER_RATE = 0.7
MOMENTUM_COEF = 0.9
CLS = ((0, 256), (256, 384), (640, 384))
PARTS = (
    (0, 128, 128, ("y", "x", "z")),
    (0, 0, 128, ("x", "y", "z")),
    (2, 0, 128, ("z", "x", "y")),
    (1, 0, 128, ("z", "y", "x")),
    (1, 128, 256, ("y", "z", "x")),
    (2, 128, 256, ("x", "z", "y")),
)

SCHEDULE = (
    ("S", "r", 0), ("S", "d", 0), ("S", "r", 1), ("S", "d", 1), ("S", "r", 2), ("W", "r", 0), ("S", "f", 0),
    ("S", "d", 2), ("W", "r", 1), ("S", "f", 1), ("S", "r", 3), ("S", "d", 3), ("W", "d", 0), ("W", "f", 0), ("E", 0),
    ("S", "2", 0, 0), ("S", "1", 0), ("D", "r", 0), ("W", "r", 2), ("S", "f", 2), ("D", "r", 1), ("S", "r", 4),
    ("W", "d", 1), ("W", "f", 1), ("E", 1), ("S", "1", 1), ("S", "2", 1, 0), ("D", "d", 0), ("W", "r", 3),
    ("S", "f", 3), ("S", "d", 4), ("W", "2", 0, 0), ("S", "2h", 0, 0), ("W", "1", 0), ("S", "1h", 0),
    ("S", "2", 0, 1), ("S", "2", 0, 2), ("W", "d", 2), ("W", "f", 2), ("E", 2), ("W", "1", 1), ("S", "2", 1, 1),
    ("D", "r", 2), ("D", "d", 1), ("D", "f", 0), ("D", "f", 1), ("W", "r", 4), ("S", "f", 4), ("W", "2", 1, 0),
    ("S", "2h", 1, 0), ("S", "1h", 1), ("D", "r", 3), ("D", "d", 2), ("S", "r", 5), ("S", "2", 1, 2), ("W", "1h", 0),
    ("S", "2", 0, 3), ("D", "d", 3), ("S", "d", 5), ("S", "2", 2, 0), ("S", "1", 2), ("S", "3", 2, 0), ("W", "d", 3),
    ("W", "f", 3), ("E", 3), ("D", "1", 0), ("S", "2", 3, 0), ("D", "2", 0, 0), ("W", "2", 0, 1), ("S", "2h", 0, 1),
    ("W", "2", 0, 2), ("S", "2h", 0, 2), ("W", "2", 1, 1), ("S", "2h", 1, 1), ("W", "1h", 1), ("S", "2", 1, 3),
    ("D", "f", 2), ("D", "r", 4), ("S", "1", 3), ("D", "1", 1), ("S", "3", 3, 0), ("W", "d", 4), ("W", "f", 4),
    ("E", 4), ("D", "2h", 0, 0), ("W", "2", 0, 3), ("S", "2h", 0, 3), ("D", "2", 1, 0), ("D", "1h", 0), ("S", "1", 4),
    ("W", "2", 2, 0), ("S", "2h", 2, 0), ("D", "f", 3), ("D", "d", 4), ("W", "r", 5), ("S", "f", 5), ("W", "1", 2),
    ("S", "2", 2, 1), ("S", "1h", 2), ("D", "2", 0, 1), ("D", "2", 0, 2), ("S", "2", 2, 2), ("S", "2", 4, 0),
    ("D", "2", 1, 1), ("D", "2h", 1, 0), ("W", "2", 1, 2), ("S", "2h", 1, 2), ("W", "2", 3, 0), ("S", "2h", 3, 0),
    ("D", "1h", 1), ("S", "3", 4, 0), ("W", "1", 3), ("S", "2", 3, 1), ("D", "f", 4), ("S", "1h", 3),
    ("W", "2", 1, 3), ("S", "2h", 1, 3), ("S", "2", 3, 2), ("S", "3", 0, 0), ("C", "tk", 0), ("S", "3", 3, 1),
    ("C", "tk", 1), ("D", "2", 0, 3), ("W", "1h", 2), ("S", "2", 2, 3), ("D", "r", 5), ("S", "3", 1, 0),
    ("D", "2", 1, 2), ("S", "3", 2, 1), ("W", "d", 5), ("W", "f", 5), ("E", 5), ("D", "1", 2), ("S", "2", 5, 0),
    ("D", "3", 2, 0), ("D", "2h", 1, 1), ("D", "2", 3, 0), ("W", "1h", 3), ("S", "2", 3, 3), ("D", "2", 2, 0),
    ("D", "2h", 0, 1), ("D", "2h", 0, 2), ("D", "3", 3, 0), ("D", "2h", 0, 3), ("S", "1", 5), ("W", "2", 2, 1),
    ("S", "2h", 2, 1), ("D", "2", 1, 3), ("W", "1", 4), ("S", "1h", 4), ("D", "1", 3), ("D", "d", 5),
    ("S", "2", 4, 1), ("D", "2h", 2, 0), ("W", "2", 2, 2), ("S", "2h", 2, 2), ("S", "2", 4, 2), ("S", "3", 5, 0),
    ("C", "tk", 2), ("C", "tk", 3), ("W", "2", 3, 1), ("S", "2h", 3, 1), ("S", "3", 3, 2), ("C", "tk", 4),
    ("W", "2", 3, 2), ("S", "2h", 3, 2), ("D", "2", 2, 1), ("W", "2", 2, 3), ("S", "2h", 2, 3), ("D", "1h", 2),
    ("D", "f", 5), ("W", "2", 4, 0), ("S", "2h", 4, 0), ("D", "2", 2, 2), ("S", "3", 4, 1), ("D", "2h", 1, 2),
    ("D", "2h", 3, 0), ("S", "3", 2, 2), ("C", "tk", 5), ("D", "1", 4), ("D", "2h", 1, 3), ("S", "3", 2, 3),
    ("W", "2", 3, 3), ("S", "2h", 3, 3), ("D", "3", 3, 1), ("S", "3", 4, 2), ("D", "1h", 3), ("D", "3", 0, 0),
    ("S", "3", 0, 1), ("W", "1h", 4), ("S", "2", 4, 3), ("D", "2", 3, 1), ("D", "2", 3, 2), ("S", "3", 2, 4),
    ("C", "tk", 6), ("D", "2", 2, 3), ("D", "3", 4, 0), ("S", "3", 3, 3), ("D", "2h", 2, 1), ("W", "1", 5),
    ("S", "1h", 5), ("D", "2", 4, 0), ("D", "3", 1, 0), ("W", "2", 5, 0), ("S", "2h", 5, 0), ("S", "2", 5, 1),
    ("S", "2", 5, 2), ("C", "tk", 7), ("D", "2h", 2, 2), ("W", "2h", 4, 0), ("S", "3", 4, 3), ("W", "2", 4, 1),
    ("S", "2h", 4, 1), ("D", "3", 2, 1), ("D", "2", 3, 3), ("D", "2h", 3, 1), ("D", "1h", 4), ("D", "2h", 3, 2),
    ("S", "3", 5, 1), ("W", "2", 4, 2), ("S", "2h", 4, 2), ("D", "2h", 2, 3), ("D", "3", 3, 2), ("S", "3", 3, 4),
    ("S", "3", 5, 2), ("C", "sq", 0), ("D", "2", 5, 0), ("D", "2h", 4, 0), ("D", "2", 4, 1), ("W", "1h", 5),
    ("S", "2", 5, 3), ("D", "2h", 3, 3), ("D", "3", 2, 2), ("D", "3", 2, 3), ("D", "3", 5, 0), ("S", "3", 2, 5),
    ("C", "sq", 1), ("D", "1", 5), ("D", "3", 4, 1), ("S", "3", 3, 5), ("C", "sq", 2), ("W", "3", 3, 0),
    ("W", "3", 3, 1), ("W", "3", 3, 2), ("W", "3", 3, 3), ("W", "3", 4, 0), ("W", "3", 4, 1), ("W", "3", 4, 2),
    ("W", "3", 4, 3), ("C", "mm", 1, 0, "near"), ("D", "2", 4, 2), ("D", "3", 0, 1), ("D", "2h", 5, 0),
    ("W", "2", 4, 3), ("S", "2h", 4, 3), ("W", "2h", 5, 0), ("S", "3", 5, 3), ("W", "2", 5, 1), ("S", "2h", 5, 1),
    ("W", "2", 5, 2), ("S", "2h", 5, 2), ("D", "3", 3, 3), ("D", "3", 4, 2), ("D", "1h", 5), ("D", "3", 4, 3),
    ("W", "2h", 4, 1), ("S", "3", 4, 4), ("D", "3", 2, 4), ("W", "2h", 2, 0), ("W", "2h", 2, 1), ("W", "2h", 2, 2),
    ("W", "2h", 2, 3), ("S", "3", 2, 6), ("W", "2", 5, 3), ("S", "2h", 5, 3), ("D", "2h", 4, 1), ("S", "3", 1, 1),
    ("D", "2h", 4, 2), ("D", "2", 4, 3), ("S", "3", 0, 2), ("S", "3", 1, 2), ("D", "3", 5, 1), ("D", "3", 5, 2),
    ("W", "3", 2, 0), ("W", "3", 2, 1), ("W", "3", 2, 2), ("W", "3", 2, 3), ("S", "3h", 2, 0), ("D", "2", 5, 1),
    ("D", "2", 5, 2), ("S", "3", 0, 3), ("D", "2", 5, 3), ("S", "3", 1, 3), ("W", "3", 5, 0), ("W", "3", 5, 1),
    ("W", "3", 5, 2), ("W", "3", 5, 3), ("C", "mm", 2, 0, "near"), ("D", "3", 2, 5), ("W", "2h", 5, 1),
    ("S", "3", 5, 4), ("D", "2h", 4, 3), ("S", "3", 0, 4), ("D", "3", 3, 4), ("D", "3", 3, 5), ("W", "2h", 4, 2),
    ("S", "3", 4, 5), ("D", "2h", 5, 1), ("D", "2h", 5, 2), ("S", "3", 1, 4), ("W", "3", 3, 4), ("W", "3", 4, 4),
    ("C", "mm", 1, 1, "near"), ("D", "3", 5, 3), ("D", "3", 2, 6), ("D", "3h", 2, 0), ("W", "2h", 5, 2),
    ("S", "3", 5, 5), ("D", "2h", 5, 3), ("D", "3", 1, 1), ("D", "3", 0, 2), ("D", "3", 1, 2), ("D", "3", 0, 3),
    ("D", "3", 1, 3), ("S", "3", 0, 5), ("W", "2h", 3, 0), ("W", "2h", 3, 1), ("W", "2h", 3, 2), ("W", "2h", 3, 3),
    ("S", "3", 3, 6), ("S", "3", 1, 5), ("D", "3", 4, 4), ("W", "2h", 4, 3), ("S", "3", 4, 6), ("W", "3", 2, 4),
    ("W", "3", 5, 4), ("C", "mm", 2, 1, "near"), ("W", "2h", 5, 3), ("S", "3", 5, 6), ("D", "3", 0, 4),
    ("W", "2h", 0, 0), ("W", "2h", 0, 1), ("W", "2h", 0, 2), ("W", "2h", 0, 3), ("S", "3", 0, 6), ("W", "3", 3, 5),
    ("W", "3", 4, 5), ("C", "mm", 1, 2, "near"), ("D", "3", 1, 4), ("W", "2h", 1, 0), ("W", "2h", 1, 1),
    ("W", "2h", 1, 2), ("W", "2h", 1, 3), ("S", "3", 1, 6), ("D", "3", 4, 5), ("S", "3h", 3, 0), ("W", "3", 2, 5),
    ("W", "3", 5, 5), ("C", "mm", 2, 2, "near"), ("D", "3", 3, 6), ("S", "3h", 4, 0), ("D", "3", 5, 4),
    ("S", "3h", 5, 0), ("D", "3", 0, 5), ("W", "3", 0, 0), ("W", "3", 0, 1), ("W", "3", 0, 2), ("W", "3", 0, 3),
    ("S", "3h", 0, 0), ("D", "3", 1, 5), ("W", "3", 1, 0), ("W", "3", 1, 1), ("W", "3", 1, 2), ("W", "3", 1, 3),
    ("S", "3h", 1, 0), ("S", "3h", 3, 1), ("D", "3", 5, 5), ("S", "3h", 2, 1), ("W", "3", 3, 6), ("W", "3", 4, 6),
    ("C", "mm", 1, 3, "near"), ("D", "3", 0, 6), ("W", "3", 0, 4), ("S", "3h", 0, 1), ("S", "3h", 4, 1),
    ("S", "3h", 5, 1), ("W", "3", 1, 4), ("S", "3h", 1, 1), ("W", "3", 2, 6), ("W", "3", 5, 6),
    ("C", "mm", 2, 3, "near"), ("W", "3", 0, 5), ("S", "3h", 0, 2), ("D", "3", 4, 6), ("D", "3h", 3, 0),
    ("S", "3h", 3, 2), ("W", "3h", 0, 0), ("W", "3h", 1, 0), ("C", "mm", 0, 0, "all"), ("W", "3h", 3, 0),
    ("W", "3h", 4, 0), ("C", "mm", 1, 0, "far"), ("D", "3", 5, 6), ("S", "3h", 2, 2), ("D", "3", 1, 6),
    ("D", "3h", 0, 0), ("W", "3", 1, 5), ("S", "3h", 1, 2), ("S", "3h", 4, 2), ("W", "3h", 2, 0), ("W", "3h", 5, 0),
    ("C", "mm", 2, 0, "far"), ("S", "3h", 5, 2), ("D", "3h", 1, 0), ("W", "3", 0, 6), ("S", "3h", 0, 3),
    ("W", "3h", 0, 1), ("W", "3h", 1, 1), ("C", "mm", 0, 1, "all"), ("W", "3", 1, 6), ("S", "3h", 1, 3),
    ("W", "3h", 2, 1), ("W", "3h", 5, 1), ("C", "mm", 2, 1, "far"), ("D", "3h", 4, 0), ("D", "3h", 3, 1),
    ("S", "3h", 3, 3), ("W", "3h", 3, 1), ("W", "3h", 4, 1), ("C", "mm", 1, 1, "far"), ("D", "3h", 2, 1),
    ("D", "3h", 5, 0), ("S", "3h", 2, 3), ("S", "3h", 4, 3), ("S", "3h", 5, 3), ("W", "3h", 0, 2), ("W", "3h", 1, 2),
    ("C", "mm", 0, 2, "all"), ("W", "3h", 0, 3), ("W", "3h", 1, 3), ("C", "mm", 0, 3, "all"), ("C", "fin", 0),
    ("W", "3h", 3, 2), ("W", "3h", 4, 2), ("C", "mm", 1, 2, "far"), ("W", "3h", 2, 2), ("W", "3h", 5, 2),
    ("C", "mm", 2, 2, "far"), ("W", "3h", 3, 3), ("W", "3h", 4, 3), ("C", "mm", 1, 3, "far"), ("C", "fin", 1),
    ("W", "3h", 2, 3), ("W", "3h", 5, 3), ("C", "mm", 2, 3, "far"), ("C", "fin", 2),
)

THRESH = ((0.25, 0.5), (0.75, 1.0), (1.25, 1.5), (1.75, 2.0), (2.5, 3.0), (3.5, 4.0), (5.0, 6.0))


def mod4(v):
    return lax.rem(v + 8, 4)


def kernel(
    tokens, gain, frag, exps, base, mom,
    nb, nm, kv,
    w0, w1, w2, tok, acc, fv, fb, rl, bs, ms, gb, gf, gn, ex, eb, er, erl, sc, iv, ss,
    loc, a_snd, a_rcv, e_snd, e_rcv, t_snd, t_rcv, g_snd, g_rcv,
):
    W = (w0, w1, w2)
    rep = lax.axis_index("replica")
    fs = lax.axis_index("fsdp")
    core = lax.axis_index("tensor")
    pos = {"x": lax.rem(fs, 4), "y": lax.div(fs, 4), "z": rep}

    def nbr(axis, step):
        c = dict(pos)
        c[axis] = mod4(pos[axis] + step)
        return (c["z"], c["y"] * 4 + c["x"], core)

    other = (rep, fs, 1 - core)

    def remote(src, dst, ss_, rs_, dev):
        return pltpu.make_async_remote_copy(
            src_ref=src, dst_ref=dst, send_sem=ss_, recv_sem=rs_, device_id=dev, device_id_type=MESH
        )

    pending = []

    def go(copy):
        copy.start()
        pending.append(copy)

    barrier = pltpu.get_barrier_semaphore()
    peers = [nbr(a, s) for a in "xyz" for s in (1, -1)] + [other]
    for p in peers:
        pl.semaphore_signal(barrier, inc=1, device_id=p, device_id_type=MESH)

    l_ex = pltpu.make_async_copy(exps, ex, loc.at[0])
    l_ex.start()
    l_fr = pltpu.make_async_copy(frag, fv, loc.at[1])
    l_fr.start()
    l_bs = pltpu.make_async_copy(base, bs, loc.at[2])
    l_bs.start()
    l_ms = pltpu.make_async_copy(mom, ms, loc.at[3])
    l_ms.start()
    l_gn = pltpu.make_async_copy(gain, gb, loc.at[4])
    l_gn.start()

    pl.semaphore_wait(barrier, len(peers))
    l_fr.wait()

    up, down = nbr("z", 1), nbr("z", -1)
    zu, zd, zo = mod4(rep + 1), mod4(rep - 1), mod4(rep + 2)

    def window(d):
        return eb.at[:, pl.ds(pl.multiple_of(128 * lax.div(3 * d, 2), 128), 256)]

    off = 64 * lax.rem(rep, 2)

    def expand(lo, width):
        j = lax.broadcasted_iota(jnp.int32, (BLOCK, width), 0)
        n = lax.broadcasted_iota(jnp.int32, (BLOCK, width), 1)
        pick = jnp.where(j == lax.div(n + lo, BLOCK), 1.0, 0.0).astype(BF16)
        for slot in range(4):
            e = (window(rep)[...] if slot == 0 else er[slot]).astype(F32)
            for ref, sign in ((sc, 1.0), (iv, -1.0)):
                small = jnp.exp2(sign * e).astype(BF16)
                full = lax.dot_general(small, pick, (((0,), (0,)), ((), ())), preferred_element_type=F32)
                ref[slot, :, pl.ds(lo, width)] = full.astype(BF16)

    e_cp = [
        remote(window(zo), erl, e_snd.at[0], e_rcv.at[0], up),
        remote(window(zu), er.at[1], e_snd.at[1], e_rcv.at[1], up),
        remote(window(zd), er.at[2], e_snd.at[2], e_rcv.at[2], down),
        remote(erl, er.at[3], e_snd.at[3], e_rcv.at[3], up),
    ]

    def cols(p):
        c, lo, width, _ = PARTS[p]
        return pl.ds(CLS[c][0] + lo, width)

    H = ROWS // 2

    def a2a(p):
        k = 6 * p
        cc = cols(p)
        return [
            remote(fv.at[zo, pl.ds(0, H), cc], rl.at[0, :, cc], a_snd.at[k], a_rcv.at[k], up),
            remote(fv.at[zo, pl.ds(H, H), cc], rl.at[1, :, cc], a_snd.at[k + 1], a_rcv.at[k + 1], down),
            remote(fv.at[zu, :, cc], fb.at[1, :, cc], a_snd.at[k + 2], a_rcv.at[k + 2], up),
            remote(fv.at[zd, :, cc], fb.at[2, :, cc], a_snd.at[k + 3], a_rcv.at[k + 3], down),
            remote(rl.at[0, :, cc], fb.at[3, pl.ds(0, H), cc], a_snd.at[k + 4], a_rcv.at[k + 4], up),
            remote(rl.at[1, :, cc], fb.at[3, pl.ds(H, H), cc], a_snd.at[k + 5], a_rcv.at[k + 5], down),
        ]

    mine = pl.ds(pl.multiple_of(core * TOK, TOK), TOK)
    t_cp, l_tk = [], []
    for i in range(8):
        src = tokens.at[pl.ds(i * SLAB, SLAB), :]
        dst = tok.at[pl.ds(pl.multiple_of(core * TOK + i * SLAB, SLAB), SLAB), :]
        t_cp.append(remote(src, dst, t_snd.at[i], t_rcv.at[i], other))
        l_tk.append(pltpu.make_async_copy(src, dst, loc.at[5 + i]))

    def early():
        l_ex.wait()
        eb[...] = ex[...].astype(F32).astype(BF16)
        for m in e_cp[:3]:
            go(m)
        l_gn.wait()
        gf[...] = gb[...].astype(F32)
        first = 6 * fs + lax.div(3 * rep, 2)
        i = lax.broadcasted_iota(jnp.int32, (128, 128), 0)
        l = lax.broadcasted_iota(jnp.int32, (128, 128), 1)
        for h in range(2):
            row = jnp.broadcast_to(gf[pl.ds(first + h, 1), :], (128, 128))
            column = jnp.sum(jnp.where(i == l, row, 0.0), axis=1, keepdims=True)
            gn[pl.ds(128 * h, 128), :] = jnp.broadcast_to(column, (128, 128))
        e_cp[0].wait_recv()
        go(e_cp[3])

    def prepare():
        for s in (1, 2, 3):
            e_cp[s].wait_recv()
        l_bs.wait()
        l_ms.wait()

    def encode(p):
        c, sub, width, _ = PARTS[p]
        lo = CLS[c][0] + sub
        row0 = pl.multiple_of(rep * ROWS, ROWS)

        def step(t, carry):
            rr = pl.ds(pl.multiple_of(t * SLAB, SLAB), SLAB)
            wr = pl.ds(pl.multiple_of(row0 + t * SLAB, SLAB), SLAB)
            fr = pl.ds(pl.multiple_of(off + t * SLAB, 16), SLAB)
            g = gn[fr, :]
            for k in range(width // 128):
                cc = pl.ds(lo + 128 * k, 128)
                b = bs[rr, cc]
                total = jnp.zeros((SLAB, 128), F32)
                for s in range(4):
                    v = (b - (fv[rep, rr, cc] if s == 0 else fb[s, rr, cc]).astype(F32)) * iv[s, fr, cc].astype(F32)
                    m = jnp.abs(v)
                    level = jnp.zeros_like(m)
                    for mid, val in THRESH:
                        level = jnp.where(m >= mid, val, level)
                    total = total + jnp.where(v < 0.0, -level, level) * sc[s, fr, cc].astype(F32)
                grad = total * 0.25
                moment = MOMENTUM_COEF * ms[rr, cc] + grad
                new = b - OUTER_RATE * (grad + MOMENTUM_COEF * moment)
                nm[rr, cc] = moment
                nb[rr, cc] = new
                W[c][pos["y"], pos["x"], wr, pl.ds(sub + 128 * k, 128)] = (new * g).astype(BF16)
            return carry

        lax.fori_loop(0, ROWS // SLAB, step, 0)

    def place(p, **at):
        half = at.pop("half", None)
        xs, ys = at.get("x", slice(None)), at.get("y", slice(None))
        if "z" in at:
            r0, n = at["z"] * ROWS, ROWS
        else:
            r0, n = 0, FROWS
        if half is not None:
            n = n // 2
            r0 = r0 + half * n
        if not isinstance(r0, int):
            r0 = pl.multiple_of(r0, 96)
        c, lo, width, _ = PARTS[p]
        return W[c].at[ys, xs, pl.ds(r0, n), pl.ds(lo, width)]

    M = {}
    OFF = (0, 1, -1, 2)
    used = [0]

    def both(*pair):
        out = []
        for j, s in enumerate((1, -1)):
            axis, ref = pair[j]
            out.append(remote(ref, ref, g_snd.at[used[0]], g_rcv.at[used[0]], nbr(axis, s)))
            used[0] += 1
        return out

    def full(p, axis, **fixed):
        here = place(p, **fixed, **{axis: pos[axis]})
        return both((axis, here), (axis, here))

    def half(p, axis, **fixed):
        return both(
            *[(axis, place(p, **fixed, **{axis: mod4(pos[axis] - s), "half": j})) for j, s in enumerate((1, -1))]
        )

    for p in range(len(PARTS)):
        m = a2a(p)
        M["r", p], M["d", p], M["f", p] = m[:2], m[2:4], m[4:]
        a, b, l = PARTS[p][3]
        R, S = (a, b) if b == "z" else (b, a)
        at = {b: pos[b], l: pos[l]}
        M["1", p], M["1h", p] = full(p, a, **at), half(p, a, **at)
        for i in range(4):
            at = {a: mod4(pos[a] + OFF[i]), l: pos[l]}
            M["2", p, i], M["2h", p, i] = full(p, b, **at), half(p, b, **at)
            M["3", p, i] = full(p, l, **{R: pos[R], S: mod4(pos[S] + OFF[i])})
            M["3h", p, i] = half(p, l, **{R: mod4(pos[R] + OFF[i])})
            if i:
                M["3", p, 3 + i] = full(p, l, **{R: mod4(pos[R] + OFF[i])})

    def mm(c, count, coords):
        lo, width = CLS[c]
        cc = pl.ds(lo, width)

        def chunk(t, carry):
            yy, xx = coords(t)
            kk = pl.ds(pl.multiple_of((yy * 4 + xx) * FROWS, FROWS), FROWS)

            def block(m, carry):
                mr = pl.ds(pl.multiple_of(m * 256, 256), 256)
                acc[mr, cc] += jnp.dot(tok[mr, kk], W[c][yy, xx], preferred_element_type=F32)
                return carry

            return lax.fori_loop(0, 3, block, carry)

        lax.fori_loop(0, count, chunk, 0)

    def offset(i):
        return i + lax.div(i, 2) - 2 * lax.div(i, 3)

    def mm_near(c, i):
        if c == 1:
            yy = mod4(pos["y"] + OFF[i])
            mm(c, 3, lambda t: (yy, mod4(pos["x"] + offset(t))))
        else:
            xx = mod4(pos["x"] + OFF[i])
            mm(c, 3, lambda t: (mod4(pos["y"] + offset(t)), xx))

    def mm_far(c, i):
        if c == 1:
            mm(c, 1, lambda t: (mod4(pos["y"] + OFF[i]), mod4(pos["x"] + 2)))
        else:
            mm(c, 1, lambda t: (mod4(pos["y"] + 2), mod4(pos["x"] + OFF[i])))

    same = len({p[3] for p in PARTS if p[0] == 0}) == 1

    def mm_row(c, i):
        by_y = PARTS[[p[0] for p in PARTS].index(0)][3][1] == "y"
        at = mod4(pos["y" if by_y else "x"] + OFF[i])
        mm(c, 4, (lambda t: (at, t)) if by_y else (lambda t: (t, at)))

    def mm_level(c, i):
        def coords(t):
            turn = lax.div(t, i + 1)
            iy = i * (1 - turn) + (t - i - 1) * turn
            ix = t * (1 - turn) + i * turn
            return mod4(pos["y"] + offset(iy)), mod4(pos["x"] + offset(ix))

        mm(c, 2 * i + 1, coords)

    def squares(i):
        rr = pl.ds(pl.multiple_of(core * TOK + i * 128, 128), 128)

        def step(t, s):
            for k in range(4):
                v = tok[rr, pl.ds(pl.multiple_of(t * 512 + k * 128, 128), 128)].astype(F32)
                s = s + v * v
            return s

        s = lax.fori_loop(0, D // 512, step, jnp.zeros((128, 128), F32))
        mean = jnp.sum(s, axis=1, keepdims=True) * (1.0 / D)
        ss[rr, :] = jnp.broadcast_to(lax.rsqrt(mean + 1e-05) * (D ** -0.5), (128, 128))

    def finish(c):
        lo, width = CLS[c]

        def scale(m, carry):
            mr = pl.ds(pl.multiple_of(m * 64, 64), 64)
            for k in range(width // 128):
                at = pl.ds(lo + 128 * k, 128)
                kv[mr, at] = (acc[mr, at] * ss[mr, :]).astype(BF16)
            return carry

        lax.fori_loop(0, 2 * TOK // 64, scale, 0)

    s_cp = remote(ss.at[mine, :], ss.at[mine, :], t_snd.at[8], t_rcv.at[8], other)
    left = []
    seen = set()

    def once(name):
        new = name not in seen
        seen.add(name)
        return new

    for kind, *key in SCHEDULE:
        key = tuple(key)
        if kind == "S":
            for m in M[key]:
                m.start()
            left.append(key)
        elif kind == "W":
            if once("wait"):
                early()
            if key[0] == "d":
                if once("prepare"):
                    prepare()
                c = PARTS[key[1]][0]
                if once(("factors", c)):
                    expand(*CLS[c])
            for m in M[key]:
                m.wait_recv()
        elif kind == "D":
            for m in M[key]:
                m.wait_send()
            left.remove(key)
        elif kind == "E":
            encode(*key)
        elif key[0] == "tk":
            l_tk[key[1]].start()
            go(t_cp[key[1]])
            if once("total"):
                acc[...] = jnp.zeros_like(acc)
        elif key[0] == "sq":
            if once("own tokens"):
                for t in l_tk:
                    t.wait()
            squares(key[1])
            if key[1] == 2:
                go(s_cp)
        elif key[0] == "fin":
            if once("factors"):
                s_cp.wait_recv()
            finish(key[1])
        else:
            if once("all tokens"):
                for t in t_cp:
                    t.wait_recv()
            {"near": mm_near, "far": mm_far, "all": mm_row if same else mm_level}[key[3]](key[1], key[2])
    for key in left:
        for m in M[key]:
            m.wait_send()

    for p in pending:
        p.wait_send()


def body(tokens, norm_gain, fragment, exponents, base_weight, momentum):
    any_ = pl.BlockSpec(memory_space=pl.ANY)
    dma = pltpu.SemaphoreType.DMA
    vm = pltpu.VMEM
    return pl.pallas_call(
        kernel,
        out_shape=(vm((ROWS, KVW), F32), vm((ROWS, KVW), F32), vm((2 * TOK, KVW), BF16)),
        in_specs=[any_] * 6,
        out_specs=[pl.BlockSpec(memory_space=vm)] * 3,
        scratch_shapes=[
            *[vm((4, 4, FROWS, width), BF16) for _, width in CLS],
            vm((2 * TOK, D), BF16),
            vm((2 * TOK, KVW), F32),
            vm((4, ROWS, KVW), BF16),
            vm((4, ROWS, KVW), BF16),
            vm((2, ROWS // 2, KVW), BF16),
            vm((ROWS, KVW), F32),
            vm((ROWS, KVW), F32),
            vm((D // 128, 128), BF16),
            vm((D // 128, 128), F32),
            vm((256, 128), F32),
            vm((BLOCK, 4 * ROWS), jnp.int32),
            vm((BLOCK, 4 * ROWS), BF16),
            vm((4, BLOCK, 256), BF16),
            vm((BLOCK, 256), BF16),
            vm((4, 256, KVW), BF16),
            vm((4, 256, KVW), BF16),
            vm((2 * TOK, 128), F32),
            dma((13,)),
            dma((6 * len(PARTS),)),
            dma((6 * len(PARTS),)),
            dma((4,)),
            dma((4,)),
            dma((9,)),
            dma((9,)),
            dma((42 * len(PARTS),)),
            dma((42 * len(PARTS),)),
        ],
        compiler_params=pltpu.CompilerParams(
            collective_id=0, has_side_effects=True, vmem_limit_bytes=59 * 1024 * 1024
        ),
        cost_estimate=pl.CostEstimate(flops=2 * 768 * 12288 * 1024, bytes_accessed=30_000_000, transcendentals=0),
    )(
        tokens,
        norm_gain.reshape(D // 128, 128),
        fragment.reshape(4, ROWS, KVW),
        exponents[0].T,
        base_weight,
        momentum,
    )


def solution(mesh):
    in_specs = (
        P(("replica", "fsdp", "tensor"), None),
        P(),
        P("replica", "fsdp", "tensor"),
        P("replica", "fsdp", "tensor"),
        P(("fsdp", "replica"), "tensor"),
        P(("fsdp", "replica"), "tensor"),
    )
    out_specs = (
        P(("fsdp", "replica"), "tensor"),
        P(("fsdp", "replica"), "tensor"),
        P(("replica", "fsdp"), "tensor"),
    )
    return jax.shard_map(body, mesh=mesh, in_specs=in_specs, out_specs=out_specs, check_vma=False)
```

time: 139 us -> 132 us (0.950)
  Pallas kernels: 138 us -> 128 us
  local copies, waits for them, and re-layouts: 0 us -> 2.9 us
    pallas_call x2 -> x1, Pallas kernels: 138 us -> 128 us  [body(): pl.pallas_call(kernel, out_shape=(vm((ROWS, KVW), F32), vm((ROWS, KVW), F...]
    unnamed x0 -> x3, local copies, waits for them, and re-layouts: none -> 2.9 us
where the time goes in v8:
time: 132 us; the launch traced here: 131 us
  Pallas kernels  128 us (97%)
  local copies, waits for them, and re-layouts  2.9 us (2%)
    pallas_call x1, Pallas kernels, body(): pl.pallas_call(kernel, out_shape=(vm((ROWS, KVW), F32), vm((ROWS, KVW), F...  128 us
    unnamed x3, local copies, waits for them, and re-layouts  2.9 us

profile of v8, /device:TPU:0, one launch (start us, length us, event | category | flops | bytes accessed | tf_op | source)
XLA Modules:
  0.0 131.4 jit_solution(4418595713986373286)
XLA Ops:
  0.6 127.9 %shard_map.85 = (f32[192,1024]{1,0:T(8,128)S(1)}, f32[192,1024]{1,0:T(8,128)S(1)}, bf16[768,1024]{1,0:T(8,128)(2,1)S(1)}) custom-call(bf16[384,12288]{1,0:T(8,128)(2,1)} %tokens.1, bf16[96,128]{1,0:T(8,128)(2,1)} %bitcast.7, bf16[4,192,1024]{2,1,0:T(8,128)(2,1)} %bitcast.5, s32[32,768]{1,0:T(8,128)} %bitcast.6, f32[192,1024]{1,0:T(8,128)} %base.1, ...), custom_call_target="tpu_custom_call" | custom-call | flops 19327352832 | bytes 30000000 | tf_op jit(solution)/shard_map/pallas_call | solution.py:459
  128.5 0.9 copy.12
  129.4 0.9 copy.13
  130.3 1.1 copy.14

commit v9 on v8

--- a/solution.py
+++ b/solution.py
@@ -15,92 +15,94 @@
 MOMENTUM_COEF = 0.9
 CLS = ((0, 256), (256, 384), (640, 384))
 PARTS = (
+    (0, 0, 128, ("x", "y", "z")),
     (0, 128, 128, ("y", "x", "z")),
-    (0, 0, 128, ("x", "y", "z")),
+    (1, 0, 128, ("z", "y", "x")),
     (2, 0, 128, ("z", "x", "y")),
-    (1, 0, 128, ("z", "y", "x")),
+    (2, 128, 256, ("x", "z", "y")),
     (1, 128, 256, ("y", "z", "x")),
-    (2, 128, 256, ("x", "z", "y")),
 )
 
+DIRECT = 2
 SCHEDULE = (
-    ("S", "r", 0), ("S", "d", 0), ("S", "r", 1), ("S", "d", 1), ("S", "r", 2), ("W", "r", 0), ("S", "f", 0),
-    ("S", "d", 2), ("W", "r", 1), ("S", "f", 1), ("S", "r", 3), ("S", "d", 3), ("W", "d", 0), ("W", "f", 0), ("E", 0),
-    ("S", "2", 0, 0), ("S", "1", 0), ("D", "r", 0), ("W", "r", 2), ("S", "f", 2), ("D", "r", 1), ("S", "r", 4),
-    ("W", "d", 1), ("W", "f", 1), ("E", 1), ("S", "1", 1), ("S", "2", 1, 0), ("D", "d", 0), ("W", "r", 3),
-    ("S", "f", 3), ("S", "d", 4), ("W", "2", 0, 0), ("S", "2h", 0, 0), ("W", "1", 0), ("S", "1h", 0),
-    ("S", "2", 0, 1), ("S", "2", 0, 2), ("W", "d", 2), ("W", "f", 2), ("E", 2), ("W", "1", 1), ("S", "2", 1, 1),
-    ("D", "r", 2), ("D", "d", 1), ("D", "f", 0), ("D", "f", 1), ("W", "r", 4), ("S", "f", 4), ("W", "2", 1, 0),
-    ("S", "2h", 1, 0), ("S", "1h", 1), ("D", "r", 3), ("D", "d", 2), ("S", "r", 5), ("S", "2", 1, 2), ("W", "1h", 0),
-    ("S", "2", 0, 3), ("D", "d", 3), ("S", "d", 5), ("S", "2", 2, 0), ("S", "1", 2), ("S", "3", 2, 0), ("W", "d", 3),
-    ("W", "f", 3), ("E", 3), ("D", "1", 0), ("S", "2", 3, 0), ("D", "2", 0, 0), ("W", "2", 0, 1), ("S", "2h", 0, 1),
-    ("W", "2", 0, 2), ("S", "2h", 0, 2), ("W", "2", 1, 1), ("S", "2h", 1, 1), ("W", "1h", 1), ("S", "2", 1, 3),
-    ("D", "f", 2), ("D", "r", 4), ("S", "1", 3), ("D", "1", 1), ("S", "3", 3, 0), ("W", "d", 4), ("W", "f", 4),
-    ("E", 4), ("D", "2h", 0, 0), ("W", "2", 0, 3), ("S", "2h", 0, 3), ("D", "2", 1, 0), ("D", "1h", 0), ("S", "1", 4),
-    ("W", "2", 2, 0), ("S", "2h", 2, 0), ("D", "f", 3), ("D", "d", 4), ("W", "r", 5), ("S", "f", 5), ("W", "1", 2),
-    ("S", "2", 2, 1), ("S", "1h", 2), ("D", "2", 0, 1), ("D", "2", 0, 2), ("S", "2", 2, 2), ("S", "2", 4, 0),
-    ("D", "2", 1, 1), ("D", "2h", 1, 0), ("W", "2", 1, 2), ("S", "2h", 1, 2), ("W", "2", 3, 0), ("S", "2h", 3, 0),
-    ("D", "1h", 1), ("S", "3", 4, 0), ("W", "1", 3), ("S", "2", 3, 1), ("D", "f", 4), ("S", "1h", 3),
-    ("W", "2", 1, 3), ("S", "2h", 1, 3), ("S", "2", 3, 2), ("S", "3", 0, 0), ("C", "tk", 0), ("S", "3", 3, 1),
-    ("C", "tk", 1), ("D", "2", 0, 3), ("W", "1h", 2), ("S", "2", 2, 3), ("D", "r", 5), ("S", "3", 1, 0),
-    ("D", "2", 1, 2), ("S", "3", 2, 1), ("W", "d", 5), ("W", "f", 5), ("E", 5), ("D", "1", 2), ("S", "2", 5, 0),
-    ("D", "3", 2, 0), ("D", "2h", 1, 1), ("D", "2", 3, 0), ("W", "1h", 3), ("S", "2", 3, 3), ("D", "2", 2, 0),
-    ("D", "2h", 0, 1), ("D", "2h", 0, 2), ("D", "3", 3, 0), ("D", "2h", 0, 3), ("S", "1", 5), ("W", "2", 2, 1),
-    ("S", "2h", 2, 1), ("D", "2", 1, 3), ("W", "1", 4), ("S", "1h", 4), ("D", "1", 3), ("D", "d", 5),
-    ("S", "2", 4, 1), ("D", "2h", 2, 0), ("W", "2", 2, 2), ("S", "2h", 2, 2), ("S", "2", 4, 2), ("S", "3", 5, 0),
-    ("C", "tk", 2), ("C", "tk", 3), ("W", "2", 3, 1), ("S", "2h", 3, 1), ("S", "3", 3, 2), ("C", "tk", 4),
-    ("W", "2", 3, 2), ("S", "2h", 3, 2), ("D", "2", 2, 1), ("W", "2", 2, 3), ("S", "2h", 2, 3), ("D", "1h", 2),
-    ("D", "f", 5), ("W", "2", 4, 0), ("S", "2h", 4, 0), ("D", "2", 2, 2), ("S", "3", 4, 1), ("D", "2h", 1, 2),
-    ("D", "2h", 3, 0), ("S", "3", 2, 2), ("C", "tk", 5), ("D", "1", 4), ("D", "2h", 1, 3), ("S", "3", 2, 3),
-    ("W", "2", 3, 3), ("S", "2h", 3, 3), ("D", "3", 3, 1), ("S", "3", 4, 2), ("D", "1h", 3), ("D", "3", 0, 0),
-    ("S", "3", 0, 1), ("W", "1h", 4), ("S", "2", 4, 3), ("D", "2", 3, 1), ("D", "2", 3, 2), ("S", "3", 2, 4),
-    ("C", "tk", 6), ("D", "2", 2, 3), ("D", "3", 4, 0), ("S", "3", 3, 3), ("D", "2h", 2, 1), ("W", "1", 5),
-    ("S", "1h", 5), ("D", "2", 4, 0), ("D", "3", 1, 0), ("W", "2", 5, 0), ("S", "2h", 5, 0), ("S", "2", 5, 1),
-    ("S", "2", 5, 2), ("C", "tk", 7), ("D", "2h", 2, 2), ("W", "2h", 4, 0), ("S", "3", 4, 3), ("W", "2", 4, 1),
-    ("S", "2h", 4, 1), ("D", "3", 2, 1), ("D", "2", 3, 3), ("D", "2h", 3, 1), ("D", "1h", 4), ("D", "2h", 3, 2),
-    ("S", "3", 5, 1), ("W", "2", 4, 2), ("S", "2h", 4, 2), ("D", "2h", 2, 3), ("D", "3", 3, 2), ("S", "3", 3, 4),
-    ("S", "3", 5, 2), ("C", "sq", 0), ("D", "2", 5, 0), ("D", "2h", 4, 0), ("D", "2", 4, 1), ("W", "1h", 5),
-    ("S", "2", 5, 3), ("D", "2h", 3, 3), ("D", "3", 2, 2), ("D", "3", 2, 3), ("D", "3", 5, 0), ("S", "3", 2, 5),
-    ("C", "sq", 1), ("D", "1", 5), ("D", "3", 4, 1), ("S", "3", 3, 5), ("C", "sq", 2), ("W", "3", 3, 0),
+    ("S", "r", 0), ("S", "d", 0), ("S", "r", 1), ("S", "d", 1), ("S", "r", 2), ("S", "d", 2), ("D", "r", 0),
+    ("S", "r", 3), ("D", "d", 0), ("S", "d", 3), ("D", "r", 1), ("D", "r", 2), ("S", "r", 4), ("W", "d", 0),
+    ("W", "r", 0), ("E", 0), ("S", "1", 0), ("S", "2", 0, 0), ("D", "d", 1), ("D", "r", 3), ("W", "r", 2),
+    ("S", "f", 2), ("D", "d", 2), ("S", "d", 4), ("W", "d", 1), ("W", "r", 1), ("E", 1), ("D", "1", 0),
+    ("S", "2", 1, 0), ("D", "2", 0, 0), ("S", "1", 1), ("D", "d", 3), ("W", "r", 3), ("S", "f", 3), ("D", "r", 4),
+    ("D", "f", 2), ("S", "r", 5), ("D", "2", 1, 0), ("W", "1", 0), ("S", "1h", 0), ("D", "1", 1), ("W", "2", 0, 0),
+    ("S", "2h", 0, 0), ("S", "2", 0, 1), ("S", "2", 0, 2), ("D", "f", 3), ("W", "r", 4), ("S", "f", 4), ("W", "d", 2),
+    ("W", "f", 2), ("E", 2), ("D", "1h", 0), ("W", "2", 1, 0), ("S", "2h", 1, 0), ("W", "1", 1), ("S", "2", 1, 1),
+    ("D", "2h", 0, 0), ("S", "1h", 1), ("S", "2", 1, 2), ("W", "1h", 0), ("S", "2", 0, 3), ("S", "d", 5),
+    ("S", "2", 2, 0), ("D", "r", 5), ("S", "1", 2), ("D", "2h", 1, 0), ("S", "3", 2, 0), ("W", "d", 3), ("W", "f", 3),
+    ("E", 3), ("S", "2", 3, 0), ("D", "d", 4), ("S", "1", 3), ("D", "2", 0, 1), ("D", "2", 0, 2), ("S", "3", 3, 0),
+    ("D", "1h", 1), ("W", "2", 0, 1), ("S", "2h", 0, 1), ("C", "tk", 0), ("W", "2", 0, 2), ("S", "2h", 0, 2),
+    ("D", "f", 4), ("W", "r", 5), ("S", "f", 5), ("D", "2", 1, 1), ("D", "2", 1, 2), ("W", "1h", 1), ("S", "2", 1, 3),
+    ("W", "d", 4), ("W", "f", 4), ("E", 4), ("D", "3", 2, 0), ("D", "2", 3, 0), ("S", "1", 4), ("D", "1", 2),
+    ("D", "1", 3), ("S", "2", 4, 0), ("D", "2", 1, 3), ("W", "2", 1, 1), ("S", "2h", 1, 1), ("D", "2", 0, 3),
+    ("D", "2", 2, 0), ("D", "2h", 0, 1), ("D", "2h", 0, 2), ("D", "3", 3, 0), ("W", "2", 0, 3), ("S", "2h", 0, 3),
+    ("W", "2", 2, 0), ("S", "2h", 2, 0), ("W", "1", 2), ("S", "2", 2, 1), ("W", "2", 1, 2), ("S", "2h", 1, 2),
+    ("D", "2h", 0, 3), ("S", "2", 2, 2), ("D", "2h", 1, 1), ("W", "2", 1, 3), ("S", "2h", 1, 3), ("D", "f", 5),
+    ("D", "d", 5), ("S", "1h", 2), ("W", "2", 3, 0), ("S", "2h", 3, 0), ("W", "1", 3), ("S", "1h", 3),
+    ("S", "2", 3, 1), ("S", "2", 3, 2), ("D", "2h", 2, 0), ("S", "3", 4, 0), ("S", "3", 0, 0), ("S", "3", 1, 0),
+    ("W", "d", 5), ("W", "f", 5), ("E", 5), ("D", "2", 2, 1), ("D", "2", 2, 2), ("S", "1", 5), ("D", "1h", 2),
+    ("D", "1h", 3), ("S", "2", 5, 0), ("D", "2h", 1, 2), ("D", "2h", 1, 3), ("D", "2h", 3, 0), ("S", "3", 5, 0),
+    ("C", "tk", 1), ("W", "1h", 2), ("S", "2", 2, 3), ("C", "tk", 2), ("W", "2", 2, 1), ("S", "2h", 2, 1),
+    ("C", "tk", 3), ("D", "1", 4), ("W", "1h", 3), ("S", "2", 3, 3), ("W", "2", 2, 2), ("S", "2h", 2, 2),
+    ("D", "2", 4, 0), ("S", "3", 0, 1), ("C", "tk", 4), ("D", "2", 3, 1), ("S", "3", 2, 1), ("D", "3", 0, 0),
+    ("D", "3", 1, 0), ("S", "3", 1, 1), ("D", "2", 3, 2), ("W", "1", 4), ("S", "1h", 4), ("W", "2", 4, 0),
+    ("S", "2h", 4, 0), ("S", "3", 3, 1), ("S", "2", 4, 1), ("C", "tk", 5), ("W", "2", 3, 1), ("S", "2h", 3, 1),
+    ("W", "2", 3, 2), ("S", "2h", 3, 2), ("D", "2h", 2, 1), ("S", "3", 4, 1), ("S", "2", 4, 2), ("S", "3", 2, 2),
+    ("C", "tk", 6), ("D", "2h", 2, 2), ("D", "3", 4, 0), ("D", "2", 2, 3), ("S", "3", 3, 2), ("D", "2", 3, 3),
+    ("S", "3", 2, 3), ("W", "2", 2, 3), ("S", "2h", 2, 3), ("D", "2h", 3, 1), ("W", "2", 3, 3), ("S", "2h", 3, 3),
+    ("C", "tk", 7), ("D", "3", 3, 1), ("D", "1", 5), ("S", "3", 4, 2), ("D", "2h", 3, 2), ("D", "3", 2, 1),
+    ("S", "3", 2, 4), ("D", "3", 0, 1), ("D", "3", 1, 1), ("D", "2h", 4, 0), ("D", "2", 5, 0), ("S", "3", 0, 2),
+    ("W", "1", 5), ("S", "2", 5, 1), ("D", "2h", 2, 3), ("S", "1h", 5), ("W", "1h", 4), ("S", "2", 4, 3),
+    ("D", "3", 3, 2), ("S", "3", 3, 3), ("W", "2h", 4, 0), ("S", "3", 4, 3), ("C", "sq", 0), ("D", "2", 4, 1),
+    ("W", "2", 5, 0), ("S", "2h", 5, 0), ("D", "1h", 4), ("D", "3", 5, 0), ("D", "2h", 3, 3), ("D", "3", 2, 2),
+    ("D", "3", 2, 3), ("S", "3", 5, 1), ("C", "sq", 1), ("D", "3", 0, 2), ("D", "2", 4, 2), ("W", "2", 4, 1),
+    ("S", "2h", 4, 1), ("D", "3", 4, 1), ("D", "1h", 5), ("S", "3", 3, 4), ("S", "2", 5, 2), ("S", "3", 5, 2),
+    ("C", "sq", 2), ("D", "3", 2, 4), ("S", "3", 2, 5), ("W", "2", 4, 2), ("S", "2h", 4, 2), ("W", "1h", 5),
+    ("S", "2", 5, 3), ("D", "3", 3, 3), ("D", "3", 4, 2), ("D", "3", 4, 3), ("S", "3", 3, 5), ("W", "3", 3, 0),
     ("W", "3", 3, 1), ("W", "3", 3, 2), ("W", "3", 3, 3), ("W", "3", 4, 0), ("W", "3", 4, 1), ("W", "3", 4, 2),
-    ("W", "3", 4, 3), ("C", "mm", 1, 0, "near"), ("D", "2", 4, 2), ("D", "3", 0, 1), ("D", "2h", 5, 0),
-    ("W", "2", 4, 3), ("S", "2h", 4, 3), ("W", "2h", 5, 0), ("S", "3", 5, 3), ("W", "2", 5, 1), ("S", "2h", 5, 1),
-    ("W", "2", 5, 2), ("S", "2h", 5, 2), ("D", "3", 3, 3), ("D", "3", 4, 2), ("D", "1h", 5), ("D", "3", 4, 3),
-    ("W", "2h", 4, 1), ("S", "3", 4, 4), ("D", "3", 2, 4), ("W", "2h", 2, 0), ("W", "2h", 2, 1), ("W", "2h", 2, 2),
-    ("W", "2h", 2, 3), ("S", "3", 2, 6), ("W", "2", 5, 3), ("S", "2h", 5, 3), ("D", "2h", 4, 1), ("S", "3", 1, 1),
-    ("D", "2h", 4, 2), ("D", "2", 4, 3), ("S", "3", 0, 2), ("S", "3", 1, 2), ("D", "3", 5, 1), ("D", "3", 5, 2),
-    ("W", "3", 2, 0), ("W", "3", 2, 1), ("W", "3", 2, 2), ("W", "3", 2, 3), ("S", "3h", 2, 0), ("D", "2", 5, 1),
-    ("D", "2", 5, 2), ("S", "3", 0, 3), ("D", "2", 5, 3), ("S", "3", 1, 3), ("W", "3", 5, 0), ("W", "3", 5, 1),
-    ("W", "3", 5, 2), ("W", "3", 5, 3), ("C", "mm", 2, 0, "near"), ("D", "3", 2, 5), ("W", "2h", 5, 1),
-    ("S", "3", 5, 4), ("D", "2h", 4, 3), ("S", "3", 0, 4), ("D", "3", 3, 4), ("D", "3", 3, 5), ("W", "2h", 4, 2),
-    ("S", "3", 4, 5), ("D", "2h", 5, 1), ("D", "2h", 5, 2), ("S", "3", 1, 4), ("W", "3", 3, 4), ("W", "3", 4, 4),
-    ("C", "mm", 1, 1, "near"), ("D", "3", 5, 3), ("D", "3", 2, 6), ("D", "3h", 2, 0), ("W", "2h", 5, 2),
-    ("S", "3", 5, 5), ("D", "2h", 5, 3), ("D", "3", 1, 1), ("D", "3", 0, 2), ("D", "3", 1, 2), ("D", "3", 0, 3),
-    ("D", "3", 1, 3), ("S", "3", 0, 5), ("W", "2h", 3, 0), ("W", "2h", 3, 1), ("W", "2h", 3, 2), ("W", "2h", 3, 3),
-    ("S", "3", 3, 6), ("S", "3", 1, 5), ("D", "3", 4, 4), ("W", "2h", 4, 3), ("S", "3", 4, 6), ("W", "3", 2, 4),
-    ("W", "3", 5, 4), ("C", "mm", 2, 1, "near"), ("W", "2h", 5, 3), ("S", "3", 5, 6), ("D", "3", 0, 4),
-    ("W", "2h", 0, 0), ("W", "2h", 0, 1), ("W", "2h", 0, 2), ("W", "2h", 0, 3), ("S", "3", 0, 6), ("W", "3", 3, 5),
-    ("W", "3", 4, 5), ("C", "mm", 1, 2, "near"), ("D", "3", 1, 4), ("W", "2h", 1, 0), ("W", "2h", 1, 1),
-    ("W", "2h", 1, 2), ("W", "2h", 1, 3), ("S", "3", 1, 6), ("D", "3", 4, 5), ("S", "3h", 3, 0), ("W", "3", 2, 5),
-    ("W", "3", 5, 5), ("C", "mm", 2, 2, "near"), ("D", "3", 3, 6), ("S", "3h", 4, 0), ("D", "3", 5, 4),
-    ("S", "3h", 5, 0), ("D", "3", 0, 5), ("W", "3", 0, 0), ("W", "3", 0, 1), ("W", "3", 0, 2), ("W", "3", 0, 3),
-    ("S", "3h", 0, 0), ("D", "3", 1, 5), ("W", "3", 1, 0), ("W", "3", 1, 1), ("W", "3", 1, 2), ("W", "3", 1, 3),
-    ("S", "3h", 1, 0), ("S", "3h", 3, 1), ("D", "3", 5, 5), ("S", "3h", 2, 1), ("W", "3", 3, 6), ("W", "3", 4, 6),
-    ("C", "mm", 1, 3, "near"), ("D", "3", 0, 6), ("W", "3", 0, 4), ("S", "3h", 0, 1), ("S", "3h", 4, 1),
-    ("S", "3h", 5, 1), ("W", "3", 1, 4), ("S", "3h", 1, 1), ("W", "3", 2, 6), ("W", "3", 5, 6),
-    ("C", "mm", 2, 3, "near"), ("W", "3", 0, 5), ("S", "3h", 0, 2), ("D", "3", 4, 6), ("D", "3h", 3, 0),
-    ("S", "3h", 3, 2), ("W", "3h", 0, 0), ("W", "3h", 1, 0), ("C", "mm", 0, 0, "all"), ("W", "3h", 3, 0),
-    ("W", "3h", 4, 0), ("C", "mm", 1, 0, "far"), ("D", "3", 5, 6), ("S", "3h", 2, 2), ("D", "3", 1, 6),
-    ("D", "3h", 0, 0), ("W", "3", 1, 5), ("S", "3h", 1, 2), ("S", "3h", 4, 2), ("W", "3h", 2, 0), ("W", "3h", 5, 0),
-    ("C", "mm", 2, 0, "far"), ("S", "3h", 5, 2), ("D", "3h", 1, 0), ("W", "3", 0, 6), ("S", "3h", 0, 3),
-    ("W", "3h", 0, 1), ("W", "3h", 1, 1), ("C", "mm", 0, 1, "all"), ("W", "3", 1, 6), ("S", "3h", 1, 3),
-    ("W", "3h", 2, 1), ("W", "3h", 5, 1), ("C", "mm", 2, 1, "far"), ("D", "3h", 4, 0), ("D", "3h", 3, 1),
-    ("S", "3h", 3, 3), ("W", "3h", 3, 1), ("W", "3h", 4, 1), ("C", "mm", 1, 1, "far"), ("D", "3h", 2, 1),
-    ("D", "3h", 5, 0), ("S", "3h", 2, 3), ("S", "3h", 4, 3), ("S", "3h", 5, 3), ("W", "3h", 0, 2), ("W", "3h", 1, 2),
-    ("C", "mm", 0, 2, "all"), ("W", "3h", 0, 3), ("W", "3h", 1, 3), ("C", "mm", 0, 3, "all"), ("C", "fin", 0),
-    ("W", "3h", 3, 2), ("W", "3h", 4, 2), ("C", "mm", 1, 2, "far"), ("W", "3h", 2, 2), ("W", "3h", 5, 2),
-    ("C", "mm", 2, 2, "far"), ("W", "3h", 3, 3), ("W", "3h", 4, 3), ("C", "mm", 1, 3, "far"), ("C", "fin", 1),
-    ("W", "3h", 2, 3), ("W", "3h", 5, 3), ("C", "mm", 2, 3, "far"), ("C", "fin", 2),
+    ("W", "3", 4, 3), ("C", "mm", 2, 0, "near"), ("D", "2h", 5, 0), ("D", "2", 5, 1), ("D", "2h", 4, 1),
+    ("D", "2", 4, 3), ("D", "2h", 4, 2), ("W", "2", 5, 1), ("S", "2h", 5, 1), ("W", "2", 4, 3), ("S", "2h", 4, 3),
+    ("D", "3", 5, 1), ("D", "3", 5, 2), ("W", "2h", 5, 0), ("S", "3", 5, 3), ("D", "3", 3, 4), ("W", "2h", 4, 1),
+    ("S", "3", 4, 4), ("W", "2h", 2, 0), ("W", "2h", 2, 1), ("W", "2h", 2, 2), ("W", "2h", 2, 3), ("S", "3", 2, 6),
+    ("S", "3", 1, 2), ("D", "2", 5, 2), ("S", "3", 0, 3), ("W", "2", 5, 2), ("S", "2h", 5, 2), ("S", "3", 1, 3),
+    ("D", "3", 2, 5), ("D", "3", 5, 3), ("W", "3", 2, 0), ("W", "3", 2, 1), ("W", "3", 2, 2), ("W", "3", 2, 3),
+    ("S", "3h", 2, 0), ("D", "2", 5, 3), ("D", "2h", 5, 1), ("D", "2h", 4, 3), ("S", "3", 0, 4), ("W", "2h", 5, 1),
+    ("S", "3", 5, 4), ("W", "3", 5, 0), ("W", "3", 5, 1), ("W", "3", 5, 2), ("W", "3", 5, 3),
+    ("C", "mm", 1, 0, "near"), ("D", "3", 1, 2), ("D", "3", 0, 3), ("D", "2h", 5, 2), ("D", "3", 1, 3),
+    ("W", "2", 5, 3), ("S", "2h", 5, 3), ("D", "3", 3, 5), ("W", "2h", 4, 2), ("S", "3", 4, 5), ("S", "3", 1, 4),
+    ("W", "3", 3, 4), ("W", "3", 4, 4), ("C", "mm", 2, 1, "near"), ("D", "2h", 5, 3), ("D", "3", 0, 4),
+    ("S", "3", 0, 5), ("D", "3", 2, 6), ("D", "3h", 2, 0), ("W", "2h", 5, 2), ("S", "3", 5, 5), ("D", "3", 4, 4),
+    ("W", "2h", 3, 0), ("W", "2h", 3, 1), ("W", "2h", 3, 2), ("W", "2h", 3, 3), ("S", "3", 3, 6), ("D", "3", 1, 4),
+    ("S", "3", 1, 5), ("W", "3", 2, 4), ("W", "3", 5, 4), ("C", "mm", 1, 1, "near"), ("D", "3", 4, 5),
+    ("W", "2h", 4, 3), ("S", "3", 4, 6), ("W", "2h", 0, 0), ("W", "2h", 0, 1), ("W", "2h", 0, 2), ("W", "2h", 0, 3),
+    ("S", "3", 0, 6), ("D", "3", 5, 4), ("W", "2h", 5, 3), ("S", "3", 5, 6), ("W", "3", 3, 5), ("W", "3", 4, 5),
+    ("C", "mm", 2, 2, "near"), ("D", "3", 0, 5), ("W", "2h", 1, 0), ("W", "2h", 1, 1), ("W", "2h", 1, 2),
+    ("W", "2h", 1, 3), ("S", "3", 1, 6), ("D", "3", 3, 6), ("S", "3h", 3, 0), ("W", "3", 2, 5), ("W", "3", 5, 5),
+    ("C", "mm", 1, 2, "near"), ("D", "3", 1, 5), ("D", "3", 0, 6), ("W", "3", 0, 0), ("W", "3", 0, 1),
+    ("W", "3", 0, 2), ("W", "3", 0, 3), ("S", "3h", 0, 0), ("S", "3h", 4, 0), ("D", "3", 5, 5), ("S", "3h", 5, 0),
+    ("W", "3", 1, 0), ("W", "3", 1, 1), ("W", "3", 1, 2), ("W", "3", 1, 3), ("S", "3h", 1, 0), ("W", "3", 0, 4),
+    ("S", "3h", 0, 1), ("D", "3", 4, 6), ("D", "3h", 3, 0), ("S", "3h", 3, 1), ("D", "3", 5, 6), ("S", "3h", 2, 1),
+    ("W", "3", 3, 6), ("W", "3", 4, 6), ("C", "mm", 2, 3, "near"), ("D", "3", 1, 6), ("D", "3h", 0, 0),
+    ("W", "3", 1, 4), ("S", "3h", 1, 1), ("S", "3h", 4, 1), ("S", "3h", 5, 1), ("W", "3", 2, 6), ("W", "3", 5, 6),
+    ("C", "mm", 1, 3, "near"), ("D", "3h", 1, 0), ("D", "3h", 0, 1), ("W", "3", 0, 5), ("S", "3h", 0, 2),
+    ("W", "3h", 0, 0), ("W", "3h", 1, 0), ("C", "mm", 0, 0, "all"), ("W", "3", 1, 5), ("S", "3h", 1, 2),
+    ("D", "3h", 4, 0), ("D", "3h", 3, 1), ("S", "3h", 3, 2), ("D", "3h", 5, 0), ("D", "3h", 2, 1), ("S", "3h", 2, 2),
+    ("W", "3h", 2, 0), ("W", "3h", 5, 0), ("C", "mm", 1, 0, "far"), ("W", "3h", 3, 0), ("W", "3h", 4, 0),
+    ("C", "mm", 2, 0, "far"), ("D", "3h", 1, 1), ("W", "3", 0, 6), ("S", "3h", 0, 3), ("S", "3h", 4, 2),
+    ("S", "3h", 5, 2), ("W", "3h", 0, 1), ("W", "3h", 1, 1), ("C", "mm", 0, 1, "all"), ("D", "3h", 0, 2),
+    ("W", "3", 1, 6), ("S", "3h", 1, 3), ("W", "3h", 3, 1), ("W", "3h", 4, 1), ("C", "mm", 2, 1, "far"),
+    ("D", "3h", 4, 1), ("D", "3h", 3, 2), ("S", "3h", 3, 3), ("D", "3h", 5, 1), ("D", "3h", 2, 2), ("S", "3h", 2, 3),
+    ("W", "3h", 2, 1), ("W", "3h", 5, 1), ("C", "mm", 1, 1, "far"), ("S", "3h", 4, 3), ("W", "3h", 0, 2),
+    ("W", "3h", 1, 2), ("C", "mm", 0, 2, "all"), ("S", "3h", 5, 3), ("W", "3h", 0, 3), ("W", "3h", 1, 3),
+    ("C", "mm", 0, 3, "all"), ("W", "3h", 2, 2), ("W", "3h", 5, 2), ("C", "mm", 1, 2, "far"), ("W", "3h", 3, 2),
+    ("W", "3h", 4, 2), ("C", "mm", 2, 2, "far"), ("C", "fin", 0), ("W", "3h", 3, 3), ("W", "3h", 4, 3),
+    ("C", "mm", 2, 3, "far"), ("W", "3h", 2, 3), ("W", "3h", 5, 3), ("C", "mm", 1, 3, "far"), ("C", "fin", 1),
+    ("C", "fin", 2),
 )
 
 THRESH = ((0.25, 0.5), (0.75, 1.0), (1.25, 1.5), (1.75, 2.0), (2.5, 3.0), (3.5, 4.0), (5.0, 6.0))
@@ -134,6 +136,13 @@
             src_ref=src, dst_ref=dst, send_sem=ss_, recv_sem=rs_, device_id=dev, device_id_type=MESH
         )
 
+    seen = set()
+
+    def once(name):
+        new = name not in seen
+        seen.add(name)
+        return new
+
     pending = []
 
     def go(copy):
@@ -141,7 +150,7 @@
         pending.append(copy)
 
     barrier = pltpu.get_barrier_semaphore()
-    peers = [nbr(a, s) for a in "xyz" for s in (1, -1)] + [other]
+    peers = [nbr(a, s) for a in "xyz" for s in (1, -1)] + [nbr("z", 2), other]
     for p in peers:
         pl.semaphore_signal(barrier, inc=1, device_id=p, device_id_type=MESH)
 
@@ -172,6 +181,8 @@
         n = lax.broadcasted_iota(jnp.int32, (BLOCK, width), 1)
         pick = jnp.where(j == lax.div(n + lo, BLOCK), 1.0, 0.0).astype(BF16)
         for slot in range(4):
+            if slot == 3 and once("far exponents"):
+                e_cp[3].wait_recv()
             e = (window(rep)[...] if slot == 0 else er[slot]).astype(F32)
             for ref, sign in ((sc, 1.0), (iv, -1.0)):
                 small = jnp.exp2(sign * e).astype(BF16)
@@ -229,7 +240,7 @@
         go(e_cp[3])
 
     def prepare():
-        for s in (1, 2, 3):
+        for s in (1, 2):
             e_cp[s].wait_recv()
         l_bs.wait()
         l_ms.wait()
@@ -304,6 +315,9 @@
     for p in range(len(PARTS)):
         m = a2a(p)
         M["r", p], M["d", p], M["f", p] = m[:2], m[2:4], m[4:]
+        if p < DIRECT:
+            far = remote(fv.at[zo, :, cols(p)], fb.at[3, :, cols(p)], a_snd.at[6 * p], a_rcv.at[6 * p], nbr("z", 2))
+            M["r", p] = [far]
         a, b, l = PARTS[p][3]
         R, S = (a, b) if b == "z" else (b, a)
         at = {b: pos[b], l: pos[l]}
@@ -325,11 +339,11 @@
             kk = pl.ds(pl.multiple_of((yy * 4 + xx) * FROWS, FROWS), FROWS)
 
             def block(m, carry):
-                mr = pl.ds(pl.multiple_of(m * 256, 256), 256)
+                mr = pl.ds(pl.multiple_of(m * TOK, TOK), TOK)
                 acc[mr, cc] += jnp.dot(tok[mr, kk], W[c][yy, xx], preferred_element_type=F32)
                 return carry
 
-            return lax.fori_loop(0, 3, block, carry)
+            return lax.fori_loop(0, 2, block, carry)
 
         lax.fori_loop(0, count, chunk, 0)
 
@@ -393,13 +407,6 @@
 
     s_cp = remote(ss.at[mine, :], ss.at[mine, :], t_snd.at[8], t_rcv.at[8], other)
     left = []
-    seen = set()
-
-    def once(name):
-        new = name not in seen
-        seen.add(name)
-        return new
-
     for kind, *key in SCHEDULE:
         key = tuple(key)
         if kind == "S":

time: 132 us -> 131 us (level)
  no operation moved by 1% of the time
where the time goes in v9:
time: 131 us
  Pallas kernels  128 us (98%)
  local copies, waits for them, and re-layouts  2.9 us (2%)
    pallas_call x1, Pallas kernels, body(): pl.pallas_call(kernel, out_shape=(vm((ROWS, KVW), F32), vm((ROWS, KVW), F...  128 us
    unnamed x3, local copies, waits for them, and re-layouts  2.9 us

profile of v9, /device:TPU:0, one launch (start us, length us, event | category | flops | bytes accessed | tf_op | source)
XLA Modules:
  0.0 131.3 jit_solution(5276796737701911)
XLA Ops:
  0.6 127.7 %shard_map.85 = (f32[192,1024]{1,0:T(8,128)S(1)}, f32[192,1024]{1,0:T(8,128)S(1)}, bf16[768,1024]{1,0:T(8,128)(2,1)S(1)}) custom-call(bf16[384,12288]{1,0:T(8,128)(2,1)} %tokens.1, bf16[96,128]{1,0:T(8,128)(2,1)} %bitcast.7, bf16[4,192,1024]{2,1,0:T(8,128)(2,1)} %bitcast.5, s32[32,768]{1,0:T(8,128)} %bitcast.6, f32[192,1024]{1,0:T(8,128)} %base.1, ...), custom_call_target="tpu_custom_call" | custom-call | flops 19327352832 | bytes 30000000 | tf_op jit(solution)/shard_map/pallas_call | solution.py:466
  128.4 0.9 copy.12
  129.2 0.9 copy.13
  130.1 1.1 copy.14

commit v10 on v9

--- a/solution.py
+++ b/solution.py
@@ -19,90 +19,91 @@
     (0, 128, 128, ("y", "x", "z")),
     (1, 0, 128, ("z", "y", "x")),
     (2, 0, 128, ("z", "x", "y")),
+    (1, 128, 256, ("y", "z", "x")),
     (2, 128, 256, ("x", "z", "y")),
-    (1, 128, 256, ("y", "z", "x")),
 )
 
 DIRECT = 2
 SCHEDULE = (
-    ("S", "r", 0), ("S", "d", 0), ("S", "r", 1), ("S", "d", 1), ("S", "r", 2), ("S", "d", 2), ("D", "r", 0),
-    ("S", "r", 3), ("D", "d", 0), ("S", "d", 3), ("D", "r", 1), ("D", "r", 2), ("S", "r", 4), ("W", "d", 0),
-    ("W", "r", 0), ("E", 0), ("S", "1", 0), ("S", "2", 0, 0), ("D", "d", 1), ("D", "r", 3), ("W", "r", 2),
-    ("S", "f", 2), ("D", "d", 2), ("S", "d", 4), ("W", "d", 1), ("W", "r", 1), ("E", 1), ("D", "1", 0),
-    ("S", "2", 1, 0), ("D", "2", 0, 0), ("S", "1", 1), ("D", "d", 3), ("W", "r", 3), ("S", "f", 3), ("D", "r", 4),
-    ("D", "f", 2), ("S", "r", 5), ("D", "2", 1, 0), ("W", "1", 0), ("S", "1h", 0), ("D", "1", 1), ("W", "2", 0, 0),
-    ("S", "2h", 0, 0), ("S", "2", 0, 1), ("S", "2", 0, 2), ("D", "f", 3), ("W", "r", 4), ("S", "f", 4), ("W", "d", 2),
-    ("W", "f", 2), ("E", 2), ("D", "1h", 0), ("W", "2", 1, 0), ("S", "2h", 1, 0), ("W", "1", 1), ("S", "2", 1, 1),
-    ("D", "2h", 0, 0), ("S", "1h", 1), ("S", "2", 1, 2), ("W", "1h", 0), ("S", "2", 0, 3), ("S", "d", 5),
-    ("S", "2", 2, 0), ("D", "r", 5), ("S", "1", 2), ("D", "2h", 1, 0), ("S", "3", 2, 0), ("W", "d", 3), ("W", "f", 3),
-    ("E", 3), ("S", "2", 3, 0), ("D", "d", 4), ("S", "1", 3), ("D", "2", 0, 1), ("D", "2", 0, 2), ("S", "3", 3, 0),
-    ("D", "1h", 1), ("W", "2", 0, 1), ("S", "2h", 0, 1), ("C", "tk", 0), ("W", "2", 0, 2), ("S", "2h", 0, 2),
-    ("D", "f", 4), ("W", "r", 5), ("S", "f", 5), ("D", "2", 1, 1), ("D", "2", 1, 2), ("W", "1h", 1), ("S", "2", 1, 3),
-    ("W", "d", 4), ("W", "f", 4), ("E", 4), ("D", "3", 2, 0), ("D", "2", 3, 0), ("S", "1", 4), ("D", "1", 2),
-    ("D", "1", 3), ("S", "2", 4, 0), ("D", "2", 1, 3), ("W", "2", 1, 1), ("S", "2h", 1, 1), ("D", "2", 0, 3),
-    ("D", "2", 2, 0), ("D", "2h", 0, 1), ("D", "2h", 0, 2), ("D", "3", 3, 0), ("W", "2", 0, 3), ("S", "2h", 0, 3),
-    ("W", "2", 2, 0), ("S", "2h", 2, 0), ("W", "1", 2), ("S", "2", 2, 1), ("W", "2", 1, 2), ("S", "2h", 1, 2),
-    ("D", "2h", 0, 3), ("S", "2", 2, 2), ("D", "2h", 1, 1), ("W", "2", 1, 3), ("S", "2h", 1, 3), ("D", "f", 5),
-    ("D", "d", 5), ("S", "1h", 2), ("W", "2", 3, 0), ("S", "2h", 3, 0), ("W", "1", 3), ("S", "1h", 3),
-    ("S", "2", 3, 1), ("S", "2", 3, 2), ("D", "2h", 2, 0), ("S", "3", 4, 0), ("S", "3", 0, 0), ("S", "3", 1, 0),
-    ("W", "d", 5), ("W", "f", 5), ("E", 5), ("D", "2", 2, 1), ("D", "2", 2, 2), ("S", "1", 5), ("D", "1h", 2),
-    ("D", "1h", 3), ("S", "2", 5, 0), ("D", "2h", 1, 2), ("D", "2h", 1, 3), ("D", "2h", 3, 0), ("S", "3", 5, 0),
-    ("C", "tk", 1), ("W", "1h", 2), ("S", "2", 2, 3), ("C", "tk", 2), ("W", "2", 2, 1), ("S", "2h", 2, 1),
-    ("C", "tk", 3), ("D", "1", 4), ("W", "1h", 3), ("S", "2", 3, 3), ("W", "2", 2, 2), ("S", "2h", 2, 2),
-    ("D", "2", 4, 0), ("S", "3", 0, 1), ("C", "tk", 4), ("D", "2", 3, 1), ("S", "3", 2, 1), ("D", "3", 0, 0),
-    ("D", "3", 1, 0), ("S", "3", 1, 1), ("D", "2", 3, 2), ("W", "1", 4), ("S", "1h", 4), ("W", "2", 4, 0),
-    ("S", "2h", 4, 0), ("S", "3", 3, 1), ("S", "2", 4, 1), ("C", "tk", 5), ("W", "2", 3, 1), ("S", "2h", 3, 1),
-    ("W", "2", 3, 2), ("S", "2h", 3, 2), ("D", "2h", 2, 1), ("S", "3", 4, 1), ("S", "2", 4, 2), ("S", "3", 2, 2),
-    ("C", "tk", 6), ("D", "2h", 2, 2), ("D", "3", 4, 0), ("D", "2", 2, 3), ("S", "3", 3, 2), ("D", "2", 3, 3),
-    ("S", "3", 2, 3), ("W", "2", 2, 3), ("S", "2h", 2, 3), ("D", "2h", 3, 1), ("W", "2", 3, 3), ("S", "2h", 3, 3),
-    ("C", "tk", 7), ("D", "3", 3, 1), ("D", "1", 5), ("S", "3", 4, 2), ("D", "2h", 3, 2), ("D", "3", 2, 1),
-    ("S", "3", 2, 4), ("D", "3", 0, 1), ("D", "3", 1, 1), ("D", "2h", 4, 0), ("D", "2", 5, 0), ("S", "3", 0, 2),
-    ("W", "1", 5), ("S", "2", 5, 1), ("D", "2h", 2, 3), ("S", "1h", 5), ("W", "1h", 4), ("S", "2", 4, 3),
-    ("D", "3", 3, 2), ("S", "3", 3, 3), ("W", "2h", 4, 0), ("S", "3", 4, 3), ("C", "sq", 0), ("D", "2", 4, 1),
-    ("W", "2", 5, 0), ("S", "2h", 5, 0), ("D", "1h", 4), ("D", "3", 5, 0), ("D", "2h", 3, 3), ("D", "3", 2, 2),
-    ("D", "3", 2, 3), ("S", "3", 5, 1), ("C", "sq", 1), ("D", "3", 0, 2), ("D", "2", 4, 2), ("W", "2", 4, 1),
-    ("S", "2h", 4, 1), ("D", "3", 4, 1), ("D", "1h", 5), ("S", "3", 3, 4), ("S", "2", 5, 2), ("S", "3", 5, 2),
-    ("C", "sq", 2), ("D", "3", 2, 4), ("S", "3", 2, 5), ("W", "2", 4, 2), ("S", "2h", 4, 2), ("W", "1h", 5),
-    ("S", "2", 5, 3), ("D", "3", 3, 3), ("D", "3", 4, 2), ("D", "3", 4, 3), ("S", "3", 3, 5), ("W", "3", 3, 0),
-    ("W", "3", 3, 1), ("W", "3", 3, 2), ("W", "3", 3, 3), ("W", "3", 4, 0), ("W", "3", 4, 1), ("W", "3", 4, 2),
-    ("W", "3", 4, 3), ("C", "mm", 2, 0, "near"), ("D", "2h", 5, 0), ("D", "2", 5, 1), ("D", "2h", 4, 1),
-    ("D", "2", 4, 3), ("D", "2h", 4, 2), ("W", "2", 5, 1), ("S", "2h", 5, 1), ("W", "2", 4, 3), ("S", "2h", 4, 3),
-    ("D", "3", 5, 1), ("D", "3", 5, 2), ("W", "2h", 5, 0), ("S", "3", 5, 3), ("D", "3", 3, 4), ("W", "2h", 4, 1),
-    ("S", "3", 4, 4), ("W", "2h", 2, 0), ("W", "2h", 2, 1), ("W", "2h", 2, 2), ("W", "2h", 2, 3), ("S", "3", 2, 6),
-    ("S", "3", 1, 2), ("D", "2", 5, 2), ("S", "3", 0, 3), ("W", "2", 5, 2), ("S", "2h", 5, 2), ("S", "3", 1, 3),
-    ("D", "3", 2, 5), ("D", "3", 5, 3), ("W", "3", 2, 0), ("W", "3", 2, 1), ("W", "3", 2, 2), ("W", "3", 2, 3),
-    ("S", "3h", 2, 0), ("D", "2", 5, 3), ("D", "2h", 5, 1), ("D", "2h", 4, 3), ("S", "3", 0, 4), ("W", "2h", 5, 1),
-    ("S", "3", 5, 4), ("W", "3", 5, 0), ("W", "3", 5, 1), ("W", "3", 5, 2), ("W", "3", 5, 3),
-    ("C", "mm", 1, 0, "near"), ("D", "3", 1, 2), ("D", "3", 0, 3), ("D", "2h", 5, 2), ("D", "3", 1, 3),
-    ("W", "2", 5, 3), ("S", "2h", 5, 3), ("D", "3", 3, 5), ("W", "2h", 4, 2), ("S", "3", 4, 5), ("S", "3", 1, 4),
-    ("W", "3", 3, 4), ("W", "3", 4, 4), ("C", "mm", 2, 1, "near"), ("D", "2h", 5, 3), ("D", "3", 0, 4),
-    ("S", "3", 0, 5), ("D", "3", 2, 6), ("D", "3h", 2, 0), ("W", "2h", 5, 2), ("S", "3", 5, 5), ("D", "3", 4, 4),
-    ("W", "2h", 3, 0), ("W", "2h", 3, 1), ("W", "2h", 3, 2), ("W", "2h", 3, 3), ("S", "3", 3, 6), ("D", "3", 1, 4),
-    ("S", "3", 1, 5), ("W", "3", 2, 4), ("W", "3", 5, 4), ("C", "mm", 1, 1, "near"), ("D", "3", 4, 5),
-    ("W", "2h", 4, 3), ("S", "3", 4, 6), ("W", "2h", 0, 0), ("W", "2h", 0, 1), ("W", "2h", 0, 2), ("W", "2h", 0, 3),
-    ("S", "3", 0, 6), ("D", "3", 5, 4), ("W", "2h", 5, 3), ("S", "3", 5, 6), ("W", "3", 3, 5), ("W", "3", 4, 5),
-    ("C", "mm", 2, 2, "near"), ("D", "3", 0, 5), ("W", "2h", 1, 0), ("W", "2h", 1, 1), ("W", "2h", 1, 2),
-    ("W", "2h", 1, 3), ("S", "3", 1, 6), ("D", "3", 3, 6), ("S", "3h", 3, 0), ("W", "3", 2, 5), ("W", "3", 5, 5),
-    ("C", "mm", 1, 2, "near"), ("D", "3", 1, 5), ("D", "3", 0, 6), ("W", "3", 0, 0), ("W", "3", 0, 1),
-    ("W", "3", 0, 2), ("W", "3", 0, 3), ("S", "3h", 0, 0), ("S", "3h", 4, 0), ("D", "3", 5, 5), ("S", "3h", 5, 0),
-    ("W", "3", 1, 0), ("W", "3", 1, 1), ("W", "3", 1, 2), ("W", "3", 1, 3), ("S", "3h", 1, 0), ("W", "3", 0, 4),
-    ("S", "3h", 0, 1), ("D", "3", 4, 6), ("D", "3h", 3, 0), ("S", "3h", 3, 1), ("D", "3", 5, 6), ("S", "3h", 2, 1),
-    ("W", "3", 3, 6), ("W", "3", 4, 6), ("C", "mm", 2, 3, "near"), ("D", "3", 1, 6), ("D", "3h", 0, 0),
-    ("W", "3", 1, 4), ("S", "3h", 1, 1), ("S", "3h", 4, 1), ("S", "3h", 5, 1), ("W", "3", 2, 6), ("W", "3", 5, 6),
-    ("C", "mm", 1, 3, "near"), ("D", "3h", 1, 0), ("D", "3h", 0, 1), ("W", "3", 0, 5), ("S", "3h", 0, 2),
-    ("W", "3h", 0, 0), ("W", "3h", 1, 0), ("C", "mm", 0, 0, "all"), ("W", "3", 1, 5), ("S", "3h", 1, 2),
-    ("D", "3h", 4, 0), ("D", "3h", 3, 1), ("S", "3h", 3, 2), ("D", "3h", 5, 0), ("D", "3h", 2, 1), ("S", "3h", 2, 2),
-    ("W", "3h", 2, 0), ("W", "3h", 5, 0), ("C", "mm", 1, 0, "far"), ("W", "3h", 3, 0), ("W", "3h", 4, 0),
-    ("C", "mm", 2, 0, "far"), ("D", "3h", 1, 1), ("W", "3", 0, 6), ("S", "3h", 0, 3), ("S", "3h", 4, 2),
-    ("S", "3h", 5, 2), ("W", "3h", 0, 1), ("W", "3h", 1, 1), ("C", "mm", 0, 1, "all"), ("D", "3h", 0, 2),
-    ("W", "3", 1, 6), ("S", "3h", 1, 3), ("W", "3h", 3, 1), ("W", "3h", 4, 1), ("C", "mm", 2, 1, "far"),
-    ("D", "3h", 4, 1), ("D", "3h", 3, 2), ("S", "3h", 3, 3), ("D", "3h", 5, 1), ("D", "3h", 2, 2), ("S", "3h", 2, 3),
-    ("W", "3h", 2, 1), ("W", "3h", 5, 1), ("C", "mm", 1, 1, "far"), ("S", "3h", 4, 3), ("W", "3h", 0, 2),
-    ("W", "3h", 1, 2), ("C", "mm", 0, 2, "all"), ("S", "3h", 5, 3), ("W", "3h", 0, 3), ("W", "3h", 1, 3),
-    ("C", "mm", 0, 3, "all"), ("W", "3h", 2, 2), ("W", "3h", 5, 2), ("C", "mm", 1, 2, "far"), ("W", "3h", 3, 2),
-    ("W", "3h", 4, 2), ("C", "mm", 2, 2, "far"), ("C", "fin", 0), ("W", "3h", 3, 3), ("W", "3h", 4, 3),
-    ("C", "mm", 2, 3, "far"), ("W", "3h", 2, 3), ("W", "3h", 5, 3), ("C", "mm", 1, 3, "far"), ("C", "fin", 1),
-    ("C", "fin", 2),
+    ("S", "r", 0), ("S", "d", 0), ("S", "r", 1), ("D", "r", 0), ("S", "d", 1), ("D", "d", 0), ("S", "r", 2),
+    ("W", "d", 0), ("W", "r", 0), ("E", 0), ("S", "1", 0), ("S", "2", 0, 0), ("D", "r", 1), ("D", "d", 1),
+    ("D", "r", 2), ("S", "d", 2), ("S", "r", 3), ("W", "d", 1), ("W", "r", 1), ("E", 1), ("D", "1", 0),
+    ("S", "2", 1, 0), ("D", "2", 0, 0), ("S", "1", 1), ("W", "r", 2), ("S", "f", 2), ("D", "d", 2), ("D", "r", 3),
+    ("S", "d", 3), ("W", "1", 0), ("S", "1h", 0), ("W", "2", 0, 0), ("S", "2h", 0, 0), ("S", "2", 0, 1),
+    ("S", "2", 0, 2), ("D", "f", 2), ("W", "r", 3), ("S", "f", 3), ("S", "r", 4), ("W", "d", 2), ("W", "f", 2),
+    ("E", 2), ("D", "2", 1, 0), ("D", "1h", 0), ("W", "2", 1, 0), ("S", "2h", 1, 0), ("D", "d", 3), ("D", "f", 3),
+    ("S", "d", 4), ("W", "1", 1), ("S", "2", 1, 1), ("D", "1", 1), ("D", "2h", 0, 0), ("S", "1h", 1), ("W", "1h", 0),
+    ("S", "2", 0, 3), ("D", "2h", 1, 0), ("S", "2", 1, 2), ("D", "2", 0, 1), ("D", "2", 0, 2), ("S", "2", 2, 0),
+    ("S", "3", 2, 0), ("W", "d", 3), ("W", "f", 3), ("E", 3), ("D", "r", 4), ("W", "r", 4), ("S", "f", 4),
+    ("D", "1h", 1), ("W", "2", 0, 1), ("S", "2h", 0, 1), ("D", "2", 1, 1), ("S", "2", 3, 0), ("W", "2", 0, 2),
+    ("S", "2h", 0, 2), ("S", "3", 3, 0), ("D", "d", 4), ("S", "r", 5), ("W", "1h", 1), ("S", "2", 1, 3),
+    ("W", "2", 1, 1), ("S", "2h", 1, 1), ("S", "d", 5), ("D", "f", 4), ("S", "1", 2), ("S", "1", 3), ("W", "d", 4),
+    ("W", "f", 4), ("E", 4), ("D", "2", 0, 3), ("D", "2h", 0, 1), ("D", "2", 2, 0), ("D", "2h", 0, 2),
+    ("D", "3", 3, 0), ("S", "1", 4), ("D", "2", 1, 2), ("D", "3", 2, 0), ("D", "2h", 1, 1), ("D", "2", 3, 0),
+    ("D", "2", 1, 3), ("W", "2", 1, 2), ("S", "2h", 1, 2), ("W", "2", 0, 3), ("S", "2h", 0, 3), ("W", "2", 2, 0),
+    ("S", "2h", 2, 0), ("D", "2h", 1, 2), ("W", "2", 3, 0), ("S", "2h", 3, 0), ("W", "2", 1, 3), ("S", "2h", 1, 3),
+    ("S", "3", 4, 0), ("C", "tk", 0), ("C", "tk", 1), ("D", "r", 5), ("D", "1", 2), ("D", "1", 3), ("W", "r", 5),
+    ("S", "f", 5), ("S", "2", 4, 0), ("D", "2h", 0, 3), ("D", "2h", 2, 0), ("W", "1", 2), ("S", "2", 2, 1),
+    ("S", "2", 2, 2), ("D", "2h", 3, 0), ("D", "2h", 1, 3), ("W", "1", 3), ("S", "2", 3, 1), ("S", "2", 3, 2),
+    ("S", "1h", 2), ("D", "d", 5), ("S", "1h", 3), ("S", "3", 3, 1), ("C", "tk", 2), ("D", "1", 4), ("S", "3", 3, 2),
+    ("S", "3", 2, 1), ("W", "1", 4), ("S", "2", 4, 1), ("S", "1h", 4), ("S", "2", 4, 2), ("S", "3", 2, 2),
+    ("C", "tk", 3), ("W", "d", 5), ("W", "f", 5), ("E", 5), ("D", "2", 2, 1), ("D", "2", 2, 2), ("W", "2", 2, 1),
+    ("S", "2h", 2, 1), ("D", "2", 3, 1), ("D", "3", 4, 0), ("D", "2", 3, 2), ("S", "1", 5), ("D", "3", 3, 1),
+    ("W", "2", 2, 2), ("S", "2h", 2, 2), ("W", "1h", 2), ("S", "2", 2, 3), ("D", "3", 2, 1), ("W", "2", 3, 1),
+    ("S", "2h", 3, 1), ("D", "f", 5), ("D", "1h", 2), ("D", "1h", 3), ("S", "2", 5, 0), ("D", "3", 2, 2),
+    ("W", "2", 3, 2), ("S", "2h", 3, 2), ("W", "1h", 3), ("S", "2", 3, 3), ("D", "3", 3, 2), ("D", "1h", 4),
+    ("S", "3", 5, 0), ("C", "tk", 4), ("D", "2", 4, 0), ("W", "1h", 4), ("S", "2", 4, 3), ("C", "tk", 5),
+    ("W", "2", 4, 0), ("S", "2h", 4, 0), ("D", "2h", 2, 1), ("D", "2h", 2, 2), ("S", "3", 3, 3), ("D", "2h", 3, 1),
+    ("S", "3", 4, 1), ("C", "tk", 6), ("D", "2", 2, 3), ("W", "2", 2, 3), ("S", "2h", 2, 3), ("D", "2h", 3, 2),
+    ("S", "3", 4, 2), ("D", "2", 4, 1), ("D", "2", 4, 2), ("W", "2", 4, 1), ("S", "2h", 4, 1), ("D", "2", 3, 3),
+    ("D", "1", 5), ("W", "2", 3, 3), ("S", "2h", 3, 3), ("W", "2", 4, 2), ("S", "2h", 4, 2), ("D", "3", 3, 3),
+    ("D", "2h", 2, 3), ("D", "3", 5, 0), ("S", "3", 3, 4), ("C", "tk", 7), ("W", "1", 5), ("S", "1h", 5),
+    ("S", "2", 5, 1), ("D", "2h", 4, 0), ("S", "2", 5, 2), ("D", "2h", 3, 3), ("S", "3", 2, 3), ("S", "3", 3, 5),
+    ("W", "2h", 4, 0), ("S", "3", 4, 3), ("D", "2", 5, 0), ("W", "2", 5, 0), ("S", "2h", 5, 0), ("D", "3", 4, 1),
+    ("D", "1h", 5), ("S", "3", 2, 4), ("D", "2h", 4, 1), ("W", "1h", 5), ("S", "2", 5, 3), ("D", "2h", 4, 2),
+    ("D", "2", 4, 3), ("W", "2", 4, 3), ("S", "2h", 4, 3), ("D", "3", 3, 4), ("S", "3", 5, 1), ("D", "3", 4, 2),
+    ("D", "3", 2, 3), ("S", "3", 5, 2), ("D", "3", 4, 3), ("W", "2h", 4, 1), ("S", "3", 4, 4), ("S", "3", 0, 0),
+    ("W", "3", 2, 0), ("W", "3", 2, 1), ("W", "3", 2, 2), ("W", "3", 2, 3), ("W", "3", 4, 0), ("W", "3", 4, 1),
+    ("W", "3", 4, 2), ("W", "3", 4, 3), ("C", "mm", 1, 0, "near"), ("D", "2h", 5, 0), ("D", "2", 5, 1),
+    ("D", "2", 5, 2), ("D", "2h", 4, 3), ("W", "2", 5, 1), ("S", "2h", 5, 1), ("W", "2", 5, 2), ("S", "2h", 5, 2),
+    ("D", "3", 3, 5), ("D", "3", 5, 1), ("D", "3", 5, 2), ("W", "2h", 5, 0), ("S", "3", 5, 3), ("C", "sq", 0),
+    ("W", "2h", 3, 0), ("W", "2h", 3, 1), ("W", "2h", 3, 2), ("W", "2h", 3, 3), ("S", "3", 3, 6), ("D", "3", 0, 0),
+    ("D", "2", 5, 3), ("S", "3", 1, 0), ("S", "3", 0, 1), ("W", "2", 5, 3), ("S", "2h", 5, 3), ("C", "sq", 1),
+    ("C", "sq", 2), ("D", "2h", 5, 1), ("D", "2h", 5, 2), ("S", "3", 1, 1), ("D", "3", 2, 4), ("D", "3", 5, 3),
+    ("W", "2h", 5, 1), ("S", "3", 5, 4), ("S", "3", 0, 2), ("S", "3", 2, 5), ("S", "3", 1, 2), ("W", "3", 3, 0),
+    ("W", "3", 3, 1), ("W", "3", 3, 2), ("W", "3", 3, 3), ("W", "3", 5, 0), ("W", "3", 5, 1), ("W", "3", 5, 2),
+    ("W", "3", 5, 3), ("C", "mm", 2, 0, "near"), ("D", "3", 1, 0), ("D", "3", 0, 1), ("D", "2h", 5, 3),
+    ("S", "3", 0, 3), ("S", "3", 1, 3), ("D", "3", 1, 1), ("S", "3", 0, 4), ("D", "3", 4, 4), ("W", "2h", 4, 2),
+    ("S", "3", 4, 5), ("W", "3", 2, 4), ("W", "3", 4, 4), ("C", "mm", 1, 1, "near"), ("D", "3", 3, 6),
+    ("D", "3", 0, 2), ("D", "3", 1, 2), ("W", "2h", 5, 2), ("S", "3", 5, 5), ("D", "3", 0, 3), ("D", "3", 1, 3),
+    ("W", "3", 0, 0), ("W", "3", 0, 1), ("W", "3", 0, 2), ("W", "3", 0, 3), ("S", "3h", 0, 0), ("D", "3", 2, 5),
+    ("W", "3", 1, 0), ("W", "3", 1, 1), ("W", "3", 1, 2), ("W", "3", 1, 3), ("S", "3h", 1, 0), ("D", "3", 0, 4),
+    ("S", "3", 1, 4), ("W", "2h", 2, 0), ("W", "2h", 2, 1), ("W", "2h", 2, 2), ("W", "2h", 2, 3), ("S", "3", 2, 6),
+    ("W", "3", 3, 4), ("W", "3", 5, 4), ("C", "mm", 2, 1, "near"), ("D", "3", 5, 4), ("D", "3h", 0, 0),
+    ("W", "2h", 5, 3), ("S", "3", 5, 6), ("D", "3h", 1, 0), ("W", "3", 0, 4), ("S", "3h", 0, 1), ("D", "3", 4, 5),
+    ("W", "2h", 4, 3), ("S", "3", 4, 6), ("W", "3", 2, 5), ("W", "3", 4, 5), ("C", "mm", 1, 2, "near"),
+    ("S", "3", 0, 5), ("W", "3h", 0, 0), ("W", "3h", 1, 0), ("C", "mm", 0, 0, "all"), ("W", "3", 3, 5),
+    ("W", "3", 5, 5), ("C", "mm", 2, 2, "near"), ("D", "3", 1, 4), ("D", "3h", 0, 1), ("W", "3", 1, 4),
+    ("S", "3h", 1, 1), ("D", "3", 2, 6), ("D", "3", 5, 5), ("S", "3h", 3, 0), ("S", "3", 1, 5), ("S", "3h", 2, 0),
+    ("S", "3h", 5, 0), ("S", "3h", 4, 0), ("D", "3", 0, 5), ("D", "3h", 1, 1), ("W", "3", 0, 5), ("S", "3h", 0, 2),
+    ("W", "3h", 0, 1), ("W", "3h", 1, 1), ("C", "mm", 0, 1, "all"), ("D", "3", 5, 6), ("D", "3h", 3, 0),
+    ("S", "3h", 3, 1), ("W", "2h", 0, 0), ("W", "2h", 0, 1), ("W", "2h", 0, 2), ("W", "2h", 0, 3), ("S", "3", 0, 6),
+    ("D", "3", 4, 6), ("D", "3h", 2, 0), ("S", "3h", 2, 1), ("W", "3", 2, 6), ("W", "3", 4, 6),
+    ("C", "mm", 1, 3, "near"), ("S", "3h", 5, 1), ("S", "3h", 4, 1), ("W", "3", 3, 6), ("W", "3", 5, 6),
+    ("C", "mm", 2, 3, "near"), ("D", "3", 1, 5), ("D", "3h", 0, 2), ("W", "3", 1, 5), ("S", "3h", 1, 2),
+    ("W", "3h", 2, 0), ("W", "3h", 4, 0), ("C", "mm", 1, 0, "far"), ("D", "3h", 5, 0), ("D", "3h", 3, 1),
+    ("S", "3h", 3, 2), ("D", "3", 0, 6), ("W", "2h", 1, 0), ("W", "2h", 1, 1), ("W", "2h", 1, 2), ("W", "2h", 1, 3),
+    ("S", "3", 1, 6), ("D", "3h", 4, 0), ("D", "3h", 2, 1), ("S", "3h", 2, 2), ("W", "3h", 3, 0), ("W", "3h", 5, 0),
+    ("C", "mm", 2, 0, "far"), ("S", "3h", 5, 2), ("S", "3h", 4, 2), ("W", "3h", 2, 1), ("W", "3h", 4, 1),
+    ("C", "mm", 1, 1, "far"), ("D", "3h", 1, 2), ("W", "3", 0, 6), ("S", "3h", 0, 3), ("W", "3h", 0, 2),
+    ("W", "3h", 1, 2), ("C", "mm", 0, 2, "all"), ("D", "3h", 5, 1), ("D", "3h", 3, 2), ("S", "3h", 3, 3),
+    ("D", "3h", 4, 1), ("D", "3h", 2, 2), ("S", "3h", 2, 3), ("W", "3h", 3, 1), ("W", "3h", 5, 1),
+    ("C", "mm", 2, 1, "far"), ("D", "3", 1, 6), ("D", "3h", 0, 3), ("W", "3", 1, 6), ("S", "3h", 1, 3),
+    ("D", "3h", 5, 2), ("S", "3h", 5, 3), ("D", "3h", 4, 2), ("S", "3h", 4, 3), ("W", "3h", 2, 2), ("W", "3h", 4, 2),
+    ("C", "mm", 1, 2, "far"), ("W", "3h", 3, 2), ("W", "3h", 5, 2), ("C", "mm", 2, 2, "far"), ("W", "3h", 0, 3),
+    ("W", "3h", 1, 3), ("C", "mm", 0, 3, "all"), ("W", "3h", 2, 3), ("W", "3h", 4, 3), ("C", "mm", 1, 3, "far"),
+    ("W", "3h", 3, 3), ("W", "3h", 5, 3), ("C", "mm", 2, 3, "far"), ("C", "fin", 1), ("C", "fin", 2), ("C", "fin", 0),
+    ("D", "3h", 1, 3), ("D", "3h", 3, 3), ("D", "3h", 2, 3), ("D", "3h", 5, 3), ("D", "3h", 4, 3),
 )
 
 THRESH = ((0.25, 0.5), (0.75, 1.0), (1.25, 1.5), (1.75, 2.0), (2.5, 3.0), (3.5, 4.0), (5.0, 6.0))
@@ -115,7 +116,7 @@
 def kernel(
     tokens, gain, frag, exps, base, mom,
     nb, nm, kv,
-    w0, w1, w2, tok, acc, fv, fb, rl, bs, ms, gb, gf, gn, ex, eb, er, erl, sc, iv, ss,
+    w0, w1, w2, tok, acc, fv, fb, rl, bs, ms, gb, gf, gn, ex, eb, er, sc, iv, ss,
     loc, a_snd, a_rcv, e_snd, e_rcv, t_snd, t_rcv, g_snd, g_rcv,
 ):
     W = (w0, w1, w2)
@@ -182,7 +183,7 @@
         pick = jnp.where(j == lax.div(n + lo, BLOCK), 1.0, 0.0).astype(BF16)
         for slot in range(4):
             if slot == 3 and once("far exponents"):
-                e_cp[3].wait_recv()
+                e_cp[0].wait_recv()
             e = (window(rep)[...] if slot == 0 else er[slot]).astype(F32)
             for ref, sign in ((sc, 1.0), (iv, -1.0)):
                 small = jnp.exp2(sign * e).astype(BF16)
@@ -190,10 +191,9 @@
                 ref[slot, :, pl.ds(lo, width)] = full.astype(BF16)
 
     e_cp = [
-        remote(window(zo), erl, e_snd.at[0], e_rcv.at[0], up),
+        remote(window(zo), er.at[3], e_snd.at[0], e_rcv.at[0], nbr("z", 2)),
         remote(window(zu), er.at[1], e_snd.at[1], e_rcv.at[1], up),
         remote(window(zd), er.at[2], e_snd.at[2], e_rcv.at[2], down),
-        remote(erl, er.at[3], e_snd.at[3], e_rcv.at[3], up),
     ]
 
     def cols(p):
@@ -225,7 +225,7 @@
     def early():
         l_ex.wait()
         eb[...] = ex[...].astype(F32).astype(BF16)
-        for m in e_cp[:3]:
+        for m in e_cp:
             go(m)
         l_gn.wait()
         gf[...] = gb[...].astype(F32)
@@ -236,8 +236,6 @@
             row = jnp.broadcast_to(gf[pl.ds(first + h, 1), :], (128, 128))
             column = jnp.sum(jnp.where(i == l, row, 0.0), axis=1, keepdims=True)
             gn[pl.ds(128 * h, 128), :] = jnp.broadcast_to(column, (128, 128))
-        e_cp[0].wait_recv()
-        go(e_cp[3])
 
     def prepare():
         for s in (1, 2):
@@ -330,7 +328,7 @@
             if i:
                 M["3", p, 3 + i] = full(p, l, **{R: mod4(pos[R] + OFF[i])})
 
-    def mm(c, count, coords):
+    def mm(c, count, coords, last=False):
         lo, width = CLS[c]
         cc = pl.ds(lo, width)
 
@@ -340,7 +338,13 @@
 
             def block(m, carry):
                 mr = pl.ds(pl.multiple_of(m * TOK, TOK), TOK)
-                acc[mr, cc] += jnp.dot(tok[mr, kk], W[c][yy, xx], preferred_element_type=F32)
+                total = acc[mr, cc] + jnp.dot(tok[mr, kk], W[c][yy, xx], preferred_element_type=F32)
+                if last:
+                    for k in range(width // 128):
+                        part = total[:, 128 * k : 128 * (k + 1)] * ss[mr, :]
+                        kv[mr, pl.ds(lo + 128 * k, 128)] = part.astype(BF16)
+                else:
+                    acc[mr, cc] = total
                 return carry
 
             return lax.fori_loop(0, 2, block, carry)
@@ -358,11 +362,11 @@
             xx = mod4(pos["x"] + OFF[i])
             mm(c, 3, lambda t: (mod4(pos["y"] + offset(t)), xx))
 
-    def mm_far(c, i):
+    def mm_far(c, i, last):
         if c == 1:
-            mm(c, 1, lambda t: (mod4(pos["y"] + OFF[i]), mod4(pos["x"] + 2)))
+            mm(c, 1, lambda t: (mod4(pos["y"] + OFF[i]), mod4(pos["x"] + 2)), last)
         else:
-            mm(c, 1, lambda t: (mod4(pos["y"] + 2), mod4(pos["x"] + OFF[i])))
+            mm(c, 1, lambda t: (mod4(pos["y"] + 2), mod4(pos["x"] + OFF[i])), last)
 
     same = len({p[3] for p in PARTS if p[0] == 0}) == 1
 
@@ -407,7 +411,13 @@
 
     s_cp = remote(ss.at[mine, :], ss.at[mine, :], t_snd.at[8], t_rcv.at[8], other)
     left = []
-    for kind, *key in SCHEDULE:
+    def own_tokens():
+        if once("own tokens"):
+            for t in l_tk:
+                t.wait()
+
+    finished = set()
+    for at, (kind, *key) in enumerate(SCHEDULE):
         key = tuple(key)
         if kind == "S":
             for m in M[key]:
@@ -436,21 +446,30 @@
             if once("total"):
                 acc[...] = jnp.zeros_like(acc)
         elif key[0] == "sq":
-            if once("own tokens"):
-                for t in l_tk:
-                    t.wait()
+            own_tokens()
             squares(key[1])
             if key[1] == 2:
                 go(s_cp)
         elif key[0] == "fin":
-            if once("factors"):
-                s_cp.wait_recv()
-            finish(key[1])
+            if key[1] not in finished:
+                if once("factors"):
+                    s_cp.wait_recv()
+                finish(key[1])
         else:
+            own_tokens()
             if once("all tokens"):
                 for t in t_cp:
                     t.wait_recv()
-            {"near": mm_near, "far": mm_far, "all": mm_row if same else mm_level}[key[3]](key[1], key[2])
+            c, i, how = key[1:]
+            if how == "far":
+                last = at == max(n for n, row in enumerate(SCHEDULE) if row[:3] == ("C", "mm", c))
+                if last:
+                    finished.add(c)
+                    if once("factors"):
+                        s_cp.wait_recv()
+                mm_far(c, i, last)
+            else:
+                {"near": mm_near, "all": mm_row if same else mm_level}[how](c, i)
     for key in left:
         for m in M[key]:
             m.wait_send()
@@ -483,15 +502,14 @@
             vm((BLOCK, 4 * ROWS), jnp.int32),
             vm((BLOCK, 4 * ROWS), BF16),
             vm((4, BLOCK, 256), BF16),
-            vm((BLOCK, 256), BF16),
             vm((4, 256, KVW), BF16),
             vm((4, 256, KVW), BF16),
             vm((2 * TOK, 128), F32),
             dma((13,)),
             dma((6 * len(PARTS),)),
             dma((6 * len(PARTS),)),
-            dma((4,)),
-            dma((4,)),
+            dma((3,)),
+            dma((3,)),
             dma((9,)),
             dma((9,)),
             dma((42 * len(PARTS),)),

time: 131 us -> 130 us (level)
  Pallas kernels: 128 us -> 126 us
    pallas_call x1, Pallas kernels: 128 us -> 126 us  [body(): pl.pallas_call(kernel, out_shape=(vm((ROWS, KVW), F32), vm((ROWS, KVW), F...]
where the time goes in v10:
time: 130 us
  Pallas kernels  126 us (97%)
  local copies, waits for them, and re-layouts  2.9 us (2%)
    pallas_call x1, Pallas kernels, body(): pl.pallas_call(kernel, out_shape=(vm((ROWS, KVW), F32), vm((ROWS, KVW), F...  126 us
    unnamed x3, local copies, waits for them, and re-layouts  2.9 us

profile of v10, /device:TPU:0, one launch (start us, length us, event | category | flops | bytes accessed | tf_op | source)
XLA Modules:
  0.0 129.9 jit_solution(1001903194342454613)
XLA Ops:
  0.6 126.4 %shard_map.85 = (f32[192,1024]{1,0:T(8,128)S(1)}, f32[192,1024]{1,0:T(8,128)S(1)}, bf16[768,1024]{1,0:T(8,128)(2,1)S(1)}) custom-call(bf16[384,12288]{1,0:T(8,128)(2,1)} %tokens.1, bf16[96,128]{1,0:T(8,128)(2,1)} %bitcast.7, bf16[4,192,1024]{2,1,0:T(8,128)(2,1)} %bitcast.5, s32[32,768]{1,0:T(8,128)} %bitcast.6, f32[192,1024]{1,0:T(8,128)} %base.1, ...), custom_call_target="tpu_custom_call" | custom-call | flops 19327352832 | bytes 30000000 | tf_op jit(solution)/shard_map/pallas_call | solution.py:485
  127.0 0.9 copy.12
  127.9 0.9 copy.13
  128.8 1.1 copy.14

commit v11 on v10

--- a/solution.py
+++ b/solution.py
@@ -17,10 +17,10 @@
 PARTS = (
     (0, 0, 128, ("x", "y", "z")),
     (0, 128, 128, ("y", "x", "z")),
+    (2, 0, 128, ("z", "x", "y")),
     (1, 0, 128, ("z", "y", "x")),
-    (2, 0, 128, ("z", "x", "y")),
+    (2, 128, 256, ("x", "z", "y")),
     (1, 128, 256, ("y", "z", "x")),
-    (2, 128, 256, ("x", "z", "y")),
 )
 
 DIRECT = 2
@@ -28,82 +28,82 @@
     ("S", "r", 0), ("S", "d", 0), ("S", "r", 1), ("D", "r", 0), ("S", "d", 1), ("D", "d", 0), ("S", "r", 2),
     ("W", "d", 0), ("W", "r", 0), ("E", 0), ("S", "1", 0), ("S", "2", 0, 0), ("D", "r", 1), ("D", "d", 1),
     ("D", "r", 2), ("S", "d", 2), ("S", "r", 3), ("W", "d", 1), ("W", "r", 1), ("E", 1), ("D", "1", 0),
-    ("S", "2", 1, 0), ("D", "2", 0, 0), ("S", "1", 1), ("W", "r", 2), ("S", "f", 2), ("D", "d", 2), ("D", "r", 3),
+    ("S", "2", 1, 0), ("D", "2", 0, 0), ("S", "1", 1), ("W", "r", 2), ("S", "f", 2), ("D", "r", 3), ("D", "d", 2),
     ("S", "d", 3), ("W", "1", 0), ("S", "1h", 0), ("W", "2", 0, 0), ("S", "2h", 0, 0), ("S", "2", 0, 1),
     ("S", "2", 0, 2), ("D", "f", 2), ("W", "r", 3), ("S", "f", 3), ("S", "r", 4), ("W", "d", 2), ("W", "f", 2),
     ("E", 2), ("D", "2", 1, 0), ("D", "1h", 0), ("W", "2", 1, 0), ("S", "2h", 1, 0), ("D", "d", 3), ("D", "f", 3),
     ("S", "d", 4), ("W", "1", 1), ("S", "2", 1, 1), ("D", "1", 1), ("D", "2h", 0, 0), ("S", "1h", 1), ("W", "1h", 0),
-    ("S", "2", 0, 3), ("D", "2h", 1, 0), ("S", "2", 1, 2), ("D", "2", 0, 1), ("D", "2", 0, 2), ("S", "2", 2, 0),
+    ("S", "2", 0, 3), ("D", "2h", 1, 0), ("S", "2", 1, 2), ("S", "2", 2, 0), ("D", "2", 0, 1), ("D", "2", 0, 2),
     ("S", "3", 2, 0), ("W", "d", 3), ("W", "f", 3), ("E", 3), ("D", "r", 4), ("W", "r", 4), ("S", "f", 4),
-    ("D", "1h", 1), ("W", "2", 0, 1), ("S", "2h", 0, 1), ("D", "2", 1, 1), ("S", "2", 3, 0), ("W", "2", 0, 2),
-    ("S", "2h", 0, 2), ("S", "3", 3, 0), ("D", "d", 4), ("S", "r", 5), ("W", "1h", 1), ("S", "2", 1, 3),
-    ("W", "2", 1, 1), ("S", "2h", 1, 1), ("S", "d", 5), ("D", "f", 4), ("S", "1", 2), ("S", "1", 3), ("W", "d", 4),
-    ("W", "f", 4), ("E", 4), ("D", "2", 0, 3), ("D", "2h", 0, 1), ("D", "2", 2, 0), ("D", "2h", 0, 2),
-    ("D", "3", 3, 0), ("S", "1", 4), ("D", "2", 1, 2), ("D", "3", 2, 0), ("D", "2h", 1, 1), ("D", "2", 3, 0),
-    ("D", "2", 1, 3), ("W", "2", 1, 2), ("S", "2h", 1, 2), ("W", "2", 0, 3), ("S", "2h", 0, 3), ("W", "2", 2, 0),
-    ("S", "2h", 2, 0), ("D", "2h", 1, 2), ("W", "2", 3, 0), ("S", "2h", 3, 0), ("W", "2", 1, 3), ("S", "2h", 1, 3),
-    ("S", "3", 4, 0), ("C", "tk", 0), ("C", "tk", 1), ("D", "r", 5), ("D", "1", 2), ("D", "1", 3), ("W", "r", 5),
-    ("S", "f", 5), ("S", "2", 4, 0), ("D", "2h", 0, 3), ("D", "2h", 2, 0), ("W", "1", 2), ("S", "2", 2, 1),
-    ("S", "2", 2, 2), ("D", "2h", 3, 0), ("D", "2h", 1, 3), ("W", "1", 3), ("S", "2", 3, 1), ("S", "2", 3, 2),
-    ("S", "1h", 2), ("D", "d", 5), ("S", "1h", 3), ("S", "3", 3, 1), ("C", "tk", 2), ("D", "1", 4), ("S", "3", 3, 2),
-    ("S", "3", 2, 1), ("W", "1", 4), ("S", "2", 4, 1), ("S", "1h", 4), ("S", "2", 4, 2), ("S", "3", 2, 2),
-    ("C", "tk", 3), ("W", "d", 5), ("W", "f", 5), ("E", 5), ("D", "2", 2, 1), ("D", "2", 2, 2), ("W", "2", 2, 1),
-    ("S", "2h", 2, 1), ("D", "2", 3, 1), ("D", "3", 4, 0), ("D", "2", 3, 2), ("S", "1", 5), ("D", "3", 3, 1),
-    ("W", "2", 2, 2), ("S", "2h", 2, 2), ("W", "1h", 2), ("S", "2", 2, 3), ("D", "3", 2, 1), ("W", "2", 3, 1),
-    ("S", "2h", 3, 1), ("D", "f", 5), ("D", "1h", 2), ("D", "1h", 3), ("S", "2", 5, 0), ("D", "3", 2, 2),
-    ("W", "2", 3, 2), ("S", "2h", 3, 2), ("W", "1h", 3), ("S", "2", 3, 3), ("D", "3", 3, 2), ("D", "1h", 4),
-    ("S", "3", 5, 0), ("C", "tk", 4), ("D", "2", 4, 0), ("W", "1h", 4), ("S", "2", 4, 3), ("C", "tk", 5),
-    ("W", "2", 4, 0), ("S", "2h", 4, 0), ("D", "2h", 2, 1), ("D", "2h", 2, 2), ("S", "3", 3, 3), ("D", "2h", 3, 1),
-    ("S", "3", 4, 1), ("C", "tk", 6), ("D", "2", 2, 3), ("W", "2", 2, 3), ("S", "2h", 2, 3), ("D", "2h", 3, 2),
-    ("S", "3", 4, 2), ("D", "2", 4, 1), ("D", "2", 4, 2), ("W", "2", 4, 1), ("S", "2h", 4, 1), ("D", "2", 3, 3),
-    ("D", "1", 5), ("W", "2", 3, 3), ("S", "2h", 3, 3), ("W", "2", 4, 2), ("S", "2h", 4, 2), ("D", "3", 3, 3),
-    ("D", "2h", 2, 3), ("D", "3", 5, 0), ("S", "3", 3, 4), ("C", "tk", 7), ("W", "1", 5), ("S", "1h", 5),
-    ("S", "2", 5, 1), ("D", "2h", 4, 0), ("S", "2", 5, 2), ("D", "2h", 3, 3), ("S", "3", 2, 3), ("S", "3", 3, 5),
-    ("W", "2h", 4, 0), ("S", "3", 4, 3), ("D", "2", 5, 0), ("W", "2", 5, 0), ("S", "2h", 5, 0), ("D", "3", 4, 1),
-    ("D", "1h", 5), ("S", "3", 2, 4), ("D", "2h", 4, 1), ("W", "1h", 5), ("S", "2", 5, 3), ("D", "2h", 4, 2),
-    ("D", "2", 4, 3), ("W", "2", 4, 3), ("S", "2h", 4, 3), ("D", "3", 3, 4), ("S", "3", 5, 1), ("D", "3", 4, 2),
-    ("D", "3", 2, 3), ("S", "3", 5, 2), ("D", "3", 4, 3), ("W", "2h", 4, 1), ("S", "3", 4, 4), ("S", "3", 0, 0),
-    ("W", "3", 2, 0), ("W", "3", 2, 1), ("W", "3", 2, 2), ("W", "3", 2, 3), ("W", "3", 4, 0), ("W", "3", 4, 1),
-    ("W", "3", 4, 2), ("W", "3", 4, 3), ("C", "mm", 1, 0, "near"), ("D", "2h", 5, 0), ("D", "2", 5, 1),
-    ("D", "2", 5, 2), ("D", "2h", 4, 3), ("W", "2", 5, 1), ("S", "2h", 5, 1), ("W", "2", 5, 2), ("S", "2h", 5, 2),
-    ("D", "3", 3, 5), ("D", "3", 5, 1), ("D", "3", 5, 2), ("W", "2h", 5, 0), ("S", "3", 5, 3), ("C", "sq", 0),
-    ("W", "2h", 3, 0), ("W", "2h", 3, 1), ("W", "2h", 3, 2), ("W", "2h", 3, 3), ("S", "3", 3, 6), ("D", "3", 0, 0),
-    ("D", "2", 5, 3), ("S", "3", 1, 0), ("S", "3", 0, 1), ("W", "2", 5, 3), ("S", "2h", 5, 3), ("C", "sq", 1),
-    ("C", "sq", 2), ("D", "2h", 5, 1), ("D", "2h", 5, 2), ("S", "3", 1, 1), ("D", "3", 2, 4), ("D", "3", 5, 3),
-    ("W", "2h", 5, 1), ("S", "3", 5, 4), ("S", "3", 0, 2), ("S", "3", 2, 5), ("S", "3", 1, 2), ("W", "3", 3, 0),
+    ("D", "1h", 1), ("W", "2", 0, 1), ("S", "2h", 0, 1), ("W", "2", 0, 2), ("S", "2h", 0, 2), ("S", "2", 3, 0),
+    ("D", "d", 4), ("S", "r", 5), ("D", "2", 1, 1), ("W", "1h", 1), ("S", "2", 1, 3), ("S", "3", 3, 0),
+    ("W", "2", 1, 1), ("S", "2h", 1, 1), ("S", "d", 5), ("D", "f", 4), ("S", "1", 2), ("S", "1", 3), ("D", "2", 1, 2),
+    ("D", "2", 2, 0), ("W", "2", 1, 2), ("S", "2h", 1, 2), ("D", "2", 0, 3), ("D", "2h", 0, 1), ("D", "3", 2, 0),
+    ("D", "2h", 0, 2), ("W", "2", 0, 3), ("S", "2h", 0, 3), ("W", "2", 2, 0), ("S", "2h", 2, 0), ("W", "d", 4),
+    ("W", "f", 4), ("E", 4), ("D", "2h", 1, 1), ("S", "1", 4), ("D", "2", 3, 0), ("D", "2h", 0, 3), ("W", "2", 3, 0),
+    ("S", "2h", 3, 0), ("S", "3", 4, 0), ("D", "r", 5), ("D", "1", 2), ("D", "1", 3), ("W", "r", 5), ("S", "f", 5),
+    ("D", "2", 1, 3), ("D", "2h", 1, 2), ("D", "3", 3, 0), ("D", "2h", 2, 0), ("W", "2", 1, 3), ("S", "2h", 1, 3),
+    ("S", "2", 4, 0), ("W", "1", 2), ("S", "2", 2, 1), ("D", "2h", 3, 0), ("W", "1", 3), ("S", "2", 3, 1),
+    ("S", "2", 3, 2), ("S", "2", 2, 2), ("D", "d", 5), ("S", "1h", 2), ("S", "1h", 3), ("S", "3", 2, 1),
+    ("D", "2h", 1, 3), ("S", "3", 3, 1), ("C", "tk", 0), ("D", "3", 4, 0), ("S", "3", 2, 2), ("S", "3", 0, 0),
+    ("D", "1", 4), ("S", "3", 3, 2), ("C", "tk", 1), ("D", "f", 5), ("D", "1h", 2), ("D", "1h", 3), ("W", "1", 4),
+    ("S", "2", 4, 1), ("S", "1h", 4), ("S", "2", 4, 2), ("W", "d", 5), ("W", "f", 5), ("E", 5), ("D", "2", 3, 1),
+    ("D", "2", 3, 2), ("D", "3", 2, 1), ("S", "1", 5), ("D", "2", 2, 1), ("D", "2", 2, 2), ("W", "2", 2, 1),
+    ("S", "2h", 2, 1), ("W", "1h", 2), ("S", "2", 2, 3), ("D", "3", 2, 2), ("W", "2", 3, 1), ("S", "2h", 3, 1),
+    ("W", "2", 3, 2), ("S", "2h", 3, 2), ("D", "3", 3, 1), ("W", "2", 2, 2), ("S", "2h", 2, 2), ("W", "1h", 3),
+    ("S", "2", 3, 3), ("D", "3", 0, 0), ("S", "2", 5, 0), ("S", "3", 5, 0), ("C", "tk", 2), ("C", "tk", 3),
+    ("S", "3", 2, 3), ("D", "2", 4, 0), ("W", "2", 4, 0), ("S", "2h", 4, 0), ("D", "2h", 3, 1), ("D", "2h", 3, 2),
+    ("S", "3", 4, 1), ("D", "3", 3, 2), ("D", "2h", 2, 1), ("D", "1h", 4), ("D", "2h", 2, 2), ("S", "3", 3, 3),
+    ("W", "1h", 4), ("S", "2", 4, 3), ("C", "tk", 4), ("D", "2", 2, 3), ("W", "2", 2, 3), ("S", "2h", 2, 3),
+    ("S", "3", 4, 2), ("C", "tk", 5), ("D", "2", 3, 3), ("D", "1", 5), ("D", "3", 2, 3), ("W", "1", 5),
+    ("S", "1h", 5), ("D", "2", 4, 1), ("S", "2", 5, 1), ("W", "2", 3, 3), ("S", "2h", 3, 3), ("D", "2", 4, 2),
+    ("S", "2", 5, 2), ("D", "3", 3, 3), ("D", "2h", 2, 3), ("D", "3", 5, 0), ("S", "3", 3, 4), ("W", "2", 4, 1),
+    ("S", "2h", 4, 1), ("W", "2", 4, 2), ("S", "2h", 4, 2), ("C", "tk", 6), ("W", "2h", 4, 0), ("S", "3", 4, 3),
+    ("S", "3", 3, 5), ("C", "tk", 7), ("D", "2h", 4, 0), ("D", "2h", 3, 3), ("D", "3", 4, 1), ("D", "1h", 5),
+    ("S", "3", 2, 4), ("D", "2", 5, 0), ("W", "1h", 5), ("S", "2", 5, 3), ("W", "2", 5, 0), ("S", "2h", 5, 0),
+    ("D", "3", 3, 4), ("S", "3", 5, 1), ("D", "3", 4, 2), ("D", "3", 4, 3), ("W", "2h", 4, 1), ("S", "3", 4, 4),
+    ("S", "3", 5, 2), ("W", "3", 2, 0), ("W", "3", 2, 1), ("W", "3", 2, 2), ("W", "3", 2, 3), ("W", "3", 4, 0),
+    ("W", "3", 4, 1), ("W", "3", 4, 2), ("W", "3", 4, 3), ("C", "mm", 2, 0, "near"), ("D", "2h", 4, 1),
+    ("D", "2h", 4, 2), ("D", "2", 4, 3), ("D", "2h", 5, 0), ("D", "2", 5, 1), ("D", "2", 5, 2), ("W", "2", 4, 3),
+    ("S", "2h", 4, 3), ("W", "2", 5, 1), ("S", "2h", 5, 1), ("D", "2", 5, 3), ("W", "2", 5, 2), ("S", "2h", 5, 2),
+    ("D", "3", 3, 5), ("W", "2h", 5, 0), ("S", "3", 5, 3), ("W", "2", 5, 3), ("S", "2h", 5, 3), ("D", "3", 5, 1),
+    ("W", "2h", 3, 0), ("W", "2h", 3, 1), ("W", "2h", 3, 2), ("W", "2h", 3, 3), ("S", "3", 3, 6), ("C", "sq", 0),
+    ("S", "3", 1, 0), ("C", "sq", 1), ("D", "2h", 4, 3), ("S", "3", 0, 1), ("C", "sq", 2), ("D", "2h", 5, 1),
+    ("D", "2h", 5, 2), ("S", "3", 1, 1), ("D", "3", 2, 4), ("S", "3", 2, 5), ("D", "3", 5, 2), ("D", "2h", 5, 3),
+    ("S", "3", 0, 2), ("D", "3", 5, 3), ("W", "2h", 5, 1), ("S", "3", 5, 4), ("S", "3", 1, 2), ("W", "3", 3, 0),
     ("W", "3", 3, 1), ("W", "3", 3, 2), ("W", "3", 3, 3), ("W", "3", 5, 0), ("W", "3", 5, 1), ("W", "3", 5, 2),
-    ("W", "3", 5, 3), ("C", "mm", 2, 0, "near"), ("D", "3", 1, 0), ("D", "3", 0, 1), ("D", "2h", 5, 3),
-    ("S", "3", 0, 3), ("S", "3", 1, 3), ("D", "3", 1, 1), ("S", "3", 0, 4), ("D", "3", 4, 4), ("W", "2h", 4, 2),
-    ("S", "3", 4, 5), ("W", "3", 2, 4), ("W", "3", 4, 4), ("C", "mm", 1, 1, "near"), ("D", "3", 3, 6),
-    ("D", "3", 0, 2), ("D", "3", 1, 2), ("W", "2h", 5, 2), ("S", "3", 5, 5), ("D", "3", 0, 3), ("D", "3", 1, 3),
-    ("W", "3", 0, 0), ("W", "3", 0, 1), ("W", "3", 0, 2), ("W", "3", 0, 3), ("S", "3h", 0, 0), ("D", "3", 2, 5),
-    ("W", "3", 1, 0), ("W", "3", 1, 1), ("W", "3", 1, 2), ("W", "3", 1, 3), ("S", "3h", 1, 0), ("D", "3", 0, 4),
-    ("S", "3", 1, 4), ("W", "2h", 2, 0), ("W", "2h", 2, 1), ("W", "2h", 2, 2), ("W", "2h", 2, 3), ("S", "3", 2, 6),
-    ("W", "3", 3, 4), ("W", "3", 5, 4), ("C", "mm", 2, 1, "near"), ("D", "3", 5, 4), ("D", "3h", 0, 0),
-    ("W", "2h", 5, 3), ("S", "3", 5, 6), ("D", "3h", 1, 0), ("W", "3", 0, 4), ("S", "3h", 0, 1), ("D", "3", 4, 5),
-    ("W", "2h", 4, 3), ("S", "3", 4, 6), ("W", "3", 2, 5), ("W", "3", 4, 5), ("C", "mm", 1, 2, "near"),
-    ("S", "3", 0, 5), ("W", "3h", 0, 0), ("W", "3h", 1, 0), ("C", "mm", 0, 0, "all"), ("W", "3", 3, 5),
-    ("W", "3", 5, 5), ("C", "mm", 2, 2, "near"), ("D", "3", 1, 4), ("D", "3h", 0, 1), ("W", "3", 1, 4),
-    ("S", "3h", 1, 1), ("D", "3", 2, 6), ("D", "3", 5, 5), ("S", "3h", 3, 0), ("S", "3", 1, 5), ("S", "3h", 2, 0),
-    ("S", "3h", 5, 0), ("S", "3h", 4, 0), ("D", "3", 0, 5), ("D", "3h", 1, 1), ("W", "3", 0, 5), ("S", "3h", 0, 2),
-    ("W", "3h", 0, 1), ("W", "3h", 1, 1), ("C", "mm", 0, 1, "all"), ("D", "3", 5, 6), ("D", "3h", 3, 0),
-    ("S", "3h", 3, 1), ("W", "2h", 0, 0), ("W", "2h", 0, 1), ("W", "2h", 0, 2), ("W", "2h", 0, 3), ("S", "3", 0, 6),
-    ("D", "3", 4, 6), ("D", "3h", 2, 0), ("S", "3h", 2, 1), ("W", "3", 2, 6), ("W", "3", 4, 6),
-    ("C", "mm", 1, 3, "near"), ("S", "3h", 5, 1), ("S", "3h", 4, 1), ("W", "3", 3, 6), ("W", "3", 5, 6),
-    ("C", "mm", 2, 3, "near"), ("D", "3", 1, 5), ("D", "3h", 0, 2), ("W", "3", 1, 5), ("S", "3h", 1, 2),
-    ("W", "3h", 2, 0), ("W", "3h", 4, 0), ("C", "mm", 1, 0, "far"), ("D", "3h", 5, 0), ("D", "3h", 3, 1),
-    ("S", "3h", 3, 2), ("D", "3", 0, 6), ("W", "2h", 1, 0), ("W", "2h", 1, 1), ("W", "2h", 1, 2), ("W", "2h", 1, 3),
-    ("S", "3", 1, 6), ("D", "3h", 4, 0), ("D", "3h", 2, 1), ("S", "3h", 2, 2), ("W", "3h", 3, 0), ("W", "3h", 5, 0),
-    ("C", "mm", 2, 0, "far"), ("S", "3h", 5, 2), ("S", "3h", 4, 2), ("W", "3h", 2, 1), ("W", "3h", 4, 1),
-    ("C", "mm", 1, 1, "far"), ("D", "3h", 1, 2), ("W", "3", 0, 6), ("S", "3h", 0, 3), ("W", "3h", 0, 2),
-    ("W", "3h", 1, 2), ("C", "mm", 0, 2, "all"), ("D", "3h", 5, 1), ("D", "3h", 3, 2), ("S", "3h", 3, 3),
-    ("D", "3h", 4, 1), ("D", "3h", 2, 2), ("S", "3h", 2, 3), ("W", "3h", 3, 1), ("W", "3h", 5, 1),
-    ("C", "mm", 2, 1, "far"), ("D", "3", 1, 6), ("D", "3h", 0, 3), ("W", "3", 1, 6), ("S", "3h", 1, 3),
-    ("D", "3h", 5, 2), ("S", "3h", 5, 3), ("D", "3h", 4, 2), ("S", "3h", 4, 3), ("W", "3h", 2, 2), ("W", "3h", 4, 2),
-    ("C", "mm", 1, 2, "far"), ("W", "3h", 3, 2), ("W", "3h", 5, 2), ("C", "mm", 2, 2, "far"), ("W", "3h", 0, 3),
-    ("W", "3h", 1, 3), ("C", "mm", 0, 3, "all"), ("W", "3h", 2, 3), ("W", "3h", 4, 3), ("C", "mm", 1, 3, "far"),
-    ("W", "3h", 3, 3), ("W", "3h", 5, 3), ("C", "mm", 2, 3, "far"), ("C", "fin", 1), ("C", "fin", 2), ("C", "fin", 0),
-    ("D", "3h", 1, 3), ("D", "3h", 3, 3), ("D", "3h", 2, 3), ("D", "3h", 5, 3), ("D", "3h", 4, 3),
+    ("W", "3", 5, 3), ("C", "mm", 1, 0, "near"), ("D", "3", 1, 0), ("D", "3", 0, 1), ("D", "3", 1, 1),
+    ("S", "3", 0, 3), ("S", "3", 1, 3), ("D", "3", 4, 4), ("W", "2h", 4, 2), ("S", "3", 4, 5), ("D", "3", 0, 2),
+    ("S", "3", 0, 4), ("W", "3", 2, 4), ("W", "3", 4, 4), ("C", "mm", 2, 1, "near"), ("D", "3", 3, 6),
+    ("D", "3", 1, 2), ("D", "3", 0, 3), ("D", "3", 1, 3), ("W", "3", 0, 0), ("W", "3", 0, 1), ("W", "3", 0, 2),
+    ("W", "3", 0, 3), ("S", "3h", 0, 0), ("W", "2h", 5, 2), ("S", "3", 5, 5), ("D", "3", 2, 5), ("W", "3", 1, 0),
+    ("W", "3", 1, 1), ("W", "3", 1, 2), ("W", "3", 1, 3), ("S", "3h", 1, 0), ("W", "2h", 2, 0), ("W", "2h", 2, 1),
+    ("W", "2h", 2, 2), ("W", "2h", 2, 3), ("S", "3", 2, 6), ("S", "3", 1, 4), ("W", "3", 3, 4), ("W", "3", 5, 4),
+    ("C", "mm", 1, 1, "near"), ("D", "3", 5, 4), ("D", "3", 0, 4), ("D", "3", 4, 5), ("W", "2h", 4, 3),
+    ("S", "3", 4, 6), ("D", "3h", 0, 0), ("D", "3h", 1, 0), ("W", "3", 0, 4), ("S", "3h", 0, 1), ("W", "2h", 5, 3),
+    ("S", "3", 5, 6), ("W", "3", 2, 5), ("W", "3", 4, 5), ("C", "mm", 2, 2, "near"), ("S", "3", 0, 5),
+    ("W", "3h", 0, 0), ("W", "3h", 1, 0), ("C", "mm", 0, 0, "all"), ("W", "3", 3, 5), ("W", "3", 5, 5),
+    ("C", "mm", 1, 2, "near"), ("D", "3", 1, 4), ("D", "3h", 0, 1), ("W", "3", 1, 4), ("S", "3h", 1, 1),
+    ("D", "3", 2, 6), ("D", "3", 5, 5), ("S", "3h", 2, 0), ("S", "3", 1, 5), ("S", "3h", 3, 0), ("S", "3h", 4, 0),
+    ("S", "3h", 5, 0), ("D", "3", 0, 5), ("D", "3h", 1, 1), ("W", "3", 0, 5), ("S", "3h", 0, 2), ("W", "3h", 0, 1),
+    ("W", "3h", 1, 1), ("C", "mm", 0, 1, "all"), ("D", "3", 4, 6), ("D", "3h", 2, 0), ("S", "3h", 2, 1),
+    ("W", "2h", 0, 0), ("W", "2h", 0, 1), ("W", "2h", 0, 2), ("W", "2h", 0, 3), ("S", "3", 0, 6), ("D", "3", 5, 6),
+    ("D", "3h", 3, 0), ("S", "3h", 3, 1), ("S", "3h", 4, 1), ("W", "3", 2, 6), ("W", "3", 4, 6),
+    ("C", "mm", 2, 3, "near"), ("S", "3h", 5, 1), ("D", "3", 1, 5), ("D", "3h", 0, 2), ("W", "3", 1, 5),
+    ("S", "3h", 1, 2), ("W", "3", 3, 6), ("W", "3", 5, 6), ("C", "mm", 1, 3, "near"), ("D", "3h", 4, 0),
+    ("D", "3h", 2, 1), ("S", "3h", 2, 2), ("W", "2h", 1, 0), ("W", "2h", 1, 1), ("W", "2h", 1, 2), ("W", "2h", 1, 3),
+    ("S", "3", 1, 6), ("D", "3h", 5, 0), ("D", "3h", 3, 1), ("S", "3h", 3, 2), ("W", "3h", 2, 0), ("W", "3h", 4, 0),
+    ("C", "mm", 2, 0, "far"), ("S", "3h", 4, 2), ("W", "3h", 3, 0), ("W", "3h", 5, 0), ("C", "mm", 1, 0, "far"),
+    ("S", "3h", 5, 2), ("W", "3h", 0, 2), ("W", "3h", 1, 2), ("C", "mm", 0, 2, "all"), ("D", "3h", 1, 2),
+    ("D", "3", 0, 6), ("W", "3", 0, 6), ("S", "3h", 0, 3), ("D", "3h", 4, 1), ("D", "3h", 2, 2), ("S", "3h", 2, 3),
+    ("W", "3h", 2, 1), ("W", "3h", 4, 1), ("C", "mm", 2, 1, "far"), ("D", "3", 1, 6), ("W", "3", 1, 6),
+    ("S", "3h", 1, 3), ("D", "3h", 5, 1), ("D", "3h", 3, 2), ("S", "3h", 3, 3), ("W", "3h", 3, 1), ("W", "3h", 5, 1),
+    ("C", "mm", 1, 1, "far"), ("S", "3h", 4, 3), ("S", "3h", 5, 3), ("W", "3h", 2, 2), ("W", "3h", 4, 2),
+    ("C", "mm", 2, 2, "far"), ("W", "3h", 3, 2), ("W", "3h", 5, 2), ("C", "mm", 1, 2, "far"), ("W", "3h", 0, 3),
+    ("W", "3h", 1, 3), ("C", "mm", 0, 3, "all"), ("W", "3h", 2, 3), ("W", "3h", 4, 3), ("C", "mm", 2, 3, "far"),
+    ("W", "3h", 3, 3), ("W", "3h", 5, 3), ("C", "mm", 1, 3, "far"), ("C", "fin", 1), ("C", "fin", 2), ("C", "fin", 0),
+    ("D", "3h", 4, 2), ("D", "3h", 0, 3), ("D", "3h", 5, 2), ("D", "3h", 1, 3), ("D", "3h", 2, 3), ("D", "3h", 3, 3),
+    ("D", "3h", 4, 3), ("D", "3h", 5, 3),
 )
 
 THRESH = ((0.25, 0.5), (0.75, 1.0), (1.25, 1.5), (1.75, 2.0), (2.5, 3.0), (3.5, 4.0), (5.0, 6.0))
@@ -331,13 +331,14 @@
     def mm(c, count, coords, last=False):
         lo, width = CLS[c]
         cc = pl.ds(lo, width)
+        rows = 2 * TOK if c == 0 else TOK
 
         def chunk(t, carry):
             yy, xx = coords(t)
             kk = pl.ds(pl.multiple_of((yy * 4 + xx) * FROWS, FROWS), FROWS)
 
             def block(m, carry):
-                mr = pl.ds(pl.multiple_of(m * TOK, TOK), TOK)
+                mr = pl.ds(pl.multiple_of(m * rows, rows), rows)
                 total = acc[mr, cc] + jnp.dot(tok[mr, kk], W[c][yy, xx], preferred_element_type=F32)
                 if last:
                     for k in range(width // 128):
@@ -347,7 +348,7 @@
                     acc[mr, cc] = total
                 return carry
 
-            return lax.fori_loop(0, 2, block, carry)
+            return lax.fori_loop(0, 2 * TOK // rows, block, carry)
 
         lax.fori_loop(0, count, chunk, 0)
 

time: 130 us -> 127 us (0.977)
  Pallas kernels: 126 us -> 124 us
    pallas_call x1, Pallas kernels: 126 us -> 124 us  [body(): pl.pallas_call(kernel, out_shape=(vm((ROWS, KVW), F32), vm((ROWS, KVW), F...]
where the time goes in v11:
time: 127 us
  Pallas kernels  124 us (98%)
  local copies, waits for them, and re-layouts  2.9 us (2%)
    pallas_call x1, Pallas kernels, body(): pl.pallas_call(kernel, out_shape=(vm((ROWS, KVW), F32), vm((ROWS, KVW), F...  124 us
    unnamed x3, local copies, waits for them, and re-layouts  2.9 us

profile of v11, /device:TPU:0, one launch (start us, length us, event | category | flops | bytes accessed | tf_op | source)
XLA Modules:
  0.0 127.3 jit_solution(2652230340807402578)
XLA Ops:
  0.6 123.8 %shard_map.85 = (f32[192,1024]{1,0:T(8,128)S(1)}, f32[192,1024]{1,0:T(8,128)S(1)}, bf16[768,1024]{1,0:T(8,128)(2,1)S(1)}) custom-call(bf16[384,12288]{1,0:T(8,128)(2,1)} %tokens.1, bf16[96,128]{1,0:T(8,128)(2,1)} %bitcast.7, bf16[4,192,1024]{2,1,0:T(8,128)(2,1)} %bitcast.5, s32[32,768]{1,0:T(8,128)} %bitcast.6, f32[192,1024]{1,0:T(8,128)} %base.1, ...), custom_call_target="tpu_custom_call" | custom-call | flops 19327352832 | bytes 30000000 | tf_op jit(solution)/shard_map/pallas_call | solution.py:486
  124.4 0.9 copy.12
  125.3 0.9 copy.13
  126.2 1.1 copy.14
